TPU v7x, 32 devices: a whole 2x2x4 slice. The times are simulated.
32 devices in a mesh: ta: 4 (over y, x), pa: 4 (over z), dev: 2 (over core).
Axes of the slice: x: 2, y: 2, z: 4, core: 2. Of those that a mesh axis runs over, the one named last changes fastest.
Arguments:
- latents: bfloat16 [4, 20, 1024, 384], P('dev', 'ta', 'pa'), may hold values from -6 to 6
- context: bfloat16 [4, 120, 384], P('dev'), may hold values from -6 to 6
- cotangent: bfloat16 [4, 20, 1024, 384], P('dev', 'ta', 'pa'), may hold values from -6 to 6
- timesteps: int32 [4], P('dev'), may hold values from 0 to 999
- frame_counts: int32 [4], P('dev'), may hold values from 6 to 20, as said below
- text_lengths: int32 [4], P('dev'), may hold values from 15 to 120, as said below
- step_proj: bfloat16 [256, 2304], replicated, may hold values from -0.1875 to 0.1875
- mod_table: bfloat16 [2, 6, 384], replicated, may hold values from -1.796875 to 1.796875
- patch_attn: bfloat16 [4, 384, 384], replicated
- cross_attn: bfloat16 [4, 384, 384], replicated
- patch_up: bfloat16 [384, 1536], replicated, may hold values from -0.3125 to 0.3125
- patch_down: bfloat16 [1536, 384], replicated, may hold values from -0.15625 to 0.15625
- frame_attn: bfloat16 [4, 384, 384], replicated
- frame_up: bfloat16 [384, 1536], replicated, may hold values from -0.3125 to 0.3125
- frame_down: bfloat16 [1536, 384], replicated, may hold values from -0.15625 to 0.15625
Outputs:
- output: bfloat16 [4, 20, 1024, 384], P('dev', 'ta', 'pa')
- latents_grad: float32 [4, 20, 1024, 384], P('dev', 'ta', 'pa')
- step_proj_grad: float32 [256, 2304], replicated
- mod_table_grad: float32 [2, 6, 384], replicated
- patch_attn_grad: float32 [4, 384, 384], replicated
- cross_attn_grad: float32 [4, 384, 384], replicated
- patch_up_grad: float32 [384, 1536], replicated
- patch_down_grad: float32 [1536, 384], replicated
- frame_attn_grad: float32 [4, 384, 384], replicated
- frame_up_grad: float32 [384, 1536], replicated
- frame_down_grad: float32 [1536, 384], replicated
Inputs may be any that keep to these rules, and one draw needn't show every extreme that they name: `frame_counts`: in every aligned block of 2 clips one clip has all 20 frames valid. `text_lengths`: in every aligned block of 2 clips one clip has all 120 text tokens live.
All inputs are finite; a program needn't handle non-finite values.
Results may differ from a plain program's by a relative error of at most 0.02.
Values may be sent and summed in bfloat16 or wider, within the bound.
A program may use at most 320 MiB of HBM per device.

v0:
```python
import math

import jax
import jax.numpy as jnp
from jax import lax
from jax.sharding import PartitionSpec as P

HEADS = 6
HDIM = 64


EPSILON = 1e-06
MASKED_SCORE = -1e30
HIGHEST = lax.Precision.HIGHEST


def merged(value, axis, join):
    pieces = jax.tree.map(lambda part: lax.all_gather(part, axis), value)
    head = jax.tree.map(lambda part: part[0], pieces)
    tail = jax.tree.map(lambda part: part[1:], pieces)
    running, _ = lax.scan(lambda running, share: (join(running, share), None), head, tail)
    return running


def layer_norm(values):
    centred = values - jnp.mean(values, axis=-1, keepdims=True)
    return centred * lax.rsqrt(jnp.mean(centred * centred, axis=-1, keepdims=True) + EPSILON)


def modulate(values, shift_by, scale_by):
    return layer_norm(values) * (1.0 + scale_by) + shift_by


def gelu_tanh(values):
    return jax.nn.gelu(values, approximate=True)


def sinusoid(step_ids, width_count):
    half_count = width_count // 2
    frequency = jnp.exp(-math.log(10000.0) * jnp.arange(half_count, dtype=jnp.float32) / half_count)
    angles = step_ids.astype(jnp.float32)[:, None] * frequency[None, :]
    return jnp.concatenate([jnp.cos(angles), jnp.sin(angles)], axis=1)


def products(operand, matrix):
    return jnp.dot(operand, matrix, preferred_element_type=jnp.float32)


def row_products(operand, matrix):
    return lax.dot_general(
        operand, matrix, (((0,), (0,)), ((), ())), preferred_element_type=jnp.float32
    )


def back_products(operand, matrix):
    return lax.dot_general(
        operand, matrix, (((1,), (1,)), ((), ())), preferred_element_type=jnp.float32
    )


def split_heads(values):
    return values.reshape(values.shape[:-1] + (HEADS, values.shape[-1] // HEADS))


def combine_stats(former, latter):
    summit = jnp.maximum(former[0], latter[0])
    return (
        summit,
        former[1] * jnp.exp(former[0] - summit) + latter[1] * jnp.exp(latter[0] - summit),
    )


def score_block(forms, queries, key_heads, scale_by, key_live):
    scores = jnp.einsum(forms[0], queries, key_heads, preferred_element_type=jnp.float32) * scale_by
    if key_live is None:
        return scores
    return jnp.where(key_live > 0.0, scores, MASKED_SCORE)


def attend_forward(forms, queries, key_heads, value_heads, scale_by, key_live):
    scores = score_block(forms, queries, key_heads, scale_by, key_live)
    largest = jnp.max(scores, axis=-1, keepdims=True)
    exponent = jnp.exp(scores - largest)
    row_totals = jnp.sum(exponent, axis=-1, keepdims=True)
    weights_low = (exponent / row_totals).astype(jnp.bfloat16)
    attended = jnp.einsum(forms[1], weights_low, value_heads, preferred_element_type=jnp.float32)
    return (attended, largest + jnp.log(row_totals))


def attend_backward(
    forms, queries, key_heads, value_heads, scale_by, key_live, log_totals, d_attended, centre_sum
):
    scores = score_block(forms, queries, key_heads, scale_by, key_live)
    chances = jnp.exp(scores - log_totals)
    d_chances = jnp.einsum(forms[0], d_attended, value_heads, preferred_element_type=jnp.float32)
    centre = centre_sum(jnp.sum(d_chances * chances, axis=-1, keepdims=True))
    d_scores = (chances * (d_chances - centre)).astype(jnp.bfloat16)
    d_queries = (
        jnp.einsum(forms[1], d_scores, key_heads, preferred_element_type=jnp.float32) * scale_by
    )
    d_keys = jnp.einsum(forms[2], d_scores, queries, preferred_element_type=jnp.float32) * scale_by
    d_values = jnp.einsum(
        forms[2], chances.astype(jnp.bfloat16), d_attended, preferred_element_type=jnp.float32
    )
    return (d_queries, d_keys, d_values)


def mlp_forward(state, modulation, keep_cube, up_weight, down_weight):
    normed, pull_norm = jax.vjp(modulate, state, modulation[3], modulation[4])
    normed = normed.astype(jnp.bfloat16).reshape(-1, state.shape[-1])
    lifted = products(normed, up_weight)
    activated, pull_gelu = jax.vjp(gelu_tanh, lifted)
    activated = activated.astype(jnp.bfloat16)
    branch = products(activated, down_weight)
    result = state + keep_cube * modulation[5] * branch.reshape(state.shape)
    return (result, (pull_norm, normed, pull_gelu, activated, branch))


def mlp_backward(grad, modulation, keep_rows, saved, up_weight, down_weight):
    pull_norm, normed, pull_gelu, activated, branch = saved
    grad_rows = grad.reshape(-1, grad.shape[-1])
    d_branch = (keep_rows * modulation[5] * grad_rows).astype(jnp.bfloat16)
    d_gate = jnp.sum(keep_rows * branch * grad_rows, axis=0)
    d_down = row_products(activated, d_branch)
    d_lifted = pull_gelu(back_products(d_branch, down_weight))[0].astype(jnp.bfloat16)
    d_up = row_products(normed, d_lifted)
    d_state, d_shift, d_scale = pull_norm(back_products(d_lifted, up_weight).reshape(grad.shape))
    return (grad + d_state, (d_shift, d_scale, d_gate), d_up, d_down)


def branch_backward(grad_rows, keep_rows, gate_row, branch, attended, projection):
    d_branch = (keep_rows * gate_row * grad_rows).astype(jnp.bfloat16)
    d_gate = jnp.sum(keep_rows * branch * grad_rows, axis=0)
    d_projection = row_products(attended, d_branch)
    d_attended = back_products(d_branch, projection).astype(jnp.bfloat16)
    return (d_attended, d_gate, d_projection)


def per_device(
    latents,
    context,
    cotangent,
    timesteps,
    frame_counts,
    text_lengths,
    step_proj,
    mod_table,
    patch_attn,
    cross_attn,
    patch_up,
    patch_down,
    frame_attn,
    frame_up,
    frame_down,
):
    frames_dev = latents.shape[1]
    patches_dev = latents.shape[2]
    width = latents.shape[3]
    row_count = frames_dev * patches_dev
    scale_by = HDIM ** (-0.5)
    frame_start = lax.axis_index("ta") * frames_dev
    step_weight = step_proj.astype(jnp.float32)
    table = mod_table.astype(jnp.float32)
    embeddings = sinusoid(timesteps, step_proj.shape[0])
    patch_forms = ("fqhe,fkhe->fhqk", "fhqk,fkhe->fqhe", "fhqk,fqhe->fkhe")
    cross_forms = ("qhe,khe->hqk", "hqk,khe->qhe", "hqk,qhe->khe")
    frame_forms = ("qphe,kphe->phqk", "phqk,kphe->qphe", "phqk,qphe->kphe")
    cube_shape = (frames_dev, patches_dev, width)

    def unchanged(values):
        return values

    def frame_centre(values):
        return lax.psum(values, "ta")

    def clip_step(totals, items):
        clip_tokens, clip_context, clip_cotangent, embedding, frame_count, text_count = items
        frame_live = (frame_start + jnp.arange(frames_dev, dtype=jnp.int32) < frame_count).astype(
            jnp.float32
        )
        keep_cube = frame_live[:, None, None]
        keep_rows = jnp.broadcast_to(keep_cube, (frames_dev, patches_dev, 1)).reshape(row_count, 1)
        text_live = (jnp.arange(clip_context.shape[0], dtype=jnp.int32) < text_count).astype(
            jnp.float32
        )
        timing = jnp.dot(embedding, step_weight, precision=HIGHEST).reshape(6, width)
        space_mod = timing + table[0]
        frame_mod = timing + table[1]
        start_state = clip_tokens.astype(jnp.float32)
        normed_a, pull_a = jax.vjp(modulate, start_state, space_mod[0], space_mod[1])
        normed_a = normed_a.astype(jnp.bfloat16).reshape(row_count, width)
        space_qkv = jnp.einsum(
            "rd,jde->jre", normed_a, patch_attn[:3], preferred_element_type=jnp.float32
        ).astype(jnp.bfloat16)
        space_keys = space_qkv[1].reshape(cube_shape)
        space_values = space_qkv[2].reshape(cube_shape)
        whole_keys, whole_values = (
            lax.all_gather(space_keys, "pa", axis=1, tiled=True),
            lax.all_gather(space_values, "pa", axis=1, tiled=True),
        )
        space_query_cube = space_qkv[0].reshape(cube_shape)
        space_queries = split_heads(space_query_cube)
        space_att, space_lse = attend_forward(
            patch_forms,
            space_queries,
            split_heads(whole_keys),
            split_heads(whole_values),
            scale_by,
            None,
        )
        space_att = space_att.reshape(row_count, width).astype(jnp.bfloat16)
        space_branch = products(space_att, patch_attn[3])
        after_space = start_state + keep_cube * space_mod[2] * space_branch.reshape(cube_shape)
        cross_in = after_space.reshape(row_count, width).astype(jnp.bfloat16)
        cross_queries = products(cross_in, cross_attn[0]).astype(jnp.bfloat16)
        cross_kv = jnp.einsum(
            "td,jde->jte", clip_context, cross_attn[1:3], preferred_element_type=jnp.float32
        ).astype(jnp.bfloat16)
        cross_att, cross_lse = attend_forward(
            cross_forms,
            split_heads(cross_queries),
            split_heads(cross_kv[0]),
            split_heads(cross_kv[1]),
            scale_by,
            text_live,
        )
        cross_att = cross_att.reshape(row_count, width).astype(jnp.bfloat16)
        cross_branch = products(cross_att, cross_attn[3])
        after_cross = after_space + keep_cube * cross_branch.reshape(cube_shape)
        after_mlp, space_saved = mlp_forward(
            after_cross, space_mod, keep_cube, patch_up, patch_down
        )
        normed_t, pull_t = jax.vjp(modulate, after_mlp, frame_mod[0], frame_mod[1])
        normed_t = normed_t.astype(jnp.bfloat16).reshape(row_count, width)
        frame_qkv = jnp.einsum(
            "rd,jde->jre", normed_t, frame_attn[:3], preferred_element_type=jnp.float32
        ).astype(jnp.bfloat16)
        all_queries = lax.all_gather(frame_qkv[0].reshape(cube_shape), "ta", axis=0, tiled=True)
        query_heads = split_heads(all_queries)
        key_heads_t = split_heads(frame_qkv[1].reshape(cube_shape))
        value_heads_t = split_heads(frame_qkv[2].reshape(cube_shape))
        scores_t = score_block(frame_forms, query_heads, key_heads_t, scale_by, frame_live)
        local_max = jnp.max(scores_t, axis=-1, keepdims=True)
        local_sum = jnp.sum(jnp.exp(scores_t - local_max) * frame_live, axis=-1, keepdims=True)
        merged_max, merged_sum = merged((local_max, local_sum), "ta", combine_stats)
        frame_lse = merged_max + jnp.log(merged_sum)
        weights_low = jnp.exp(scores_t - frame_lse).astype(jnp.bfloat16)
        partial_att = jnp.einsum(
            frame_forms[1], weights_low, value_heads_t, preferred_element_type=jnp.float32
        ).reshape(all_queries.shape)
        own_att = lax.psum_scatter(partial_att, "ta", scatter_dimension=0, tiled=True)
        frame_att = own_att.reshape(row_count, width).astype(jnp.bfloat16)
        frame_branch = products(frame_att, frame_attn[3])
        after_frame = after_mlp + keep_cube * frame_mod[2] * frame_branch.reshape(cube_shape)
        final_state, frame_saved = mlp_forward(
            after_frame, frame_mod, keep_cube, frame_up, frame_down
        )
        grad = clip_cotangent.astype(jnp.float32)
        grad, frame_mlp_mods, d_frame_up, d_frame_down = mlp_backward(
            grad, frame_mod, keep_rows, frame_saved, frame_up, frame_down
        )
        grad_rows = grad.reshape(row_count, width)
        d_frame_att, d_frame_gate, d_frame_proj = branch_backward(
            grad_rows, keep_rows, frame_mod[2], frame_branch, frame_att, frame_attn[3]
        )
        all_d_att = lax.all_gather(d_frame_att.reshape(cube_shape), "ta", axis=0, tiled=True)
        d_query_part, d_key_t, d_value_t = attend_backward(
            frame_forms,
            query_heads,
            key_heads_t,
            value_heads_t,
            scale_by,
            frame_live,
            frame_lse,
            split_heads(all_d_att),
            frame_centre,
        )
        d_query_t = lax.psum_scatter(
            d_query_part.reshape(all_queries.shape), "ta", scatter_dimension=0, tiled=True
        )
        frame_dqkv = jnp.stack(
            [
                d_query_t.reshape(row_count, width),
                d_key_t.reshape(row_count, width),
                d_value_t.reshape(row_count, width),
            ]
        ).astype(jnp.bfloat16)
        d_frame_qkv = jnp.einsum(
            "rd,jre->jde", normed_t, frame_dqkv, preferred_element_type=jnp.float32
        )
        d_normed_t = jnp.einsum(
            "jre,jde->rd", frame_dqkv, frame_attn[:3], preferred_element_type=jnp.float32
        )
        d_state, d_shift_t, d_scale_t = pull_t(d_normed_t.reshape(cube_shape))
        grad = grad + d_state
        grad, space_mlp_mods, d_patch_up, d_patch_down = mlp_backward(
            grad, space_mod, keep_rows, space_saved, patch_up, patch_down
        )
        grad_rows = grad.reshape(row_count, width)
        d_cross_att, unused_gate, d_cross_proj = branch_backward(
            grad_rows, keep_rows, 1.0, cross_branch, cross_att, cross_attn[3]
        )
        d_cross_q, d_cross_k, d_cross_v = attend_backward(
            cross_forms,
            split_heads(cross_queries),
            split_heads(cross_kv[0]),
            split_heads(cross_kv[1]),
            scale_by,
            text_live,
            cross_lse,
            split_heads(d_cross_att),
            unchanged,
        )
        d_cross_q = d_cross_q.reshape(row_count, width).astype(jnp.bfloat16)
        context_values = clip_context.astype(jnp.float32)
        d_cross_keys = jnp.dot(context_values.T, d_cross_k.reshape(-1, width), precision=HIGHEST)
        d_cross_values = jnp.dot(context_values.T, d_cross_v.reshape(-1, width), precision=HIGHEST)
        d_cross_query_w = row_products(cross_in, d_cross_q)
        grad = grad + back_products(d_cross_q, cross_attn[0]).reshape(cube_shape)
        grad_rows = grad.reshape(row_count, width)
        d_space_att, d_space_gate, d_space_proj = branch_backward(
            grad_rows, keep_rows, space_mod[2], space_branch, space_att, patch_attn[3]
        )
        back_keys, back_values = (
            lax.all_gather(space_keys, "pa", axis=1, tiled=True),
            lax.all_gather(space_values, "pa", axis=1, tiled=True),
        )
        d_space_cube = d_space_att.reshape(cube_shape)
        d_space_q, d_whole_k, d_whole_v = attend_backward(
            patch_forms,
            space_queries,
            split_heads(back_keys),
            split_heads(back_values),
            scale_by,
            None,
            space_lse,
            split_heads(d_space_cube),
            unchanged,
        )
        d_own_k, d_own_v = (
            lax.psum_scatter(
                d_whole_k.reshape(back_keys.shape), "pa", scatter_dimension=1, tiled=True
            ),
            lax.psum_scatter(
                d_whole_v.reshape(back_keys.shape), "pa", scatter_dimension=1, tiled=True
            ),
        )
        space_dqkv = jnp.stack(
            [
                d_space_q.reshape(row_count, width),
                d_own_k.reshape(row_count, width),
                d_own_v.reshape(row_count, width),
            ]
        ).astype(jnp.bfloat16)
        d_space_qkv = jnp.einsum(
            "rd,jre->jde", normed_a, space_dqkv, preferred_element_type=jnp.float32
        )
        d_normed_a = jnp.einsum(
            "jre,jde->rd", space_dqkv, patch_attn[:3], preferred_element_type=jnp.float32
        )
        d_state, d_shift_a, d_scale_a = pull_a(d_normed_a.reshape(cube_shape))
        grad = grad + d_state
        space_mods = jnp.stack(
            [
                d_shift_a,
                d_scale_a,
                d_space_gate,
                space_mlp_mods[0],
                space_mlp_mods[1],
                space_mlp_mods[2],
            ]
        )
        frame_mods = jnp.stack(
            [
                d_shift_t,
                d_scale_t,
                d_frame_gate,
                frame_mlp_mods[0],
                frame_mlp_mods[1],
                frame_mlp_mods[2],
            ]
        )
        d_table = jnp.stack([space_mods, frame_mods])
        d_step = embedding[:, None] * (space_mods + frame_mods).reshape(1, -1)
        additions = (
            d_step,
            d_table,
            jnp.concatenate([d_space_qkv, d_space_proj[None]], axis=0),
            jnp.stack([d_cross_query_w, d_cross_keys, d_cross_values, d_cross_proj]),
            d_patch_up,
            d_patch_down,
            jnp.concatenate([d_frame_qkv, d_frame_proj[None]], axis=0),
            d_frame_up,
            d_frame_down,
        )
        totals = tuple((former + latter for former, latter in zip(totals, additions)))
        return (totals, (final_state.astype(jnp.bfloat16), grad))

    empty = tuple(
        (
            jnp.zeros(weight.shape, jnp.float32)
            for weight in (
                step_proj,
                mod_table,
                patch_attn,
                cross_attn,
                patch_up,
                patch_down,
                frame_attn,
                frame_up,
                frame_down,
            )
        )
    )
    totals, (outputs, input_grads) = lax.scan(
        clip_step, empty, (latents, context, cotangent, embeddings, frame_counts, text_lengths)
    )
    shares = (
        lax.psum_scatter(
            totals[0].reshape(-1), ("ta", "pa", "dev"), scatter_dimension=0, tiled=True
        ),
        lax.psum_scatter(
            totals[1].reshape(-1), ("ta", "pa", "dev"), scatter_dimension=0, tiled=True
        ),
        lax.psum_scatter(
            totals[2].reshape(-1), ("ta", "pa", "dev"), scatter_dimension=0, tiled=True
        ),
        lax.psum_scatter(
            totals[3].reshape(-1), ("ta", "pa", "dev"), scatter_dimension=0, tiled=True
        ),
        lax.psum_scatter(
            totals[4].reshape(-1), ("ta", "pa", "dev"), scatter_dimension=0, tiled=True
        ),
        lax.psum_scatter(
            totals[5].reshape(-1), ("ta", "pa", "dev"), scatter_dimension=0, tiled=True
        ),
        lax.psum_scatter(
            totals[6].reshape(-1), ("ta", "pa", "dev"), scatter_dimension=0, tiled=True
        ),
        lax.psum_scatter(
            totals[7].reshape(-1), ("ta", "pa", "dev"), scatter_dimension=0, tiled=True
        ),
        lax.psum_scatter(
            totals[8].reshape(-1), ("ta", "pa", "dev"), scatter_dimension=0, tiled=True
        ),
    )
    whole = (
        lax.all_gather(shares[0], ("ta", "pa", "dev"), axis=0, tiled=True),
        lax.all_gather(shares[1], ("ta", "pa", "dev"), axis=0, tiled=True),
        lax.all_gather(shares[2], ("ta", "pa", "dev"), axis=0, tiled=True),
        lax.all_gather(shares[3], ("ta", "pa", "dev"), axis=0, tiled=True),
        lax.all_gather(shares[4], ("ta", "pa", "dev"), axis=0, tiled=True),
        lax.all_gather(shares[5], ("ta", "pa", "dev"), axis=0, tiled=True),
        lax.all_gather(shares[6], ("ta", "pa", "dev"), axis=0, tiled=True),
        lax.all_gather(shares[7], ("ta", "pa", "dev"), axis=0, tiled=True),
        lax.all_gather(shares[8], ("ta", "pa", "dev"), axis=0, tiled=True),
    )
    return (
        outputs,
        input_grads,
        whole[0].reshape(step_proj.shape),
        whole[1].reshape(mod_table.shape),
        whole[2].reshape(patch_attn.shape),
        whole[3].reshape(cross_attn.shape),
        whole[4].reshape(patch_up.shape),
        whole[5].reshape(patch_down.shape),
        whole[6].reshape(frame_attn.shape),
        whole[7].reshape(frame_up.shape),
        whole[8].reshape(frame_down.shape),
    )


def solution(mesh):
    in_specs = (
        P("dev", "ta", "pa", None),
        P("dev", None, None),
        P("dev", "ta", "pa", None),
        P("dev"),
        P("dev"),
        P("dev"),
        P(),
        P(),
        P(),
        P(),
        P(),
        P(),
        P(),
        P(),
        P(),
    )
    out_specs = (
        P("dev", "ta", "pa", None),
        P("dev", "ta", "pa", None),
        P(),
        P(),
        P(),
        P(),
        P(),
        P(),
        P(),
        P(),
        P(),
    )
    return jax.shard_map(
        per_device, mesh=mesh, in_specs=in_specs, out_specs=out_specs, check_vma=False
    )
```

profile of v0, /device:TPU:1, one launch (start us, length us, event | category | flops | bytes accessed | tf_op | source)
XLA Modules:
  0.0 3031.3 jit_solution(18255034119104655098)
XLA Ops:
  14.1 2188.8 %while.64 = (s32[]{:T(128)}, f32[256,2304]{1,0:T(8,128)}, f32[2,6,384]{2,1,0:T(8,128)}, f32[4,384,384]{1,2,0:T(8,128)}, f32[4,384,384]{2,1,0:T(8,128)}, /*index=...) while((s32[]{:T(128)}, f32[256,2304]{1,0:T(8,128)}, ...), condition=%wide.region_45.46_spmd.clone, body=%wide.region_0.45_spmd.clone.sunk | while | flops 37237444608 | bytes 1708513536 | solution.py:415
  41.6 63.8 %all-gather.39.cloned.1.call-done = bf16[5,1024,384]{2,1,0:T(8,128)(2,1)} async-done(((bf16[5,256,384]{2,1,0:T(8,128)(2,1)}), bf16[5,1024,384]{2,1,0:T(8,128)(2,1)}) %all-gather.39.cloned.1.call-update) | async-done | bytes 3932176 | tf_op jit(solution)/shard_map/while/body/eval_jaxpr/all_gather | solution.py:325
  111.8 15.1 multiply_reduce_fusion.27
  126.8 14.2 fusion.445
  141.0 41.1 %all-gather.37.cloned.1.call-done = bf16[5,1024,384]{2,1,0:T(8,128)(2,1)} async-done(((bf16[5,256,384]{2,1,0:T(8,128)(2,1)}), bf16[5,1024,384]{2,1,0:T(8,128)(2,1)}) %all-gather.37.cloned.1.call-update) | async-done | bytes 3932176 | tf_op jit(solution)/shard_map/while/body/eval_jaxpr/all_gather | solution.py:199
  188.4 14.8 fusion.446
  241.6 42.1 %all-gather.41.cloned.1.call-done = bf16[20,256,384]{2,1,0:T(8,128)(2,1)} async-done(((bf16[5,256,384]{2,1,0:T(8,128)(2,1)}), bf16[20,256,384]{2,1,0:T(8,128)(2,1)}) %all-gather.41.cloned.1.call-update) | async-done | bytes 3932176 | tf_op jit(solution)/shard_map/while/body/eval_jaxpr/all_gather | solution.py:238
  301.7 12.1 fusion.458
  354.9 15.5 copy.311
  373.6 84.5 %reduce-scatter.13.cloned.1.call-done = f32[5,256,384]{1,2,0:T(8,128)} async-done(((f32[20,256,384]{1,2,0:T(8,128)}), f32[5,256,384]{1,2,0:T(8,128)}) %reduce-scatter.13.cloned.1.call-update) | async-done | bytes 1966096 | tf_op jit(solution)/shard_map/while
  488.0 50.6 %all-gather.43.cloned.1.call-done = bf16[20,256,384]{2,1,0:T(8,128)(2,1)} async-done(((bf16[5,256,384]{2,1,0:T(8,128)(2,1)}), bf16[20,256,384]{2,1,0:T(8,128)(2,1)}) %all-gather.43.cloned.1.call-update) | async-done | bytes 3932176 | tf_op jit(solution)/shard_map/while/body/eval_jaxpr/all_gather | solution.py:266
  568.5 52.7 %all-reduce.18.cloned.1.call-done = f32[256,6,20]{2,1,0:T(8,128)} async-done(((f32[256,6,20]{2,1,0:T(8,128)}), f32[256,6,20]{2,1,0:T(8,128)}) %all-reduce.18.cloned.1.call-update) | async-done | bytes 122896 | tf_op jit(solution)/shard_map/while/body/eval_jaxpr/psum | solution.py:174
  638.1 15.5 copy.317
  686.1 50.9 %reduce-scatter.15.cloned.1.call-done = f32[5,256,384]{1,2,0:T(8,128)} async-done(((f32[20,256,384]{1,2,0:T(8,128)}), f32[5,256,384]{1,2,0:T(8,128)}) %reduce-scatter.15.cloned.1.call-update) | async-done | bytes 1966096 | tf_op jit(solution)/shard_map/while
  786.6 16.2 fusion.471
  802.8 23.7 multiply_reduce_fusion.39
  826.5 26.8 multiply_convert_fusion.25
  883.0 12.8 fusion.472
  942.3 136.1 %reduce-scatter.19.cloned.1.call-done = f32[5,256,384]{1,2,0:T(8,128)} async-done(((f32[5,1024,384]{1,2,0:T(8,128)}), f32[5,256,384]{1,2,0:T(8,128)}) %reduce-scatter.19.cloned.1.call-update) | async-done | bytes 1966096 | tf_op jit(solution)/shard_map/while/body/eval_jaxpr/reduce_scatter | solution.py:341
  1134.0 62.2 %all-gather.39.cloned.1.call-done = bf16[5,1024,384]{2,1,0:T(8,128)(2,1)} async-done(((bf16[5,256,384]{2,1,0:T(8,128)(2,1)}), bf16[5,1024,384]{2,1,0:T(8,128)(2,1)}) %all-gather.39.cloned.1.call-update) | async-done | bytes 3932176 | tf_op jit(solution)/shard_map/while/body/eval_jaxpr/all_gather | solution.py:325
  1202.5 15.1 multiply_reduce_fusion.27
  1217.6 14.2 fusion.445
  1231.8 41.1 %all-gather.37.cloned.1.call-done = bf16[5,1024,384]{2,1,0:T(8,128)(2,1)} async-done(((bf16[5,256,384]{2,1,0:T(8,128)(2,1)}), bf16[5,1024,384]{2,1,0:T(8,128)(2,1)}) %all-gather.37.cloned.1.call-update) | async-done | bytes 3932176 | tf_op jit(solution)/shard_map/while/body/eval_jaxpr/all_gather | solution.py:199
  1279.2 14.8 fusion.446
  1332.3 42.1 %all-gather.41.cloned.1.call-done = bf16[20,256,384]{2,1,0:T(8,128)(2,1)} async-done(((bf16[5,256,384]{2,1,0:T(8,128)(2,1)}), bf16[20,256,384]{2,1,0:T(8,128)(2,1)}) %all-gather.41.cloned.1.call-update) | async-done | bytes 3932176 | tf_op jit(solution)/shard_map/while/body/eval_jaxpr/all_gather | solution.py:238
  1392.4 12.1 fusion.458
  1433.8 11.9 convolution_bitcast_fusion.18
  1445.7 15.5 copy.311
  1464.4 84.5 %reduce-scatter.13.cloned.1.call-done = f32[5,256,384]{1,2,0:T(8,128)} async-done(((f32[20,256,384]{1,2,0:T(8,128)}), f32[5,256,384]{1,2,0:T(8,128)}) %reduce-scatter.13.cloned.1.call-update) | async-done | bytes 1966096 | tf_op jit(solution)/shard_map/while
  1578.7 50.6 %all-gather.43.cloned.1.call-done = bf16[20,256,384]{2,1,0:T(8,128)(2,1)} async-done(((bf16[5,256,384]{2,1,0:T(8,128)(2,1)}), bf16[20,256,384]{2,1,0:T(8,128)(2,1)}) %all-gather.43.cloned.1.call-update) | async-done | bytes 3932176 | tf_op jit(solution)/shard_map/while/body/eval_jaxpr/all_gather | solution.py:266
  1659.3 52.7 %all-reduce.18.cloned.1.call-done = f32[256,6,20]{2,1,0:T(8,128)} async-done(((f32[256,6,20]{2,1,0:T(8,128)}), f32[256,6,20]{2,1,0:T(8,128)}) %all-reduce.18.cloned.1.call-update) | async-done | bytes 122896 | tf_op jit(solution)/shard_map/while/body/eval_jaxpr/psum | solution.py:174
  1728.8 15.5 copy.317
  1776.9 50.9 %reduce-scatter.15.cloned.1.call-done = f32[5,256,384]{1,2,0:T(8,128)} async-done(((f32[20,256,384]{1,2,0:T(8,128)}), f32[5,256,384]{1,2,0:T(8,128)}) %reduce-scatter.15.cloned.1.call-update) | async-done | bytes 1966096 | tf_op jit(solution)/shard_map/while
  1877.3 16.2 fusion.471
  1893.6 23.7 multiply_reduce_fusion.39
  1917.3 26.8 multiply_convert_fusion.25
  1974.5 12.7 fusion.472
  2033.1 136.0 %reduce-scatter.19.cloned.1.call-done = f32[5,256,384]{1,2,0:T(8,128)} async-done(((f32[5,1024,384]{1,2,0:T(8,128)}), f32[5,256,384]{1,2,0:T(8,128)}) %reduce-scatter.19.cloned.1.call-update) | async-done | bytes 1966096 | tf_op jit(solution)/shard_map/while/body/eval_jaxpr/reduce_scatter | solution.py:341
  2229.8 307.9 %all-reduce.16.cloned.1.call-done = (f32[589824]{0:T(1024)}, f32[589824]{0:T(1024)}, f32[589824]{0:T(1024)}, f32[589824]{0:T(1024)}, f32[589824]{0:T(1024)}, /*i...) async-done(((f32[589824]{0:T(1024)}, f32[589824]{0:T(1024)}, f32[589824]{0:T(1024)}, f32[589824]{0:T(1024)}, f32[589824]{0:T(1024)}, /*index=5*/f32[589824]{0:T(1024)}, ...) | async-done | bytes 18874384
  2550.4 41.4 %all-reduce.4 = f32[4608]{0:T(1024)S(1)} all-reduce(f32[4608]{0:T(1024)S(1)} %reshape.909), channel_id=9, replica_groups=mesh['ta'=4,'pa'=4,'dev'=2] {'ta','pa','dev'}, use_global_device_ids=true, to_apply=%region_47.48.clone | all-reduce | flops 4608 | bytes 36864
  2592.0 38.5 %all-reduce = f32[4608]{0:T(1024)S(1)} all-reduce(f32[4608]{0:T(1024)S(1)} %dynamic-slice_dynamic-update-slice_fusion), channel_id=1, replica_groups=mesh['ta'=4,'pa'=4,'dev'=2] {'ta','pa','dev'}, use_global_device_ids=true, to_apply=%add | all-reduce | flops 4608 | bytes 36864
  2634.3 26.7 all-gather.23.cloned.1.call-done
  2664.4 56.9 %all-gather.25.cloned.1.call-done = f32[589824]{0:T(1024)} async-done(((f32[18432]{0:T(1024)}), f32[589824]{0:T(1024)}) %all-gather.25.cloned.1.call-update) | async-done | bytes 2359312 | tf_op jit(solution)/shard_map/all_gather | solution.py:451
  2724.7 56.9 %all-gather.27.cloned.1.call-done = f32[589824]{0:T(1024)} async-done(((f32[18432]{0:T(1024)}), f32[589824]{0:T(1024)}) %all-gather.27.cloned.1.call-update) | async-done | bytes 2359312 | tf_op jit(solution)/shard_map/all_gather | solution.py:452
  2784.9 56.5 %all-gather.29.cloned.1.call-done = f32[589824]{0:T(1024)} async-done(((f32[18432]{0:T(1024)}), f32[589824]{0:T(1024)}) %all-gather.29.cloned.1.call-update) | async-done | bytes 2359312 | tf_op jit(solution)/shard_map/all_gather | solution.py:453
  2844.8 56.2 %all-gather.31.cloned.1.call-done = f32[589824]{0:T(1024)} async-done(((f32[18432]{0:T(1024)}), f32[589824]{0:T(1024)}) %all-gather.31.cloned.1.call-update) | async-done | bytes 2359312 | tf_op jit(solution)/shard_map/all_gather | solution.py:454
  2904.3 56.2 %all-gather.35.cloned.1.call-done = f32[589824]{0:T(1024)} async-done(((f32[18432]{0:T(1024)}), f32[589824]{0:T(1024)}) %all-gather.35.cloned.1.call-update) | async-done | bytes 2359312 | tf_op jit(solution)/shard_map/all_gather | solution.py:456
  2963.9 56.2 %all-gather.33.cloned.1.call-done = f32[589824]{0:T(1024)} async-done(((f32[18432]{0:T(1024)}), f32[589824]{0:T(1024)}) %all-gather.33.cloned.1.call-update) | async-done | bytes 2359312 | tf_op jit(solution)/shard_map/all_gather | solution.py:455
  (1103 shorter events, 868.0 us)
Async XLA Ops:
  14.1 91.4 %all-gather.39.cloned.1.call-start = ((), (), s32[]{:S(2)}) async-start(), calls=%async_computation.14 | async-start | bytes 4915200 | tf_op jit(solution)/shard_map/while/body/eval_jaxpr/all_gather | solution.py:325
  26.7 155.4 %all-gather.37.cloned.1.call-start = ((), (), s32[]{:S(2)}) async-start(), calls=%async_computation.13 | async-start | bytes 4915200 | tf_op jit(solution)/shard_map/while/body/eval_jaxpr/all_gather | solution.py:199
  27.5 256.2 %all-gather.41.cloned.1.call-start = ((), (), s32[]{:S(2)}) async-start(), calls=%async_computation.15 | async-start | bytes 4915200 | tf_op jit(solution)/shard_map/while/body/eval_jaxpr/all_gather | solution.py:238
  32.0 177.4 %copy-start.84 = (bf16[1,120,384]{1,2,0:T(8,128)(2,1)}, bf16[1,120,384]{1,2,0:T(8,128)(2,1)S(1)}, u32[]{:S(2)}) copy-start(bf16[1,120,384]{1,2,0:T(8,128)(2,1)S(1)} %copy.297) | copy-start | bytes 276484 | tf_op jit(solution)/shard_map/while
  32.2 178.7 %copy-start.88 = (bf16[1,120,384]{1,2,0:T(8,128)(2,1)}, bf16[1,120,384]{1,2,0:T(8,128)(2,1)S(1)}, u32[]{:S(2)}) copy-start(bf16[1,120,384]{1,2,0:T(8,128)(2,1)S(1)} %copy.303) | copy-start | bytes 276484 | tf_op jit(solution)/shard_map/while
  38.4 73.3 %copy-start.27 = (bf16[5,256,6,64]{1,3,2,0:T(8,128)(2,1)}, bf16[5,256,6,64]{1,3,2,0:T(8,128)(2,1)S(1)}, u32[]{:S(2)}) copy-start(bf16[5,256,6,64]{1,3,2,0:T(8,128)(2,1)S(1)} %copy.299) | copy-start | bytes 2949124 | tf_op jit(solution)/shard_map/while
  40.3 71.5 %copy-start.130 = (f32[5]{0:T(128)}, f32[5]{0:T(128)S(1)}, u32[]{:S(2)}) copy-start(f32[5]{0:T(128)S(1)} %get-tuple-element.1053) | copy-start | bytes 64 | tf_op jit(solution)/shard_map/while
  40.9 70.8 %copy-start.135 = (f32[384]{0:T(512)}, f32[384]{0:T(512)S(1)}, u32[]{:S(2)}) copy-start(f32[384]{0:T(512)S(1)} %get-tuple-element.1056) | copy-start | bytes 4612 | tf_op jit(solution)/shard_map/while
  40.9 70.8 %copy-start.139 = (f32[384]{0:T(512)}, f32[384]{0:T(512)S(1)}, u32[]{:S(2)}) copy-start(f32[384]{0:T(512)S(1)} %get-tuple-element.1057) | copy-start | bytes 4612 | tf_op jit(solution)/shard_map/while
  126.8 61.6 %copy-start.90 = (f32[5,6,256]{2,1,0:T(8,128)}, f32[5,6,256]{2,1,0:T(8,128)S(1)}, u32[]{:S(2)}) copy-start(f32[5,6,256]{2,1,0:T(8,128)S(1)} %get-tuple-element.1066) | copy-start | bytes 92164 | tf_op jit(solution)/shard_map/while
  141.0 47.4 %copy-start.99 = (f32[5,6,256]{2,1,0:T(8,128)}, f32[5,6,256]{2,1,0:T(8,128)S(1)}, u32[]{:S(2)}) copy-start(f32[5,6,256]{2,1,0:T(8,128)S(1)} %fusion.445) | copy-start | bytes 92164 | tf_op jit(solution)/shard_map/while
  234.4 223.6 %reduce-scatter.13.cloned.1.call-start = ((), (), s32[]{:S(2)}) async-start(), calls=%async_computation.16 | async-start | bytes 9830400 | tf_op jit(solution)/shard_map/while
  370.5 168.1 %all-gather.43.cloned.1.call-start = ((), (), s32[]{:S(2)}) async-start(), calls=%async_computation.17 | async-start | bytes 4915200 | tf_op jit(solution)/shard_map/while/body/eval_jaxpr/all_gather | solution.py:266
  487.9 133.3 %all-reduce.18.cloned.1.call-start = ((), (), s32[]{:S(2)}) async-start(), calls=%async_computation.18 | async-start | bytes 2097152 | tf_op jit(solution)/shard_map/while/body/eval_jaxpr/psum | solution.py:174
  568.5 168.6 %reduce-scatter.15.cloned.1.call-start = ((), (), s32[]{:S(2)}) async-start(), calls=%async_computation.19 | async-start | bytes 9830400 | tf_op jit(solution)/shard_map/while
  653.6 285.7 %reduce-scatter.17.cloned.1.call-start = ((), (), s32[]{:S(2)}) async-start(), calls=%async_computation.20 | async-start | bytes 9830400 | tf_op jit(solution)/shard_map/while/body/eval_jaxpr/reduce_scatter | solution.py:344
  654.4 114.2 %copy-start.86 = (f32[6,1280]{1,0:T(8,128)}, f32[6,1280]{1,0:T(8,128)S(1)}, u32[]{:S(2)}) copy-start(f32[6,1280]{1,0:T(8,128)S(1)} %log_add_fusion.6) | copy-start | bytes 92164 | tf_op jit(solution)/shard_map/while
  802.8 275.6 %reduce-scatter.19.cloned.1.call-start = ((), (), s32[]{:S(2)}) async-start(), calls=%async_computation.21 | async-start | bytes 9830400 | tf_op jit(solution)/shard_map/while/body/eval_jaxpr/reduce_scatter | solution.py:341
  942.3 139.4 %copy-start.73 = (bf16[1280,384]{1,0:T(8,128)(2,1)S(1)}, bf16[1280,384]{1,0:T(8,128)(2,1)}, u32[]{:S(2)}) copy-start(bf16[1280,384]{1,0:T(8,128)(2,1)} %copy-done.72) | copy-start | bytes 2949124 | tf_op jit(solution)/shard_map/while
  1106.4 89.8 %all-gather.39.cloned.1.call-start = ((), (), s32[]{:S(2)}) async-start(), calls=%async_computation.14 | async-start | bytes 4915200 | tf_op jit(solution)/shard_map/while/body/eval_jaxpr/all_gather | solution.py:325
  1119.1 153.8 %all-gather.37.cloned.1.call-start = ((), (), s32[]{:S(2)}) async-start(), calls=%async_computation.13 | async-start | bytes 4915200 | tf_op jit(solution)/shard_map/while/body/eval_jaxpr/all_gather | solution.py:199
  1119.9 254.6 %all-gather.41.cloned.1.call-start = ((), (), s32[]{:S(2)}) async-start(), calls=%async_computation.15 | async-start | bytes 4915200 | tf_op jit(solution)/shard_map/while/body/eval_jaxpr/all_gather | solution.py:238
  1124.4 175.8 %copy-start.84 = (bf16[1,120,384]{1,2,0:T(8,128)(2,1)}, bf16[1,120,384]{1,2,0:T(8,128)(2,1)S(1)}, u32[]{:S(2)}) copy-start(bf16[1,120,384]{1,2,0:T(8,128)(2,1)S(1)} %copy.297) | copy-start | bytes 276484 | tf_op jit(solution)/shard_map/while
  1124.5 177.1 %copy-start.88 = (bf16[1,120,384]{1,2,0:T(8,128)(2,1)}, bf16[1,120,384]{1,2,0:T(8,128)(2,1)S(1)}, u32[]{:S(2)}) copy-start(bf16[1,120,384]{1,2,0:T(8,128)(2,1)S(1)} %copy.303) | copy-start | bytes 276484 | tf_op jit(solution)/shard_map/while
  1130.8 71.7 %copy-start.27 = (bf16[5,256,6,64]{1,3,2,0:T(8,128)(2,1)}, bf16[5,256,6,64]{1,3,2,0:T(8,128)(2,1)S(1)}, u32[]{:S(2)}) copy-start(bf16[5,256,6,64]{1,3,2,0:T(8,128)(2,1)S(1)} %copy.299) | copy-start | bytes 2949124 | tf_op jit(solution)/shard_map/while
  1132.7 69.8 %copy-start.130 = (f32[5]{0:T(128)}, f32[5]{0:T(128)S(1)}, u32[]{:S(2)}) copy-start(f32[5]{0:T(128)S(1)} %get-tuple-element.1053) | copy-start | bytes 64 | tf_op jit(solution)/shard_map/while
  1133.3 69.2 %copy-start.135 = (f32[384]{0:T(512)}, f32[384]{0:T(512)S(1)}, u32[]{:S(2)}) copy-start(f32[384]{0:T(512)S(1)} %get-tuple-element.1056) | copy-start | bytes 4612 | tf_op jit(solution)/shard_map/while
  1133.3 69.2 %copy-start.139 = (f32[384]{0:T(512)}, f32[384]{0:T(512)S(1)}, u32[]{:S(2)}) copy-start(f32[384]{0:T(512)S(1)} %get-tuple-element.1057) | copy-start | bytes 4612 | tf_op jit(solution)/shard_map/while
  1217.6 61.6 %copy-start.90 = (f32[5,6,256]{2,1,0:T(8,128)}, f32[5,6,256]{2,1,0:T(8,128)S(1)}, u32[]{:S(2)}) copy-start(f32[5,6,256]{2,1,0:T(8,128)S(1)} %get-tuple-element.1066) | copy-start | bytes 92164 | tf_op jit(solution)/shard_map/while
  1231.8 47.4 %copy-start.99 = (f32[5,6,256]{2,1,0:T(8,128)}, f32[5,6,256]{2,1,0:T(8,128)S(1)}, u32[]{:S(2)}) copy-start(f32[5,6,256]{2,1,0:T(8,128)S(1)} %fusion.445) | copy-start | bytes 92164 | tf_op jit(solution)/shard_map/while
  1325.2 223.6 %reduce-scatter.13.cloned.1.call-start = ((), (), s32[]{:S(2)}) async-start(), calls=%async_computation.16 | async-start | bytes 9830400 | tf_op jit(solution)/shard_map/while
  1461.2 168.1 %all-gather.43.cloned.1.call-start = ((), (), s32[]{:S(2)}) async-start(), calls=%async_computation.17 | async-start | bytes 4915200 | tf_op jit(solution)/shard_map/while/body/eval_jaxpr/all_gather | solution.py:266
  1578.6 133.3 %all-reduce.18.cloned.1.call-start = ((), (), s32[]{:S(2)}) async-start(), calls=%async_computation.18 | async-start | bytes 2097152 | tf_op jit(solution)/shard_map/while/body/eval_jaxpr/psum | solution.py:174
  1659.2 168.6 %reduce-scatter.15.cloned.1.call-start = ((), (), s32[]{:S(2)}) async-start(), calls=%async_computation.19 | async-start | bytes 9830400 | tf_op jit(solution)/shard_map/while
  1744.3 285.7 %reduce-scatter.17.cloned.1.call-start = ((), (), s32[]{:S(2)}) async-start(), calls=%async_computation.20 | async-start | bytes 9830400 | tf_op jit(solution)/shard_map/while/body/eval_jaxpr/reduce_scatter | solution.py:344
  1745.2 114.2 %copy-start.86 = (f32[6,1280]{1,0:T(8,128)}, f32[6,1280]{1,0:T(8,128)S(1)}, u32[]{:S(2)}) copy-start(f32[6,1280]{1,0:T(8,128)S(1)} %log_add_fusion.6) | copy-start | bytes 92164 | tf_op jit(solution)/shard_map/while
  1893.5 275.5 %reduce-scatter.19.cloned.1.call-start = ((), (), s32[]{:S(2)}) async-start(), calls=%async_computation.21 | async-start | bytes 9830400 | tf_op jit(solution)/shard_map/while/body/eval_jaxpr/reduce_scatter | solution.py:341
  2033.1 139.2 %copy-start.73 = (bf16[1280,384]{1,0:T(8,128)(2,1)S(1)}, bf16[1280,384]{1,0:T(8,128)(2,1)}, u32[]{:S(2)}) copy-start(bf16[1280,384]{1,0:T(8,128)(2,1)} %copy-done.72) | copy-start | bytes 2949124 | tf_op jit(solution)/shard_map/while
  2202.9 334.8 %all-reduce.16.cloned.1.call-start = ((), (), s32[]{:S(2)}) async-start(), calls=%async_computation.12 | async-start | bytes 37748736
  2229.7 320.7 %copy-start.127 = (f32[2,6,384]{2,1,0:T(8,128)S(1)}, f32[2,6,384]{2,1,0:T(8,128)}, u32[]{:S(2)}) copy-start(f32[2,6,384]{2,1,0:T(8,128)} %get-tuple-element.1297) | copy-start | bytes 55300
  2229.7 401.5 %all-gather.21.cloned.1.call-start = ((), (), s32[]{:S(2)}) async-start(), calls=%async_computation.4 | async-start | bytes 2433024 | tf_op jit(solution)/shard_map/all_gather | solution.py:448
  2539.2 121.9 %all-gather.23.cloned.1.call-start = ((), (), s32[]{:S(2)}) async-start(), calls=%async_computation.5 | async-start | bytes 2433024 | tf_op jit(solution)/shard_map/all_gather | solution.py:450
  2540.8 180.6 %all-gather.25.cloned.1.call-start = ((), (), s32[]{:S(2)}) async-start(), calls=%async_computation.6 | async-start | bytes 2433024 | tf_op jit(solution)/shard_map/all_gather | solution.py:451
  2542.4 239.3 %all-gather.27.cloned.1.call-start = ((), (), s32[]{:S(2)}) async-start(), calls=%async_computation.7 | async-start | bytes 2433024 | tf_op jit(solution)/shard_map/all_gather | solution.py:452
  2544.0 297.4 %all-gather.29.cloned.1.call-start = ((), (), s32[]{:S(2)}) async-start(), calls=%async_computation.8 | async-start | bytes 2433024 | tf_op jit(solution)/shard_map/all_gather | solution.py:453
  2545.6 355.4 %all-gather.31.cloned.1.call-start = ((), (), s32[]{:S(2)}) async-start(), calls=%async_computation.9 | async-start | bytes 2433024 | tf_op jit(solution)/shard_map/all_gather | solution.py:454
  2547.2 413.4 %all-gather.35.cloned.1.call-start = ((), (), s32[]{:S(2)}) async-start(), calls=%async_computation.11 | async-start | bytes 2433024 | tf_op jit(solution)/shard_map/all_gather | solution.py:456
  2548.8 471.3 %all-gather.33.cloned.1.call-start = ((), (), s32[]{:S(2)}) async-start(), calls=%async_computation.10 | async-start | bytes 2433024 | tf_op jit(solution)/shard_map/all_gather | solution.py:455
  (295 other events, 1101.5 us)
Sparse Core Ops, SparseCore 0:
  26.9 78.5 all-gather.38
  107.1 75.0 all-gather.36
  234.6 49.0 all-gather.40
  370.6 87.4 reduce-scatter.12
  488.0 50.4 all-gather.42
  568.6 52.5 all-reduce.17
  653.7 83.3 reduce-scatter.14
  802.9 136.2 reduce-scatter.16
  941.7 136.7 reduce-scatter.18
  1119.2 76.9 all-gather.38
  1197.8 74.9 all-gather.36
  1325.3 49.0 all-gather.40
  1461.3 87.4 reduce-scatter.12
  1578.8 50.4 all-gather.42
  1659.4 52.5 all-reduce.17
  1744.5 83.3 reduce-scatter.14
  1893.7 136.2 reduce-scatter.16
  2032.3 136.7 reduce-scatter.18
Sparse Core Ops, SparseCore 1:
  2229.8 307.8 all-reduce.15
  2541.5 59.1 all-gather.20
  2604.6 56.4 all-gather.22
  2665.1 56.2 all-gather.24
  2725.4 56.2 all-gather.26
  2785.2 56.2 all-gather.28
  2844.7 56.2 all-gather.30
  2904.3 56.2 all-gather.34
  2963.9 56.2 all-gather.32
where the time goes:
time: 3040 us; the launch traced here: 3030 us
  waiting for transfers between devices  1740 us (57%)
  matrix products  540 us (18%)
  local copies, waits for them, and re-layouts  421 us (14%)
  other arithmetic  193 us (6%)
  blocking collectives  113 us (4%)
    unnamed x10, waiting for transfers between devices  308 us
    while x22, waiting for transfers between devices  272 us
    reduce_scatter x2, waiting for transfers between devices, clip_step(): lax.psum_scatter(d_whole_k.reshape(back_keys.shape), 'pa', scatter_dimens...  272 us
    all_gather x2, waiting for transfers between devices, clip_step(): lax.all_gather(space_keys, 'pa', axis=1, tiled=True)  126 us
    psum x2, waiting for transfers between devices, frame_centre(): return lax.psum(values, 'ta')  105 us
    all_gather x2, waiting for transfers between devices, clip_step(): lax.all_gather(d_frame_att.reshape(cube_shape), 'ta', axis=0, tiled=True)  101 us
    all_gather x2, waiting for transfers between devices, clip_step(): lax.all_gather(frame_qkv[0].reshape(cube_shape), 'ta', axis=0, tiled=True)  84.2 us
    all_gather x2, waiting for transfers between devices, clip_step(): lax.all_gather(space_values, 'pa', axis=1, tiled=True)  82.2 us
  transfers between devices with their start and end apart: 27, of which 26 were waited for; matrix products, arithmetic and copies ran while one was open for 15% of the time, Pallas kernels for 0%

commit v1 on v0

v1 whole, which is shorter than its diff:
```python
import math

import jax
import jax.numpy as jnp
from jax import lax
from jax.experimental import pallas as pl
from jax.experimental.pallas import tpu as pltpu
from jax.sharding import PartitionSpec as P

HEADS = 6
HDIM = 64
PAIRS = HEADS // 2
LANES = 2 * HDIM
EPSILON = 1e-06
MASKED_SCORE = -1e30
HIGHEST = lax.Precision.HIGHEST
F32 = jnp.float32
BF = jnp.bfloat16
VMEM_BYTES = 60 * 2**20
SUM_ROWS = 16
FRAME_GROUPS = ((0, 1, 2, 3, 4),)
BLOCK = 16


def dot(a, b):
    return jnp.dot(a, b, preferred_element_type=F32)


def dot_nt(a, b):
    return lax.dot_general(a, b, (((1,), (1,)), ((), ())), preferred_element_type=F32)


def norm_parts(values):
    centred = values - jnp.mean(values, axis=-1, keepdims=True)
    inverse = lax.rsqrt(jnp.mean(centred * centred, axis=-1, keepdims=True) + EPSILON)
    return centred * inverse, inverse


def norm_back(d_normed, hat, inverse, scale_by):
    d_hat = d_normed * (1.0 + scale_by)
    mean_d = jnp.mean(d_hat, axis=-1, keepdims=True)
    mean_dh = jnp.mean(d_hat * hat, axis=-1, keepdims=True)
    return inverse * (d_hat - mean_d - hat * mean_dh)


GELU_A = math.sqrt(2.0 / math.pi)
GELU_B = 0.044715


def gelu_parts(values):
    square = values * values
    bent = jnp.tanh(GELU_A * values * (1.0 + GELU_B * square))
    half = 0.5 * (1.0 + bent)
    slope = half + (0.5 * GELU_A) * values * (1.0 - bent * bent) * (1.0 + 3.0 * GELU_B * square)
    return values * half, slope


def row_sums(values):
    return jnp.sum(values, axis=0, keepdims=True)


def head_lanes(values, head):
    lane = lax.broadcasted_iota(jnp.int32, values.shape, 1)
    return jnp.where((lane >= HDIM) == (head % 2 == 1), values, jnp.zeros_like(values))


def pair_of(values, pair):
    return values[:, pair * LANES : (pair + 1) * LANES]


def head_rows(values, head):
    return values[head * HDIM : (head + 1) * HDIM, :]


def lone_rows(values, head):
    rows = head_rows(values, head)
    blank = jnp.zeros_like(rows)
    return jnp.concatenate([rows, blank] if head % 2 == 0 else [blank, rows], axis=0)


def attend(queries, keys, values_t, bias, keep_exponent):
    ones = jnp.ones((SUM_ROWS, values_t.shape[1]), BF)
    parts, inverses = [], []
    for head in range(HEADS):
        pair = head // 2
        scores = dot_nt(pair_of(keys, pair), head_lanes(pair_of(queries, pair), head))
        if bias is not None:
            scores = scores + bias
        largest = jnp.max(scores, axis=0, keepdims=True)
        exponent = jnp.exp(scores - largest).astype(BF)
        keep_exponent(head, exponent)
        lifted = jnp.concatenate([head_rows(values_t, head), ones], axis=0)
        summed = dot(lifted, exponent)
        inverse = 1.0 / summed[HDIM : HDIM + 1, :]
        parts.append(summed[:HDIM, :] * inverse)
        inverses.append(inverse)
    return jnp.concatenate(parts, axis=0), inverses


def attend_back(exponent_of, queries_of, keys_t_of, values_of, d_att_t, att_t, inverse_of, keys_chunk):
    n_keys, chunk = keys_chunk
    d_query_parts, d_key_pairs, d_value_pairs = [], [], []
    for pair in range(PAIRS):
        d_keys = [None] * (n_keys // chunk)
        d_values = [None] * (n_keys // chunk)
        for head in (2 * pair, 2 * pair + 1):
            inverse = inverse_of(head)
            d_att_head = head_rows(d_att_t, head)
            centre = row_sums(d_att_head * head_rows(att_t, head)) * inverse
            scaled = (d_att_head * inverse).astype(BF)
            blank = jnp.zeros_like(scaled)
            scaled_pair = jnp.concatenate([scaled, blank] if head % 2 == 0 else [blank, scaled], axis=0)
            query_pair = head_lanes(queries_of(pair), head)
            d_query = None
            for at in range(n_keys // chunk):
                rows = slice(at * chunk, (at + 1) * chunk)
                exponent = exponent_of(head, rows)
                d_chance = dot(values_of(pair, rows), scaled_pair)
                d_score = (exponent.astype(F32) * (d_chance - centre)).astype(BF)
                d_value = dot_nt(exponent, scaled_pair)
                d_key = dot(d_score, query_pair)
                part = dot(keys_t_of(head, rows), d_score)
                d_query = part if d_query is None else d_query + part
                d_keys[at] = d_key if d_keys[at] is None else d_keys[at] + d_key
                d_values[at] = d_value if d_values[at] is None else d_values[at] + d_value
            d_query_parts.append(d_query)
        d_key_pairs.append(jnp.concatenate(d_keys, axis=0))
        d_value_pairs.append(jnp.concatenate(d_values, axis=0))
    return (
        jnp.concatenate(d_query_parts, axis=0),
        jnp.concatenate(d_key_pairs, axis=1),
        jnp.concatenate(d_value_pairs, axis=1),
    )


def fold(ref):
    value = ref[...]
    return value.reshape(-1, value.shape[-1])


def space_forward_kernel(
    first_frame,
    counts_ref,
    own_ref,
    other_ref,
    mod_ref,
    attn_ref,
    turned_ref,
    cross_ref,
    text_keys_ref,
    text_values_t_ref,
    up_ref,
    down_ref,
    state_ref,
    normed_ref,
    query_ref,
    keys_t_ref,
    value_ref,
    exponent_ref,
    att_t_ref,
    att_ref,
    inverse_ref,
    cross_in_ref,
    cross_query_ref,
    cross_exponent_ref,
    cross_att_t_ref,
    cross_att_ref,
    cross_inverse_ref,
    middle_ref,
    normed2_ref,
    act_ref,
    slope_ref,
):
    scale_by = HDIM ** (-0.5)
    frame = counts_ref[2] + first_frame + pl.program_id(0)
    keep = (frame < counts_ref[0]).astype(F32)
    mod = mod_ref[...]
    own = fold(own_ref).astype(F32)
    rows = own.shape[0]
    normed_own = (norm_parts(own)[0] * (1.0 + mod[1:2]) + mod[0:1]).astype(BF)
    normed_other = (norm_parts(fold(other_ref).astype(F32))[0] * (1.0 + mod[1:2]) + mod[0:1]).astype(BF)
    normed = jnp.concatenate([normed_own, normed_other], axis=0)
    normed_ref[0] = normed
    queries = (dot(normed_own, attn_ref[0]).astype(BF) * scale_by).astype(BF)
    keys = dot(normed, attn_ref[1]).astype(BF)
    values = dot(normed, attn_ref[2]).astype(BF)
    query_ref[0] = queries
    value_ref[0] = values
    keys_t_ref[0] = dot_nt(turned_ref[0], normed).astype(BF)
    values_t = dot_nt(turned_ref[1], normed).astype(BF)

    def keep_exponent(head, exponent):
        exponent_ref[0, head] = exponent

    att_t, inverses = attend(queries, keys, values_t, None, keep_exponent)
    for head in range(HEADS):
        inverse_ref[0, head : head + 1, :] = inverses[head]
    att_t_ref[0] = att_t.astype(BF)
    att = att_t.T.astype(BF)
    att_ref[0] = att
    state = own + (keep * mod[2:3]) * dot(att, attn_ref[3])
    cross_in = state.astype(BF)
    cross_in_ref[0] = cross_in
    cross_queries = (dot(cross_in, cross_ref[0]).astype(BF) * scale_by).astype(BF)
    cross_query_ref[0] = cross_queries
    text_id = lax.broadcasted_iota(jnp.int32, (text_keys_ref.shape[0], rows), 0)
    bias = jnp.where(text_id < counts_ref[1], 0.0, MASKED_SCORE)

    def keep_cross(head, exponent):
        cross_exponent_ref[0, head] = exponent

    cross_t, inverses = attend(cross_queries, text_keys_ref[...], text_values_t_ref[...], bias, keep_cross)
    for head in range(HEADS):
        cross_inverse_ref[0, head : head + 1, :] = inverses[head]
    cross_att_t_ref[0] = cross_t.astype(BF)
    cross_att = cross_t.T.astype(BF)
    cross_att_ref[0] = cross_att
    state = state + keep * dot(cross_att, cross_ref[1])
    middle_ref[0] = state
    normed2 = (norm_parts(state)[0] * (1.0 + mod[4:5]) + mod[3:4]).astype(BF)
    normed2_ref[0] = normed2
    act, slope = gelu_parts(dot(normed2, up_ref[...]))
    act = act.astype(BF)
    act_ref[0] = act
    slope_ref[0] = slope.astype(BF)
    state = state + (keep * mod[5:6]) * dot(act, down_ref[...])
    state_ref[0] = state.astype(BF)


def space_backward_kernel(
    first_frame,
    counts_ref,
    grad_ref,
    mod_ref,
    attn_ref,
    cross_ref,
    text_keys_t_ref,
    text_values_ref,
    up_ref,
    down_ref,
    query_ref,
    keys_t_ref,
    value_ref,
    exponent_ref,
    att_t_ref,
    inverse_ref,
    cross_query_ref,
    cross_exponent_ref,
    cross_att_t_ref,
    cross_inverse_ref,
    middle_ref,
    slope_ref,
    state_grad_ref,
    own_grad_ref,
    other_grad_ref,
    kept3_ref,
    d_lifted_ref,
    kept2_ref,
    d_cross_query_ref,
    kept1_ref,
    d_query_ref,
    d_key_ref,
    d_value_ref,
    d_text_keys_ref,
    d_text_values_ref,
    mods_ref,
):
    scale_by = HDIM ** (-0.5)
    frame = counts_ref[2] + first_frame + pl.program_id(0)
    keep = (frame < counts_ref[0]).astype(F32)
    mod = mod_ref[...]
    grad = fold(grad_ref).astype(F32)
    rows = grad.shape[0]
    kept = keep * grad
    kept3_ref[0] = kept.astype(BF)
    d_act = dot_nt((kept * mod[5:6]).astype(BF), down_ref[...])
    d_lifted = (d_act * slope_ref[0].astype(F32)).astype(BF)
    d_lifted_ref[0] = d_lifted
    d_normed = dot_nt(d_lifted, up_ref[...])
    hat, inverse = norm_parts(middle_ref[0])
    grad = grad + norm_back(d_normed, hat, inverse, mod[4:5])
    mods_ref[0] = jnp.concatenate(
        [row_sums(d_normed), row_sums(d_normed * hat), jnp.zeros((6, hat.shape[1]), F32)], axis=0
    )
    kept = (keep * grad).astype(BF)
    kept2_ref[0] = kept
    d_att_t = dot_nt(cross_ref[1], kept)
    d_query_t, d_keys, d_values = attend_back(
        lambda head, at: cross_exponent_ref[0, head, at, :],
        lambda pair: cross_query_ref[0, :, pair * LANES : (pair + 1) * LANES],
        lambda head, at: text_keys_t_ref[head * HDIM : (head + 1) * HDIM, at],
        lambda pair, at: text_values_ref[at, pair * LANES : (pair + 1) * LANES],
        d_att_t,
        cross_att_t_ref[0].astype(F32),
        lambda head: cross_inverse_ref[0, head : head + 1, :],
        (text_values_ref.shape[0], text_values_ref.shape[0]),
    )
    d_text_keys_ref[0] = d_keys
    d_text_values_ref[0] = d_values
    d_query = (d_query_t.T * scale_by).astype(BF)
    d_cross_query_ref[0] = d_query
    grad = grad + dot_nt(d_query, cross_ref[0])
    state_grad_ref[0] = grad
    kept = keep * grad
    kept1_ref[0] = kept.astype(BF)
    d_att_t = dot_nt(attn_ref[3], (kept * mod[2:3]).astype(BF))
    n_keys = value_ref.shape[1]
    d_query_t, d_keys, d_values = attend_back(
        lambda head, at: exponent_ref[0, head, at, :],
        lambda pair: query_ref[0, :, pair * LANES : (pair + 1) * LANES],
        lambda head, at: keys_t_ref[0, head * HDIM : (head + 1) * HDIM, at],
        lambda pair, at: value_ref[0, at, pair * LANES : (pair + 1) * LANES],
        d_att_t,
        att_t_ref[0].astype(F32),
        lambda head: inverse_ref[0, head : head + 1, :],
        (n_keys, min(n_keys, 256)),
    )
    d_query = (d_query_t.T * scale_by).astype(BF)
    d_keys, d_values = d_keys.astype(BF), d_values.astype(BF)
    d_query_ref[0] = d_query
    d_key_ref[0] = d_keys
    d_value_ref[0] = d_values
    d_normed = dot_nt(d_keys, attn_ref[1]) + dot_nt(d_values, attn_ref[2])
    own_grad_ref[0] = d_normed[:rows] + dot_nt(d_query, attn_ref[0])
    other_grad_ref[0] = d_normed[rows:].astype(BF)


def space_finish_kernel(n_parts, own_ref, state_grad_ref, own_grad_ref, *rest):
    parts, (mod_ref, out_ref, mods_ref) = rest[:n_parts], rest[n_parts:]
    d_normed = own_grad_ref[0]
    for part in parts:
        d_normed = d_normed + part[0].astype(F32)
    hat, inverse = norm_parts(fold(own_ref).astype(F32))
    grad = state_grad_ref[0] + norm_back(d_normed, hat, inverse, mod_ref[1:2, :])
    out_ref[...] = grad.astype(BF).reshape(out_ref.shape)
    mods_ref[0] = jnp.concatenate(
        [row_sums(d_normed), row_sums(d_normed * hat), jnp.zeros((6, hat.shape[1]), F32)], axis=0
    )


def time_kernel(
    counts_ref,
    state_ref,
    cot_ref,
    mod_ref,
    bias_ref,
    attn_ref,
    turned_ref,
    up_ref,
    down_ref,
    out_ref,
    grad_ref,
    normed_ref,
    d_qkv_ref,
    att_ref,
    kept4_ref,
    normed2_ref,
    act_ref,
    d_lifted_ref,
    kept5_ref,
    mods_ref,
    exponent_ref,
):
    scale_by = HDIM ** (-0.5)
    block = state_ref.shape
    mod = mod_ref[...]

    def put(ref, value):
        ref[...] = value.reshape(ref.shape)

    state = fold(state_ref).astype(F32)
    rows = state.shape[0]
    frame = lax.broadcasted_iota(jnp.int32, (rows, 1), 0) // block[1]
    keep = (frame < counts_ref[0]).astype(F32)
    hat1, inverse1 = norm_parts(state)
    normed = (hat1 * (1.0 + mod[1:2]) + mod[0:1]).astype(BF)
    put(normed_ref, normed)
    queries = (dot(normed, attn_ref[0]).astype(BF) * scale_by).astype(BF)
    keys = dot(normed, attn_ref[1]).astype(BF)
    values = dot(normed, attn_ref[2]).astype(BF)
    keys_t = dot_nt(turned_ref[0], normed).astype(BF)
    values_t = dot_nt(turned_ref[1], normed).astype(BF)

    def keep_exponent(head, exponent):
        exponent_ref[head] = exponent

    att_t, inverses = attend(queries, keys, values_t, bias_ref[...], keep_exponent)
    att = att_t.T.astype(BF)
    put(att_ref, att)
    state = state + (keep * mod[2:3]) * dot(att, attn_ref[3])
    hat2, inverse2 = norm_parts(state)
    normed2 = (hat2 * (1.0 + mod[4:5]) + mod[3:4]).astype(BF)
    put(normed2_ref, normed2)
    act, slope = gelu_parts(dot(normed2, up_ref[...]))
    act = act.astype(BF)
    put(act_ref, act)
    put(out_ref, (state + (keep * mod[5:6]) * dot(act, down_ref[...])).astype(BF))
    grad = fold(cot_ref).astype(F32)
    kept = keep * grad
    put(kept5_ref, kept.astype(BF))
    d_act = dot_nt((kept * mod[5:6]).astype(BF), down_ref[...])
    d_lifted = (d_act * slope).astype(BF)
    put(d_lifted_ref, d_lifted)
    d_normed2 = dot_nt(d_lifted, up_ref[...])
    grad = grad + norm_back(d_normed2, hat2, inverse2, mod[4:5])
    kept = keep * grad
    put(kept4_ref, kept.astype(BF))
    d_att_t = dot_nt(attn_ref[3], (kept * mod[2:3]).astype(BF))
    d_query_t, d_keys, d_values = attend_back(
        lambda head, at: exponent_ref[head, at, :],
        lambda pair: pair_of(queries, pair),
        lambda head, at: head_rows(keys_t, head)[:, at],
        lambda pair, at: pair_of(values, pair)[at],
        d_att_t,
        att_t,
        lambda head: inverses[head],
        (rows, rows),
    )
    d_qkv = jnp.concatenate(
        [(d_query_t.T * scale_by).astype(BF), d_keys.astype(BF), d_values.astype(BF)], axis=1
    )
    put(d_qkv_ref, d_qkv)
    width = hat1.shape[1]
    d_normed1 = (
        dot_nt(d_qkv[:, :width], attn_ref[0])
        + dot_nt(d_qkv[:, width : 2 * width], attn_ref[1])
        + dot_nt(d_qkv[:, 2 * width :], attn_ref[2])
    )
    grad = grad + norm_back(d_normed1, hat1, inverse1, mod[1:2])
    put(grad_ref, grad.astype(BF))
    mods_ref[0] = jnp.concatenate(
        [
            row_sums(d_normed1),
            row_sums(d_normed1 * hat1),
            row_sums(d_normed2),
            row_sums(d_normed2 * hat2),
            jnp.zeros((4, width), F32),
        ],
        axis=0,
    )


def whole(array):
    zeros = (0,) * array.ndim
    return pl.BlockSpec(array.shape, lambda *grid: zeros)


def framed(array):
    tail = (0,) * (array.ndim - 1)
    return pl.BlockSpec((1,) + tuple(array.shape[1:]), lambda frame: (frame,) + tail)


SCALARS = pl.BlockSpec(memory_space=pltpu.SMEM)


def shape_of(shape, dtype):
    return jax.ShapeDtypeStruct(shape, dtype)


def call(kernel, grid, inputs, in_specs, outputs, out_specs, flops, scratch=()):
    moved = sum(math.prod(a.shape) * a.dtype.itemsize for a in (*inputs, *outputs))
    return pl.pallas_call(
        kernel,
        grid=grid,
        in_specs=in_specs,
        out_specs=out_specs,
        out_shape=outputs,
        scratch_shapes=list(scratch),
        compiler_params=pltpu.CompilerParams(vmem_limit_bytes=VMEM_BYTES),
        cost_estimate=pl.CostEstimate(flops=int(flops), bytes_accessed=int(moved), transcendentals=0),
    )(*inputs)


def make_per_device(n_ta, n_pa, n_dev):
    def per_device(
        latents,
        context,
        cotangent,
        timesteps,
        frame_counts,
        text_lengths,
        step_proj,
        mod_table,
        patch_attn,
        cross_attn,
        patch_up,
        patch_down,
        frame_attn,
        frame_up,
        frame_down,
    ):
        clips_dev, frames, patches, width = latents.shape
        clips = clips_dev * n_dev
        run = n_pa // clips
        group = run * n_dev
        near = n_pa // group
        space_rows = near * patches
        time_patches = space_rows // n_ta
        other_rows = (group - 1) * space_rows
        key_rows = group * space_rows
        all_frames = n_ta * frames
        ta, pa, dev = (lax.axis_index(name) for name in ("ta", "pa", "dev"))
        clip = pa // run
        member = dev * run + pa % run

        def place(clip_id, member_id):
            return (clip_id * run + member_id % run) * n_dev + member_id // run

        def space_pairs(step):
            pairs = []
            for p in range(n_pa):
                for d in range(n_dev):
                    k = d * clips_dev + (p + step) % clips_dev
                    pairs.append((p * n_dev + d, place(k, p // near)))
            return pairs

        halves = n_ta // near

        def time_pairs(step):
            u, w = step % halves, step // halves
            pairs = []
            for t in range(n_ta):
                for p in range(n_pa):
                    for d in range(n_dev):
                        s = (t % halves + u) % halves
                        j = (t // halves + w) % clips_dev
                        k = d * clips_dev + j
                        pairs.append(
                            (
                                (t * n_pa + p) * n_dev + d,
                                ((p % near) * halves + s) * n_pa * n_dev + place(k, p // near),
                            )
                        )
            return pairs

        def back(pairs):
            return [(b, a) for a, b in pairs]

        def group_pairs(step):
            return [
                (place(k, g), place(k, (g + step) % group)) for k in range(clips) for g in range(group)
            ]

        def ta_pairs(step):
            return [(t, t ^ step) for t in range(n_ta)]

        whole_axes = ("ta", "pa", "dev")
        pair_axes = ("pa", "dev")

        def of_clip(local):
            both = lax.all_gather(local, "dev", axis=0, tiled=True)
            return lax.dynamic_index_in_dim(both, clip, 0, keepdims=False)

        def sinusoid(steps):
            half = step_proj.shape[0] // 2
            frequency = jnp.exp(-math.log(10000.0) * jnp.arange(half, dtype=F32) / half)
            angles = steps.astype(F32)[:, None] * frequency[None, :]
            return jnp.concatenate([jnp.cos(angles), jnp.sin(angles)], axis=1)

        numbers = lax.all_gather(jnp.stack([timesteps, frame_counts, text_lengths], axis=1), "dev", axis=0, tiled=True)
        own_numbers = lax.dynamic_index_in_dim(numbers, clip, 0, keepdims=False)
        embeddings = sinusoid(numbers[:, 0])
        embedding = lax.dynamic_index_in_dim(embeddings, clip, 0, keepdims=True)
        timing = jnp.dot(embedding, step_proj.astype(F32), precision=HIGHEST).reshape(6, width)
        table = mod_table.astype(F32)
        pad = jnp.zeros((2, width), F32)
        space_mod = jnp.concatenate([timing + table[0], pad])
        frame_mod = jnp.concatenate([timing + table[1], pad])
        counts = jnp.stack([own_numbers[1], own_numbers[2], ta * frames, 0]).astype(jnp.int32)
        text = of_clip(context)
        text_count = text.shape[0]
        text_rows = -(-text_count // LANES) * LANES
        text_wide = jnp.pad(text, ((0, text_rows - text_count), (0, 0)))
        text_keys = dot(text_wide, cross_attn[1]).astype(BF)
        text_values = dot(text_wide, cross_attn[2]).astype(BF)
        cross_ends = jnp.stack([cross_attn[0], cross_attn[3]])
        patch_turned = jnp.swapaxes(patch_attn[1:3], 1, 2)
        frame_turned = jnp.swapaxes(frame_attn[1:3], 1, 2)

        def to_space(frame_ids):
            picked = latents[:, frame_ids[0] : frame_ids[-1] + 1]
            parts = []
            for step in range(clips_dev):
                sent = lax.dynamic_index_in_dim(picked, (pa + step) % clips_dev, 0, keepdims=False)
                parts.append(lax.ppermute(sent, pair_axes, space_pairs(step)))
            stacked = jnp.stack(parts)
            slots = [
                lax.dynamic_index_in_dim(stacked, (clip - b) % clips_dev, 0, keepdims=False) for b in range(near)
            ]
            own = jnp.concatenate(slots, axis=1)
            others = [lax.ppermute(own, pair_axes, group_pairs(step)) for step in range(1, group)]
            return own, jnp.concatenate(others, axis=1)

        def space_forward(frame_ids, own, other):
            count = len(frame_ids)

            def out(*shape, dtype=BF):
                return shape_of((count,) + shape, dtype)

            inputs = (
                counts, own, other, space_mod, patch_attn, patch_turned, cross_ends, text_keys, text_values.T,
                patch_up, patch_down,
            )
            hidden = patch_up.shape[1]
            outputs = (
                out(space_rows, width),
                out(key_rows, width),
                out(space_rows, width),
                out(width, key_rows),
                out(key_rows, width),
                out(HEADS, key_rows, space_rows),
                out(width, space_rows),
                out(space_rows, width),
                out(8, space_rows, dtype=F32),
                out(space_rows, width),
                out(space_rows, width),
                out(HEADS, text_rows, space_rows),
                out(width, space_rows),
                out(space_rows, width),
                out(8, space_rows, dtype=F32),
                out(space_rows, width, dtype=F32),
                out(space_rows, width),
                out(space_rows, hidden),
                out(space_rows, hidden),
            )
            dense = 2 * count * space_rows * width * (6 * width + 2 * hidden) + 8 * count * key_rows * width * width
            return call(
                lambda *refs: space_forward_kernel(frame_ids[0], *refs),
                (count,),
                inputs,
                [SCALARS, framed(own), framed(other)] + [whole(a) for a in inputs[3:]],
                outputs,
                [framed(a) for a in outputs],
                dense + 16 * count * space_rows * key_rows * width,
            )

        def space_backward(frame_ids, grad, saved):
            count = len(frame_ids)

            def out(*shape, dtype=BF):
                return shape_of((count,) + shape, dtype)

            (_, _, query, keys_t, value, exponent, att_t, _, inverse, _, cross_query, cross_exponent, cross_att_t, _,
             cross_inverse, middle, _, _, slope) = saved
            inputs = (
                counts, grad, space_mod, patch_attn, cross_ends, text_keys.T, text_values, patch_up, patch_down,
                query, keys_t, value, exponent, att_t, inverse, cross_query, cross_exponent, cross_att_t,
                cross_inverse, middle, slope,
            )
            hidden = patch_up.shape[1]
            outputs = (
                out(space_rows, width, dtype=F32),
                out(space_rows, width, dtype=F32),
                out(other_rows, width),
                out(space_rows, width),
                out(space_rows, hidden),
                out(space_rows, width),
                out(space_rows, width),
                out(space_rows, width),
                out(space_rows, width),
                out(key_rows, width),
                out(key_rows, width),
                out(text_rows, width, dtype=F32),
                out(text_rows, width, dtype=F32),
                out(8, width, dtype=F32),
            )
            grad_spec = pl.BlockSpec((n_ta, 1, time_patches, width), lambda frame: (0, frame, 0, 0))
            dense = 2 * count * space_rows * width * (6 * width + 2 * hidden) + 8 * count * key_rows * width * width
            return call(
                lambda *refs: space_backward_kernel(frame_ids[0], *refs),
                (count,),
                inputs,
                [SCALARS, grad_spec] + [whole(a) for a in inputs[2:9]] + [framed(a) for a in inputs[9:]],
                outputs,
                [framed(a) for a in outputs],
                dense + 32 * count * space_rows * key_rows * width,
            )

        def space_finish(own, state_grad, own_grad, parts):
            count = own.shape[0]
            inputs = (own, state_grad, own_grad, *parts, space_mod)
            outputs = (
                shape_of((count, near, patches, width), BF),
                shape_of((count, 8, width), F32),
            )
            return call(
                lambda *refs: space_finish_kernel(len(parts), *refs),
                (count,),
                inputs,
                [framed(a) for a in inputs[:-1]] + [whole(space_mod)],
                outputs,
                [framed(a) for a in outputs],
                count * space_rows * width * 30,
            )

        owns, saves, states = [], [], []
        for frame_ids in FRAME_GROUPS:
            own, other = to_space(frame_ids)
            saved = space_forward(frame_ids, own, other)
            owns.append(own)
            saves.append(saved)
            states.append(saved[0])

        n_steps = halves * clips_dev
        cot_parts = []
        for step in range(n_steps):
            u, w = step % halves, step // halves
            s = (ta % halves + u) % halves
            j = (ta // halves + w) % clips_dev
            sent = lax.dynamic_slice(
                cotangent, (j, 0, s * time_patches, 0), (1, frames, time_patches, width)
            )[0]
            cot_parts.append(lax.ppermute(sent, whole_axes, time_pairs(step)))
        cot_stack = jnp.stack(cot_parts)
        slot = ta % halves

        def step_from(source):
            u = (slot - source % halves) % halves
            w = (clip % clips_dev - source // halves) % clips_dev
            return w * halves + u

        cot = jnp.concatenate(
            [lax.dynamic_index_in_dim(cot_stack, step_from(t), 0, keepdims=False) for t in range(n_ta)]
        )

        def exchange(pieces):
            got = [lax.dynamic_index_in_dim(pieces, ta, 0, keepdims=False)]
            for step in range(1, n_ta):
                sent = lax.dynamic_index_in_dim(pieces, ta ^ step, 0, keepdims=False)
                got.append(lax.ppermute(sent, "ta", ta_pairs(step)))
            stacked = jnp.stack(got)
            return jnp.stack(
                [lax.dynamic_index_in_dim(stacked, ta ^ t, 0, keepdims=False) for t in range(n_ta)]
            )

        state_groups = []
        for state in states:
            pieces = state.reshape(state.shape[0], n_ta, time_patches, width).swapaxes(0, 1)
            state_groups.append(exchange(pieces))
        state = jnp.concatenate(state_groups, axis=1).reshape(all_frames, time_patches, width)

        block_rows = all_frames * BLOCK
        ids = jnp.arange(block_rows, dtype=jnp.int32)
        same = (ids[:, None] % BLOCK == ids[None, :] % BLOCK) & (ids[:, None] // BLOCK < counts[0])
        bias = jnp.where(same, 0.0, MASKED_SCORE).astype(F32)
        hidden = frame_up.shape[1]
        n_blocks = time_patches // BLOCK

        def tokens(features):
            return shape_of((all_frames, time_patches, features), BF)

        time_inputs = (counts, state, cot, frame_mod, bias, frame_attn, frame_turned, frame_up, frame_down)
        time_outputs = (
            tokens(width),
            tokens(width),
            tokens(width),
            tokens(3 * width),
            tokens(width),
            tokens(width),
            tokens(width),
            tokens(hidden),
            tokens(hidden),
            tokens(width),
            shape_of((n_blocks, 8, width), F32),
        )

        def blocked(array):
            return pl.BlockSpec((all_frames, BLOCK, array.shape[2]), lambda at: (0, at, 0))

        (out_t, grad_t, normed_t, d_qkv_t, att_tt, kept4, normed4, act4, d_lifted4, kept5, frame_mods) = call(
            time_kernel,
            (n_blocks,),
            time_inputs,
            [SCALARS, blocked(state), blocked(cot)] + [whole(a) for a in time_inputs[3:]],
            time_outputs,
            [blocked(a) for a in time_outputs[:-1]] + [framed(time_outputs[-1])],
            all_frames * time_patches * width * (24 * width + 12 * hidden),
            [pltpu.VMEM((HEADS, block_rows, block_rows), BF)],
        )

        out_pieces = out_t.reshape(n_ta, frames, time_patches, width)
        out_parts = []
        for step in range(n_steps):
            u, w = step % halves, step // halves
            source = (slot - u) % halves + halves * ((clip % clips_dev - w) % clips_dev)
            sent = lax.dynamic_index_in_dim(out_pieces, source, 0, keepdims=False)
            out_parts.append(lax.ppermute(sent, whole_axes, back(time_pairs(step))))
        out_stack = jnp.stack(out_parts)
        rows = []
        for j in range(clips_dev):
            runs = []
            for s in range(halves):
                step = ((j - ta // halves) % clips_dev) * halves + (s - ta % halves) % halves
                runs.append(lax.dynamic_index_in_dim(out_stack, step, 0, keepdims=False))
            rows.append(jnp.concatenate(runs, axis=1))
        output = jnp.stack(rows)

        grad_s = exchange(grad_t.reshape(n_ta, frames, time_patches, width))

        def weight_grad(left, right):
            n = left.ndim - 1
            axes = tuple(range(n))
            return lax.dot_general(left, right, ((axes, axes), ((), ())), preferred_element_type=F32)

        def gated(product, gate, weight):
            return product * gate, jnp.sum(weight.astype(F32) * product, axis=0)

        d_frame_qkv = weight_grad(normed_t, d_qkv_t).reshape(width, 3, width).swapaxes(0, 1)
        d_frame_proj, d_gate2_t = gated(weight_grad(att_tt, kept4), frame_mod[2], frame_attn[3])
        d_frame_up = weight_grad(normed4, d_lifted4)
        d_frame_down, d_gate5_t = gated(weight_grad(act4, kept5), frame_mod[5], frame_down)
        frame_mods = jnp.sum(frame_mods, axis=0)

        def summed(arrays):
            flat = jnp.concatenate([a.reshape(-1).astype(BF) for a in arrays])
            total = lax.psum(flat, whole_axes).astype(F32)
            results, at = [], 0
            for a in arrays:
                results.append(total[at : at + a.size].reshape(a.shape))
                at += a.size
            return results

        d_frame_attn = jnp.concatenate([d_frame_qkv, d_frame_proj[None]])
        d_frame_attn, d_frame_up, d_frame_down = summed([d_frame_attn, d_frame_up, d_frame_down])

        pieces = []
        finished, first_mods, backs = [], [], []
        for frame_ids, own, saved in zip(FRAME_GROUPS, owns, saves):
            grad = grad_s[:, frame_ids[0] : frame_ids[-1] + 1]
            backed = space_backward(frame_ids, grad, saved)
            backs.append(backed)
            other_grad = backed[2]
            parts = []
            for step in range(1, group):
                sent = other_grad[:, (step - 1) * space_rows : step * space_rows]
                parts.append(lax.ppermute(sent, pair_axes, back(group_pairs(step))))
            done, mods = space_finish(own, backed[0], backed[1], parts)
            finished.append(done)
            first_mods.append(jnp.sum(mods, axis=0))
            got = []
            for step in range(clips_dev):
                b = (clip - step) % clips_dev
                sent = lax.dynamic_index_in_dim(done, b, 1, keepdims=False)
                got.append(lax.ppermute(sent, pair_axes, back(space_pairs(step))))
            stacked = jnp.stack(got)
            pieces.append(
                jnp.stack(
                    [
                        lax.dynamic_index_in_dim(stacked, (j - pa) % clips_dev, 0, keepdims=False)
                        for j in range(clips_dev)
                    ]
                )
            )
        latents_grad = jnp.concatenate(pieces, axis=1).astype(F32)

        def over_frames(lists, index):
            picked = [entry[index] for entry in lists]
            return picked[0] if len(picked) == 1 else jnp.concatenate(picked)

        normed1, att1, cross_in, cross_att, normed2, act2 = (
            over_frames(saves, i) for i in (1, 7, 9, 13, 16, 17)
        )
        kept3, d_lifted2, kept2, d_cross_query, kept1, d_query, d_key, d_value, d_tk, d_tv, space_mods = (
            over_frames(backs, i) for i in range(3, 14)
        )
        d_patch_up = weight_grad(normed2, d_lifted2)
        d_patch_down, d_gate5 = gated(weight_grad(act2, kept3), space_mod[5], patch_down)
        d_cross_proj = weight_grad(cross_att, kept2)
        d_cross_q = weight_grad(cross_in, d_cross_query)
        text_t = text.astype(F32).T
        d_cross_k = jnp.dot(text_t, jnp.sum(d_tk, axis=0)[:text_count], precision=HIGHEST)
        d_cross_v = jnp.dot(text_t, jnp.sum(d_tv, axis=0)[:text_count], precision=HIGHEST)
        d_cross = jnp.stack([d_cross_q, d_cross_k, d_cross_v, d_cross_proj])
        d_patch_proj, d_gate2 = gated(weight_grad(att1, kept1), space_mod[2], patch_attn[3])
        d_patch_attn = jnp.stack(
            [
                weight_grad(normed1[:, :space_rows], d_query),
                weight_grad(normed1, d_key),
                weight_grad(normed1, d_value),
                d_patch_proj,
            ]
        )
        space_mods = jnp.sum(space_mods, axis=0)
        first_mods = sum(first_mods[1:], first_mods[0])
        d_cross, d_patch_up, d_patch_down = summed([d_cross, d_patch_up, d_patch_down])
        (d_patch_attn,) = summed([d_patch_attn])

        space_six = jnp.stack([first_mods[0], first_mods[1], d_gate2, space_mods[0], space_mods[1], d_gate5])
        frame_six = jnp.stack([frame_mods[0], frame_mods[1], d_gate2_t, frame_mods[2], frame_mods[3], d_gate5_t])
        mine = jnp.stack([space_six, frame_six])
        spread = jnp.where(jnp.arange(clips)[:, None, None, None] == clip, mine[None], 0.0)
        by_clip = lax.psum(spread, whole_axes)
        d_table = jnp.sum(by_clip, axis=0)
        d_step = lax.dot_general(
            embeddings,
            jnp.sum(by_clip, axis=1).reshape(clips, -1),
            (((0,), (0,)), ((), ())),
            precision=HIGHEST,
        )
        return (
            output,
            latents_grad,
            d_step,
            d_table,
            d_patch_attn,
            d_cross,
            d_patch_up,
            d_patch_down,
            d_frame_attn,
            d_frame_up,
            d_frame_down,
        )

    return per_device


def solution(mesh):
    sizes = dict(mesh.shape)
    tokens = P("dev", "ta", "pa", None)
    in_specs = (tokens, P("dev", None, None), tokens, P("dev"), P("dev"), P("dev")) + (P(),) * 9
    out_specs = (tokens, tokens) + (P(),) * 9
    return jax.shard_map(
        make_per_device(sizes["ta"], sizes["pa"], sizes["dev"]),
        mesh=mesh,
        in_specs=in_specs,
        out_specs=out_specs,
        check_vma=False,
    )
```

time: 3040 us -> 901 us (0.30)
  waiting for transfers between devices: 1740 us -> 397 us
  matrix products: 540 us -> 67.9 us
  local copies, waits for them, and re-layouts: 421 us -> 60.7 us
  Pallas kernels: 0 us -> 230 us
  other arithmetic: 193 us -> 72.8 us
  blocking collectives: 113 us -> 8.84 us
  starting transfers between devices: 2.07 us -> 41.2 us
    all_gather x16 -> x0, waiting for transfers between devices: 759 us -> none  [the longest x2 126 us: clip_step(): lax.all_gather(space_keys, 'pa', axis=1, tiled=True)]
    dot_general x104 -> x18, matrix products: 540 us -> 67.9 us  [the longest x12 58.5 us: weight_grad(): lax.dot_general(left, right, ((axes, axes), ((), ())), preferred_element_...]
    unnamed x10 -> x2, waiting for transfers between devices: 308 us -> 0.03 us
    reduce_scatter x4 -> x0, waiting for transfers between devices: 291 us -> none  [the longest x2 272 us: clip_step(): lax.psum_scatter(d_whole_k.reshape(back_keys.shape), 'pa', scatter_dimens...]
    while x22 -> x0, waiting for transfers between devices: 272 us -> none
    pallas_call x0 -> x4, Pallas kernels: none -> 230 us  [call(): pl.pallas_call(kernel, grid=grid, in_specs=in_specs, out_specs=out_specs,...]
    psum x2, waiting for transfers between devices: 105 us -> 291 us  [the longest x1 176 us: summed(): total = lax.psum(flat, whole_axes).astype(F32)]
    reshape x38 -> x0, local copies, waits for them, and re-layouts: 149 us -> none  [the longest x8 59.5 us: split_heads(): values.reshape(values.shape[:-1] + (HEADS, values.shape[-1] // HEADS))]
  transfers between devices with their start and end apart: 27 -> 22, of which waited for: 26 -> 10; matrix products, arithmetic and copies ran while one was open for 15% -> 14% of each run, Pallas kernels for 0% -> 8%
where the time goes in v1:
time: 901 us; the launch traced here: 894 us
  waiting for transfers between devices  397 us (44%)
  Pallas kernels  230 us (26%)
  other arithmetic  72.8 us (8%)
  matrix products  67.9 us (8%)
  local copies, waits for them, and re-layouts  60.7 us (7%)
  starting transfers between devices  41.2 us (5%)
  between operations  15.7 us (2%)
    pallas_call x4, Pallas kernels, call(): pl.pallas_call(kernel, grid=grid, in_specs=in_specs, out_specs=out_specs,...  230 us
    psum x1, waiting for transfers between devices, summed(): total = lax.psum(flat, whole_axes).astype(F32)  176 us
    psum x1, waiting for transfers between devices, per_device(): by_clip = lax.psum(spread, whole_axes)  115 us
    dot_general x12, matrix products, weight_grad(): lax.dot_general(left, right, ((axes, axes), ((), ())), preferred_element_...  58.5 us
    ppermute x2, waiting for transfers between devices, to_space(): parts.append(lax.ppermute(sent, pair_axes, space_pairs(step)))  52.4 us
    concatenate x2, other arithmetic, summed(): flat = jnp.concatenate([a.reshape(-1).astype(BF) for a in arrays])  37.8 us
    ppermute x4, waiting for transfers between devices, per_device(): out_parts.append(lax.ppermute(sent, whole_axes, back(time_pairs(step))))  35.1 us
    slice x7, local copies, waits for them, and re-layouts, summed(): results.append(total[at:at + a.size].reshape(a.shape))  24.8 us
  transfers between devices with their start and end apart: 22, of which 10 were waited for; matrix products, arithmetic and copies ran while one was open for 14% of the time, Pallas kernels for 8%

profile of v1, /device:TPU:1, one launch (start us, length us, event | category | flops | bytes accessed | tf_op | source)
XLA Modules:
  0.0 893.8 jit_solution(11198785581521608494)
XLA Ops:
  7.3 3.0 dynamic-slice_bitcast_fusion.22
  10.3 5.6 collective-permute-start.6
  16.9 5.4 collective-permute-start.9
  23.9 2.8 collective-permute-start
  26.8 7.0 all_gather.7
  38.8 27.4 %collective-permute-done.1 = bf16[5,256,384]{2,1,0:T(8,128)(2,1)} collective-permute-done((bf16[5,256,384]{2,1,0:T(8,128)(2,1)}, bf16[5,256,384]{2,1,0:T(8,128)(2,1)}, u32[]{:S(2)}, u32[]{:S(2)}) %collective-permute-start.1) | collective-permute-done | bytes 983072 | tf_op jit(solution)/shard_map/ppermute | solution.py:585
  66.3 25.0 %collective-permute-done = bf16[5,256,384]{2,1,0:T(8,128)(2,1)} collective-permute-done((bf16[5,256,384]{2,1,0:T(8,128)(2,1)}, bf16[5,256,384]{2,1,0:T(8,128)(2,1)}, u32[]{:S(2)}, u32[]{:S(2)}) %collective-permute-start) | collective-permute-done | bytes 983072 | tf_op jit(solution)/shard_map/ppermute | solution.py:585
  91.2 2.3 fusion.29
  108.2 73.5 %shard_map.230 = (bf16[5,512,384]{2,1,0:T(8,128)(2,1)}, bf16[5,1024,384]{2,1,0:T(8,128)(2,1)}, bf16[5,512,384]{2,1,0:T(8,128)(2,1)}, bf16[5,384,1024]{2,1,0:T(8,...) custom-call(s32[4]{0:T(128)} %pad_add_fusion.1.refs_0_.counts_ref, ...), custom_call_target="tpu_custom_call" | custom-call | flops 32715571200 | bytes 93564944 | tf_op jit(solution)/shard_map/pallas_call | solution.py:462
  183.4 10.1 %collective-permute-start.5 = (bf16[5,128,384]{2,1,0:T(8,128)(2,1)S(1)}, bf16[5,128,384]{2,1,0:T(8,128)(2,1)S(1)}, u32[]{:S(2)}, u32[]{:S(2)}) collective-permute-start(bf16[5,128,384]{2,1,0:T(8,128)(2,1)S(1)} %get-tuple-element.166), channel_id=1, source_target_pairs={{0,24},{8,16},{16,8},{24,0},{1,25},{9,17},{17,9},{25,1},{2,26},{10... | collective-permute-start | bytes 1474568 | tf_op jit(solution)/shard_map/ppermute | solution.py:730
  197.5 7.8 collective-permute-done.5
  205.3 10.4 %collective-permute-done.4 = bf16[5,128,384]{2,1,0:T(8,128)(2,1)S(1)} collective-permute-done((bf16[5,128,384]{2,1,0:T(8,128)(2,1)S(1)}, bf16[5,128,384]{2,1,0:T(8,128)(2,1)S(1)}, u32[]{:S(2)}, u32[]{:S(2)}) %collective-permute-start.4) | collective-permute-done | bytes 491552 | tf_op jit(solution)/shard_map/ppermute | solution.py:730
  217.9 77.8 %shard_map.231 = (bf16[20,128,384]{2,1,0:T(8,128)(2,1)}, bf16[20,128,384]{2,1,0:T(8,128)(2,1)}, bf16[20,128,384]{2,1,0:T(8,128)(2,1)}, bf16[20,128,1152]{2,1,0:T...) custom-call(s32[4]{0:T(128)} %pad_add_fusion.1.refs_0_.counts_ref, ...), custom_call_target="tpu_custom_call" | custom-call | flops 27179089920 | bytes 43970576 | tf_op jit(solution)/shard_map/pallas_call | solution.py:462
  295.7 3.0 constant_dynamic-slice_fusion.4
  298.7 2.8 fusion.33
  304.4 6.0 fusion.2
  312.8 7.1 fusion.1
  321.3 10.0 %multiply_convert_fusion = (bf16[1536,384]{1,0:T(8,128)(2,1)}, f32[384]{0:T(512)}) fusion(f32[384]{0:T(512)S(1)} %get-tuple-element.117, bf16[1536,384]{1,0:T(8,128)(2,1)} %down_ref.1, bf16[20,128,1536]{2,1,0:T(8,128)(2,1)} %get-tuple-element.85, bf16[20,128,384]{2,1,0:T(8,128)(2,1)} %get-tuple-element.86), kind=kOutput, calls=%fused_computation.10 | convolution fusion | flops 3022847488 | bytes 12192768 | tf_op jit(solution)/shard_map/dot_general | solution.py:803
  331.3 2.3 convert_element_type.109
  333.6 18.8 %pad_maximum_fusion.1 = bf16[1769472]{0:T(1024)(128)(2,1)} fusion(bf16[589824]{0:T(1024)(128)(2,1)S(1)} %convert_element_type.109, bf16[589824]{0:T(1024)(128)(2,1)S(1)} %convert_element_type.107, bf16[589824]{0:T(1024)(128)(2,1)S(1)} %convert_element_type.105), kind=kLoop, calls=%fused_computation.1 | loop fusion | flops 10616832 | bytes 7077888 | tf_op jit(solution)/shard_map/concatenate | solution.py:815
  357.0 70.2 %shard_map.232 = (f32[5,512,384]{2,1,0:T(8,128)}, f32[5,512,384]{2,1,0:T(8,128)}, bf16[5,512,384]{2,1,0:T(8,128)(2,1)}, bf16[5,512,384]{2,1,0:T(8,128)(2,1)}, bf...) custom-call(s32[4]{0:T(128)} %pad_add_fusion.1.refs_0_.counts_ref, ...), custom_call_target="tpu_custom_call" | custom-call | flops 48821698560 | bytes 106799120 | tf_op jit(solution)/shard_map/pallas_call | solution.py:462
  427.3 7.1 fusion
  435.7 10.0 %multiply_convert_fusion.1 = (bf16[1536,384]{1,0:T(8,128)(2,1)}, f32[384]{0:T(512)}) fusion(f32[384]{0:T(512)S(1)} %copy-done.25, bf16[1536,384]{1,0:T(8,128)(2,1)} %refs_8_.1, bf16[5,512,1536]{2,1,0:T(8,128)(2,1)} %get-tuple-element.80, bf16[5,512,384]{2,1,0:T(8,128)(2,1)} %get-tuple-element.81), kind=kOutput, calls=%fused_computation.11 | convolution fusion | flops 3022847488 | bytes 12192768 | tf_op jit(solution)/shard_map/dot_general | solution.py:803
  445.7 2.4 convert_element_type.103
  452.0 3.5 fusion.22
  457.9 2.3 convert_element_type.99
  461.6 19.0 %pad_maximum_fusion = bf16[1769472]{0:T(1024)(128)(2,1)} fusion(bf16[589824]{0:T(1024)(128)(2,1)S(1)} %convert_element_type.103, bf16[589824]{0:T(1024)(128)(2,1)S(1)} %convert_element_type.101, bf16[589824]{0:T(1024)(128)(2,1)S(1)} %convert_element_type.99), kind=kLoop, calls=%fused_computation | loop fusion | flops 10616832 | bytes 7077888 | tf_op jit(solution)/shard_map/concatenate | solution.py:815
  482.3 2.9 fusion.19
  485.2 4.5 fusion.18
  489.7 2.2 fusion.17
  492.0 8.2 shard_map.233
  509.6 2.4 collective-permute-start.12
  517.1 4.3 collective-permute-done.10
  521.4 2.2 collective-permute-start.18
  523.6 12.3 %collective-permute-done.13 = bf16[5,128,384]{2,1,0:T(8,128)(2,1)} collective-permute-done((bf16[5,128,384]{2,1,0:T(8,128)(2,1)}, bf16[5,128,384]{2,1,0:T(8,128)(2,1)}, u32[]{:S(2)}, u32[]{:S(2)}) %collective-permute-start.13) | collective-permute-done | bytes 491552 | tf_op jit(solution)/shard_map/ppermute | solution.py:787
  535.8 9.4 %collective-permute-done.12 = bf16[5,128,384]{2,1,0:T(8,128)(2,1)} collective-permute-done((bf16[5,128,384]{2,1,0:T(8,128)(2,1)}, bf16[5,128,384]{2,1,0:T(8,128)(2,1)}, u32[]{:S(2)}, u32[]{:S(2)}) %collective-permute-start.12) | collective-permute-done | bytes 491552 | tf_op jit(solution)/shard_map/ppermute | solution.py:787
  545.2 9.2 %collective-permute-done.11 = bf16[5,128,384]{2,1,0:T(8,128)(2,1)} collective-permute-done((bf16[5,128,384]{2,1,0:T(8,128)(2,1)S(1)}, bf16[5,128,384]{2,1,0:T(8,128)(2,1)}, u32[]{:S(2)}, u32[]{:S(2)}) %collective-permute-start.11) | collective-permute-done | bytes 491552 | tf_op jit(solution)/shard_map/ppermute | solution.py:787
  558.2 115.3 %all-reduce.7.cloned.1.call-done = f32[4,2,6,384]{3,0,2,1:T(4,128)} async-done(((f32[4,2,6,384]{3,0,2,1:T(4,128)}), f32[4,2,6,384]{3,0,2,1:T(4,128)}) %all-reduce.7.cloned.1.call-update) | async-done | bytes 73744 | tf_op jit(solution)/shard_map/psum | solution.py:892
  675.0 3.5 fusion.44
  680.5 2.2 maximum_convert_fusion
  682.7 175.9 %all-reduce.9.cloned.1.call-done = (bf16[1769472]{0:T(1024)(128)(2,1)}, bf16[1769472]{0:T(1024)(128)(2,1)}, bf16[4,384,384]{2,1,0:T(8,128)(2,1)}) async-done(((bf16[1769472]{0:T(1024)(128)(2,1)}, bf16[1769472]{0:T(1024)(128)(2,1)}, bf16[4,384,384]{2,1,0:T(8,128)(2,1)}), (bf16[1769472]{0:T(1024)(128)(2,1)}, bf16[1769472]{0:T(1024)(128)(2,1)}, bf16[4,384,384]{2,1,0:T(8,128)(2,1)})) %all-reduce.9.cloned.1.call-update) | async-done | bytes 8257552 | tf_op jit(solution)/shard_map/psum | solution.py:816
  858.6 3.0 reshape.223
  861.6 6.5 fusion.60
  868.1 3.4 slice.201
  871.5 3.2 slice.199
  874.8 3.4 slice.197
  878.2 3.4 slice.189
  881.5 3.2 slice.191
  (187 shorter events, 75.1 us)
Async XLA Ops:
  7.2 666.3 %all-reduce.7.cloned.1.call-start = ((), (), s32[]{:S(2)}) async-start(), calls=%async_computation | async-start | bytes 147456 | tf_op jit(solution)/shard_map/psum | solution.py:892
  7.3 15.0 %copy-start.11 = (bf16[2,5,256,384]{3,2,1,0:T(8,128)(2,1)S(1)}, bf16[2,5,256,384]{3,2,1,0:T(8,128)(2,1)}, u32[]{:S(2)}) copy-start(bf16[2,5,256,384]{3,2,1,0:T(8,128)(2,1)} %param.15) | copy-start | bytes 5898244
  10.3 183.2 %collective-permute-start.6 = (bf16[5,128,384]{2,1,0:T(8,128)(2,1)}, bf16[5,128,384]{2,1,0:T(8,128)(2,1)}, u32[]{:S(2)}, u32[]{:S(2)}) collective-permute-start(bf16[5,128,384]{2,1,0:T(8,128)(2,1)} %get-tuple-element.157), channel_id=1, source_target_pairs={{0,0},{1,4},{2,16},{3,20},{4,1},{5,5},{6,17},{7,21},{8,8},{9,12},{... | collective-permute-start | bytes 1474568 | tf_op jit(solution)/shard_map/ppermute | solution.py:713
  15.9 177.6 %collective-permute-start.7 = (bf16[5,128,384]{2,1,0:T(8,128)(2,1)}, bf16[5,128,384]{2,1,0:T(8,128)(2,1)}, u32[]{:S(2)}, u32[]{:S(2)}) collective-permute-start(bf16[5,128,384]{2,1,0:T(8,128)(2,1)} %get-tuple-element.158), channel_id=1, source_target_pairs={{0,8},{1,12},{2,24},{3,28},{4,9},{5,13},{6,25},{7,29},{8,0},{9,4},... | collective-permute-start | bytes 1474568 | tf_op jit(solution)/shard_map/ppermute | solution.py:713
  16.9 176.9 %collective-permute-start.9 = (bf16[5,128,384]{2,1,0:T(8,128)(2,1)}, bf16[5,128,384]{2,1,0:T(8,128)(2,1)}, u32[]{:S(2)}, u32[]{:S(2)}) collective-permute-start(bf16[5,128,384]{2,1,0:T(8,128)(2,1)} %get-tuple-element.159), channel_id=1, source_target_pairs={{0,10},{1,14},{2,26},{3,30},{4,11},{5,15},{6,27},{7,31},{8,2},{9,6... | collective-permute-start | bytes 1474568 | tf_op jit(solution)/shard_map/ppermute | solution.py:713
  22.3 4.4 copy-start.29
  22.3 4.4 copy-start.30
  22.3 4.4 copy-start.31
  22.4 4.4 copy-start.16
  22.4 13.3 %copy-start.12 = (bf16[256,2304]{1,0:T(8,128)(2,1)S(1)}, bf16[256,2304]{1,0:T(8,128)(2,1)}, u32[]{:S(2)}) copy-start(bf16[256,2304]{1,0:T(8,128)(2,1)} %param.21) | copy-start | bytes 3538948
  23.9 42.4 %collective-permute-start.1 = (bf16[5,256,384]{2,1,0:T(8,128)(2,1)}, bf16[5,256,384]{2,1,0:T(8,128)(2,1)}, u32[]{:S(2)}, u32[]{:S(2)}) collective-permute-start(bf16[5,256,384]{2,1,0:T(8,128)(2,1)} %get-tuple-element.171), channel_id=1, source_target_pairs={{0,2},{1,6},{2,0},{3,4},{4,3},{5,7},{6,1},{7,5},{8,10},{9,14},{10,... | collective-permute-start | bytes 2949128 | tf_op jit(solution)/shard_map/ppermute | solution.py:585
  23.9 67.3 %collective-permute-start = (bf16[5,256,384]{2,1,0:T(8,128)(2,1)}, bf16[5,256,384]{2,1,0:T(8,128)(2,1)}, u32[]{:S(2)}, u32[]{:S(2)}) collective-permute-start(bf16[5,256,384]{2,1,0:T(8,128)(2,1)} %get-tuple-element.172), channel_id=1, source_target_pairs={{0,0},{1,4},{2,2},{3,6},{4,1},{5,5},{6,3},{7,7},{8,8},{9,12},{10,1... | collective-permute-start | bytes 2949128 | tf_op jit(solution)/shard_map/ppermute | solution.py:585
  36.5 57.4 %copy-start.8 = (bf16[120,384]{1,0:T(8,128)(2,1)}, bf16[120,384]{1,0:T(8,128)(2,1)S(1)}, u32[]{:S(2)}) copy-start(bf16[120,384]{1,0:T(8,128)(2,1)S(1)} %dynamic-slice_bitcast_fusion.27) | copy-start | bytes 276484
  36.6 57.0 %copy-start.19 = (f32[4,128]{1,0:T(4,128)}, f32[4,128]{1,0:T(4,128)S(1)}, u32[]{:S(2)}) copy-start(f32[4,128]{1,0:T(4,128)S(1)} %get-tuple-element.183) | copy-start | bytes 6148
  36.6 57.0 %copy-start.21 = (f32[4,128]{1,0:T(4,128)}, f32[4,128]{1,0:T(4,128)S(1)}, u32[]{:S(2)}) copy-start(f32[4,128]{1,0:T(4,128)S(1)} %get-tuple-element.184) | copy-start | bytes 6148
  37.8 58.9 %copy-start.14 = (bf16[128,384]{1,0:T(8,128)(2,1)}, bf16[128,384]{1,0:T(8,128)(2,1)S(1)}, u32[]{:S(2)}) copy-start(bf16[128,384]{1,0:T(8,128)(2,1)S(1)} %convolution_convert_fusion.2.refs_6_) | copy-start | bytes 294916
  66.3 127.6 %collective-permute-start.8 = (bf16[5,128,384]{2,1,0:T(8,128)(2,1)}, bf16[5,128,384]{2,1,0:T(8,128)(2,1)}, u32[]{:S(2)}, u32[]{:S(2)}) collective-permute-start(bf16[5,128,384]{2,1,0:T(8,128)(2,1)} %get-tuple-element.160), channel_id=1, source_target_pairs={{0,2},{1,6},{2,18},{3,22},{4,3},{5,7},{6,19},{7,23},{8,10},{9,14},... | collective-permute-start | bytes 1474568 | tf_op jit(solution)/shard_map/ppermute | solution.py:713
  93.8 4.7 copy-start.2
  93.8 3.7 slice-start
  93.8 14.4 %collective-permute-start.2 = (bf16[5,512,384]{2,1,0:T(8,128)(2,1)S(1)}, bf16[5,512,384]{2,1,0:T(8,128)(2,1)}, u32[]{:S(2)}, u32[]{:S(2)}) collective-permute-start(bf16[5,512,384]{2,1,0:T(8,128)(2,1)S(1)} %pad_maximum_fusion.2.refs_1_.refs_0_), channel_id=1, source_target_pairs={{0,1},{1,0},{2,3},{3,2},{4,5},{5,4},{6,7},{7,6},{8,9},{9,8},{10,11... | collective-permute-start | bytes 5898248 | tf_op jit(solution)/shard_map/ppermute | solution.py:591
  183.4 21.9 %collective-permute-start.5 = (bf16[5,128,384]{2,1,0:T(8,128)(2,1)S(1)}, bf16[5,128,384]{2,1,0:T(8,128)(2,1)S(1)}, u32[]{:S(2)}, u32[]{:S(2)}) collective-permute-start(bf16[5,128,384]{2,1,0:T(8,128)(2,1)S(1)} %get-tuple-element.166), channel_id=1, source_target_pairs={{0,24},{8,16},{16,8},{24,0},{1,25},{9,17},{17,9},{25,1},{2,26},{10... | collective-permute-start | bytes 1474568 | tf_op jit(solution)/shard_map/ppermute | solution.py:730
  193.5 22.3 %collective-permute-start.4 = (bf16[5,128,384]{2,1,0:T(8,128)(2,1)S(1)}, bf16[5,128,384]{2,1,0:T(8,128)(2,1)S(1)}, u32[]{:S(2)}, u32[]{:S(2)}) collective-permute-start(bf16[5,128,384]{2,1,0:T(8,128)(2,1)S(1)} %get-tuple-element.167), channel_id=1, source_target_pairs={{0,16},{8,24},{16,0},{24,8},{1,17},{9,25},{17,1},{25,9},{2,18},{10... | collective-permute-start | bytes 1474568 | tf_op jit(solution)/shard_map/ppermute | solution.py:730
  193.5 22.3 %collective-permute-start.3 = (bf16[5,128,384]{2,1,0:T(8,128)(2,1)S(1)}, bf16[5,128,384]{2,1,0:T(8,128)(2,1)S(1)}, u32[]{:S(2)}, u32[]{:S(2)}) collective-permute-start(bf16[5,128,384]{2,1,0:T(8,128)(2,1)S(1)} %get-tuple-element.168), channel_id=1, source_target_pairs={{0,8},{8,0},{16,24},{24,16},{1,9},{9,1},{17,25},{25,17},{2,10},{10... | collective-permute-start | bytes 1474568 | tf_op jit(solution)/shard_map/ppermute | solution.py:730
  301.7 51.6 %collective-permute-start.16 = (bf16[5,128,384]{2,1,0:T(8,128)(2,1)}, bf16[5,128,384]{2,1,0:T(8,128)(2,1)}, u32[]{:S(2)}, u32[]{:S(2)}) collective-permute-start(bf16[5,128,384]{2,1,0:T(8,128)(2,1)} %get-tuple-element.142), channel_id=1, source_target_pairs={{0,24},{8,16},{16,8},{24,0},{1,25},{9,17},{17,9},{25,1},{2,26},{10... | collective-permute-start | bytes 1474568 | tf_op jit(solution)/shard_map/ppermute | solution.py:730
  303.1 50.3 %collective-permute-start.15 = (bf16[5,128,384]{2,1,0:T(8,128)(2,1)}, bf16[5,128,384]{2,1,0:T(8,128)(2,1)}, u32[]{:S(2)}, u32[]{:S(2)}) collective-permute-start(bf16[5,128,384]{2,1,0:T(8,128)(2,1)} %get-tuple-element.143), channel_id=1, source_target_pairs={{0,16},{8,24},{16,0},{24,8},{1,17},{9,25},{17,1},{25,9},{2,18},{10... | collective-permute-start | bytes 1474568 | tf_op jit(solution)/shard_map/ppermute | solution.py:730
  304.2 49.1 %collective-permute-start.14 = (bf16[5,128,384]{2,1,0:T(8,128)(2,1)}, bf16[5,128,384]{2,1,0:T(8,128)(2,1)}, u32[]{:S(2)}, u32[]{:S(2)}) collective-permute-start(bf16[5,128,384]{2,1,0:T(8,128)(2,1)} %get-tuple-element.144), channel_id=1, source_target_pairs={{0,8},{8,0},{16,24},{24,16},{1,9},{9,1},{17,25},{25,17},{2,10},{10... | collective-permute-start | bytes 1474568 | tf_op jit(solution)/shard_map/ppermute | solution.py:730
  333.5 19.8 %copy-start.27 = (f32[384]{0:T(512)S(1)}, f32[384]{0:T(512)}, u32[]{:S(2)}) copy-start(f32[384]{0:T(512)} %get-tuple-element.130) | copy-start | bytes 4612
  445.7 3.1 copy-start.9
  452.0 3.5 copy-start.33
  452.0 3.5 copy-start.34
  460.2 20.4 %copy-start.4 = (bf16[5,512,384]{2,1,0:T(8,128)(2,1)S(1)}, bf16[5,512,384]{2,1,0:T(8,128)(2,1)}, u32[]{:S(2)}) copy-start(bf16[5,512,384]{2,1,0:T(8,128)(2,1)} %get-tuple-element.77) | copy-start | bytes 5898244
  460.2 20.4 %copy-start.5 = (bf16[5,512,384]{2,1,0:T(8,128)(2,1)S(1)}, bf16[5,512,384]{2,1,0:T(8,128)(2,1)}, u32[]{:S(2)}) copy-start(bf16[5,512,384]{2,1,0:T(8,128)(2,1)} %get-tuple-element.78) | copy-start | bytes 5898244
  460.2 20.4 %copy-start.7 = (bf16[4,384,384]{2,1,0:T(8,128)(2,1)S(1)}, bf16[4,384,384]{2,1,0:T(8,128)(2,1)}, u32[]{:S(2)}) copy-start(bf16[4,384,384]{2,1,0:T(8,128)(2,1)} %refs_3_.1) | copy-start | bytes 3538948
  460.3 20.4 %copy-start.24 = (f32[384]{0:T(512)S(1)}, f32[384]{0:T(512)}, u32[]{:S(2)}) copy-start(f32[384]{0:T(512)} %get-tuple-element.119) | copy-start | bytes 4612
  460.3 31.7 %collective-permute-start.17 = (bf16[5,512,384]{2,1,0:T(8,128)(2,1)}, bf16[5,512,384]{2,1,0:T(8,128)(2,1)}, u32[]{:S(2)}, u32[]{:S(2)}) collective-permute-start(bf16[5,512,384]{2,1,0:T(8,128)(2,1)} %get-tuple-element.74), channel_id=1, source_target_pairs={{1,0},{0,1},{3,2},{2,3},{5,4},{4,5},{7,6},{6,7},{9,8},{8,9},{11,10... | collective-permute-start | bytes 5898248 | tf_op jit(solution)/shard_map/ppermute | solution.py:836
  482.0 3.2 copy-start.18
  485.2 4.5 copy-start.3
  492.0 9.1 %slice-start.2 = ((f32[8,384]{1,0:T(8,128)}), f32[2,384]{1,0:T(2,128)S(1)}, s32[]{:S(2)}) async-start(f32[8,384]{1,0:T(8,128)} %copy-done.18), calls=%async_computation.4 | async-start | bytes 6144 | tf_op jit(solution)/shard_map/slice | solution.py:888
  492.0 9.2 %copy-start.28 = (pred[4]{0:T(512)(128)(4,1)S(1)}, pred[4]{0:T(512)(128)(4,1)}, u32[]{:S(2)}) copy-start(pred[4]{0:T(512)(128)(4,1)} %iota_compare_fusion) | copy-start | bytes 16
  501.9 356.8 %all-reduce.9.cloned.1.call-start = ((), (), s32[]{:S(2)}) async-start(), calls=%async_computation.1 | async-start | bytes 16515072 | tf_op jit(solution)/shard_map/psum | solution.py:816
  505.8 15.5 %collective-permute-start.10 = (bf16[5,128,384]{2,1,0:T(8,128)(2,1)}, bf16[5,128,384]{2,1,0:T(8,128)(2,1)}, u32[]{:S(2)}, u32[]{:S(2)}) collective-permute-start(bf16[5,128,384]{2,1,0:T(8,128)(2,1)} %get-tuple-element.149), channel_id=1, source_target_pairs={{0,0},{4,1},{16,2},{20,3},{1,4},{5,5},{17,6},{21,7},{8,8},{12,9},{... | collective-permute-start | bytes 1474568 | tf_op jit(solution)/shard_map/ppermute | solution.py:787
  507.7 28.1 %collective-permute-start.13 = (bf16[5,128,384]{2,1,0:T(8,128)(2,1)}, bf16[5,128,384]{2,1,0:T(8,128)(2,1)}, u32[]{:S(2)}, u32[]{:S(2)}) collective-permute-start(bf16[5,128,384]{2,1,0:T(8,128)(2,1)} %get-tuple-element.150), channel_id=1, source_target_pairs={{10,0},{14,1},{26,2},{30,3},{11,4},{15,5},{27,6},{31,7},{2,8},{6,9... | collective-permute-start | bytes 1474568 | tf_op jit(solution)/shard_map/ppermute | solution.py:787
  509.6 35.6 %collective-permute-start.12 = (bf16[5,128,384]{2,1,0:T(8,128)(2,1)}, bf16[5,128,384]{2,1,0:T(8,128)(2,1)}, u32[]{:S(2)}, u32[]{:S(2)}) collective-permute-start(bf16[5,128,384]{2,1,0:T(8,128)(2,1)} %get-tuple-element.151), channel_id=1, source_target_pairs={{2,0},{6,1},{18,2},{22,3},{3,4},{7,5},{19,6},{23,7},{10,8},{14,9},... | collective-permute-start | bytes 1474568 | tf_op jit(solution)/shard_map/ppermute | solution.py:787
  512.1 42.3 %collective-permute-start.11 = (bf16[5,128,384]{2,1,0:T(8,128)(2,1)S(1)}, bf16[5,128,384]{2,1,0:T(8,128)(2,1)}, u32[]{:S(2)}, u32[]{:S(2)}) collective-permute-start(bf16[5,128,384]{2,1,0:T(8,128)(2,1)S(1)} %get-tuple-element.152), channel_id=1, source_target_pairs={{8,0},{12,1},{24,2},{28,3},{9,4},{13,5},{25,6},{29,7},{0,8},{4,9},... | collective-permute-start | bytes 1474568 | tf_op jit(solution)/shard_map/ppermute | solution.py:787
  515.4 163.1 %collective-permute-start.19 = (bf16[5,256,384]{2,1,0:T(8,128)(2,1)S(1)}, bf16[5,256,384]{2,1,0:T(8,128)(2,1)S(1)}, u32[]{:S(2)}, u32[]{:S(2)}) collective-permute-start(bf16[5,256,384]{2,1,0:T(8,128)(2,1)S(1)} %get-tuple-element.135), channel_id=1, source_target_pairs={{2,0},{6,1},{0,2},{4,3},{3,4},{7,5},{1,6},{5,7},{10,8},{14,9},{8,1... | collective-permute-start | bytes 2949128 | tf_op jit(solution)/shard_map/ppermute | solution.py:844
  521.4 157.2 %collective-permute-start.18 = (bf16[5,256,384]{2,1,0:T(8,128)(2,1)S(1)}, bf16[5,256,384]{2,1,0:T(8,128)(2,1)}, u32[]{:S(2)}, u32[]{:S(2)}) collective-permute-start(bf16[5,256,384]{2,1,0:T(8,128)(2,1)S(1)} %get-tuple-element.136), channel_id=1, source_target_pairs={{0,0},{4,1},{2,2},{6,3},{1,4},{5,5},{3,6},{7,7},{8,8},{12,9},{10,1... | collective-permute-start | bytes 2949128 | tf_op jit(solution)/shard_map/ppermute | solution.py:844
  556.7 118.4 %copy-start.20 = (f32[4,128]{1,0:T(4,128)S(1)}, f32[4,128]{1,0:T(4,128)}, u32[]{:S(2)}) copy-start(f32[4,128]{1,0:T(4,128)} %copy-done.19) | copy-start | bytes 6148
  556.7 118.4 %copy-start.22 = (f32[4,128]{1,0:T(4,128)S(1)}, f32[4,128]{1,0:T(4,128)}, u32[]{:S(2)}) copy-start(f32[4,128]{1,0:T(4,128)} %copy-done.21) | copy-start | bytes 6148
  (13 other events, 28.8 us)
Sparse Core Ops, SparseCore 0:
  502.0 171.4 all-reduce.6
  680.2 178.3 all-reduce.8

commit v2 on v1

--- a/solution.py
+++ b/solution.py
@@ -18,8 +18,11 @@
 BF = jnp.bfloat16
 VMEM_BYTES = 60 * 2**20
 SUM_ROWS = 16
-FRAME_GROUPS = ((0, 1, 2, 3, 4),)
 BLOCK = 16
+SUB = 8
+TILE = 16
+PARTS = (7, 5, 4, 3, 2, 1)
+PATTERN = (0, 1, 2, 0, 1, 0, 1)
 
 
 def dot(a, b):
@@ -170,6 +173,8 @@
     normed2_ref,
     act_ref,
     slope_ref,
+    branch2_ref,
+    branch5_ref,
 ):
     scale_by = HDIM ** (-0.5)
     frame = counts_ref[2] + first_frame + pl.program_id(0)
@@ -198,7 +203,9 @@
     att_t_ref[0] = att_t.astype(BF)
     att = att_t.T.astype(BF)
     att_ref[0] = att
-    state = own + (keep * mod[2:3]) * dot(att, attn_ref[3])
+    branch = dot(att, attn_ref[3])
+    branch2_ref[0] = branch.astype(BF)
+    state = own + (keep * mod[2:3]) * branch
     cross_in = state.astype(BF)
     cross_in_ref[0] = cross_in
     cross_queries = (dot(cross_in, cross_ref[0]).astype(BF) * scale_by).astype(BF)
@@ -223,7 +230,9 @@
     act = act.astype(BF)
     act_ref[0] = act
     slope_ref[0] = slope.astype(BF)
-    state = state + (keep * mod[5:6]) * dot(act, down_ref[...])
+    branch = dot(act, down_ref[...])
+    branch5_ref[0] = branch.astype(BF)
+    state = state + (keep * mod[5:6]) * branch
     state_ref[0] = state.astype(BF)
 
 
@@ -250,6 +259,8 @@
     cross_inverse_ref,
     middle_ref,
     slope_ref,
+    branch2_ref,
+    branch5_ref,
     state_grad_ref,
     own_grad_ref,
     other_grad_ref,
@@ -272,16 +283,16 @@
     grad = fold(grad_ref).astype(F32)
     rows = grad.shape[0]
     kept = keep * grad
-    kept3_ref[0] = kept.astype(BF)
-    d_act = dot_nt((kept * mod[5:6]).astype(BF), down_ref[...])
+    d_gate5 = row_sums(kept * branch5_ref[0].astype(F32))
+    d_branch = (kept * mod[5:6]).astype(BF)
+    kept3_ref[0] = d_branch
+    d_act = dot_nt(d_branch, down_ref[...])
     d_lifted = (d_act * slope_ref[0].astype(F32)).astype(BF)
     d_lifted_ref[0] = d_lifted
     d_normed = dot_nt(d_lifted, up_ref[...])
     hat, inverse = norm_parts(middle_ref[0])
     grad = grad + norm_back(d_normed, hat, inverse, mod[4:5])
-    mods_ref[0] = jnp.concatenate(
-        [row_sums(d_normed), row_sums(d_normed * hat), jnp.zeros((6, hat.shape[1]), F32)], axis=0
-    )
+    d_shift, d_scale = row_sums(d_normed), row_sums(d_normed * hat)
     kept = (keep * grad).astype(BF)
     kept2_ref[0] = kept
     d_att_t = dot_nt(cross_ref[1], kept)
@@ -302,8 +313,14 @@
     grad = grad + dot_nt(d_query, cross_ref[0])
     state_grad_ref[0] = grad
     kept = keep * grad
-    kept1_ref[0] = kept.astype(BF)
-    d_att_t = dot_nt(attn_ref[3], (kept * mod[2:3]).astype(BF))
+    d_gate2 = row_sums(kept * branch2_ref[0].astype(F32))
+    mods_ref[0] = jnp.concatenate(
+        [jnp.zeros((2, hat.shape[1]), F32), d_gate2, d_shift, d_scale, d_gate5, jnp.zeros((2, hat.shape[1]), F32)],
+        axis=0,
+    )
+    d_branch = (kept * mod[2:3]).astype(BF)
+    kept1_ref[0] = d_branch
+    d_att_t = dot_nt(attn_ref[3], d_branch)
     n_keys = value_ref.shape[1]
     d_query_t, d_keys, d_values = attend_back(
         lambda head, at: exponent_ref[0, head, at, :],
@@ -353,91 +370,337 @@
     normed_ref,
     d_qkv_ref,
     att_ref,
-    kept4_ref,
+    branch4_ref,
     normed2_ref,
     act_ref,
     d_lifted_ref,
-    kept5_ref,
+    branch5_ref,
     mods_ref,
     exponent_ref,
 ):
     scale_by = HDIM ** (-0.5)
-    block = state_ref.shape
+    frames, block, width = state_ref.shape
+    run_rows = frames * SUB
+    runs = block // SUB
     mod = mod_ref[...]
 
-    def put(ref, value):
-        ref[...] = value.reshape(ref.shape)
-
-    state = fold(state_ref).astype(F32)
+    def load(ref):
+        cube = ref[...].astype(F32)
+        parts = [cube[:, r * SUB : (r + 1) * SUB].reshape(run_rows, width) for r in range(runs)]
+        return jnp.concatenate(parts, axis=0)
+
+    def store(ref, value):
+        parts = [value[r * run_rows : (r + 1) * run_rows].reshape(frames, SUB, width) for r in range(runs)]
+        ref[...] = jnp.concatenate(parts, axis=1).astype(ref.dtype)
+
+    def run_of(value, r):
+        return value[r * run_rows : (r + 1) * run_rows]
+
+    state = load(state_ref)
     rows = state.shape[0]
-    frame = lax.broadcasted_iota(jnp.int32, (rows, 1), 0) // block[1]
+    frame = (lax.broadcasted_iota(jnp.int32, (rows, 1), 0) // SUB) % frames
     keep = (frame < counts_ref[0]).astype(F32)
     hat1, inverse1 = norm_parts(state)
     normed = (hat1 * (1.0 + mod[1:2]) + mod[0:1]).astype(BF)
-    put(normed_ref, normed)
+    normed_ref[0] = normed
     queries = (dot(normed, attn_ref[0]).astype(BF) * scale_by).astype(BF)
     keys = dot(normed, attn_ref[1]).astype(BF)
     values = dot(normed, attn_ref[2]).astype(BF)
-    keys_t = dot_nt(turned_ref[0], normed).astype(BF)
-    values_t = dot_nt(turned_ref[1], normed).astype(BF)
-
-    def keep_exponent(head, exponent):
-        exponent_ref[head] = exponent
-
-    att_t, inverses = attend(queries, keys, values_t, bias_ref[...], keep_exponent)
-    att = att_t.T.astype(BF)
-    put(att_ref, att)
-    state = state + (keep * mod[2:3]) * dot(att, attn_ref[3])
+    att_parts, att_t_parts, inverse_parts, keys_t_parts = [], [], [], []
+    for r in range(runs):
+        normed_run = run_of(normed, r)
+        keys_t_parts.append(dot_nt(turned_ref[0], normed_run).astype(BF))
+        values_t = dot_nt(turned_ref[1], normed_run).astype(BF)
+
+        def keep_exponent(head, exponent):
+            exponent_ref[r, head] = exponent
+
+        att_t, inverses = attend(
+            run_of(queries, r), run_of(keys, r), values_t, bias_ref[...], keep_exponent
+        )
+        att_t_parts.append(att_t)
+        inverse_parts.append(inverses)
+        att_parts.append(att_t.T.astype(BF))
+    att = jnp.concatenate(att_parts, axis=0)
+    att_ref[0] = att
+    branch2 = dot(att, attn_ref[3])
+    state = state + (keep * mod[2:3]) * branch2
     hat2, inverse2 = norm_parts(state)
     normed2 = (hat2 * (1.0 + mod[4:5]) + mod[3:4]).astype(BF)
-    put(normed2_ref, normed2)
+    normed2_ref[0] = normed2
     act, slope = gelu_parts(dot(normed2, up_ref[...]))
     act = act.astype(BF)
-    put(act_ref, act)
-    put(out_ref, (state + (keep * mod[5:6]) * dot(act, down_ref[...])).astype(BF))
-    grad = fold(cot_ref).astype(F32)
+    act_ref[0] = act
+    branch5 = dot(act, down_ref[...])
+    store(out_ref, state + (keep * mod[5:6]) * branch5)
+    grad = load(cot_ref)
     kept = keep * grad
-    put(kept5_ref, kept.astype(BF))
-    d_act = dot_nt((kept * mod[5:6]).astype(BF), down_ref[...])
+    d_gate5 = row_sums(kept * branch5)
+    d_branch = (kept * mod[5:6]).astype(BF)
+    branch5_ref[0] = d_branch
+    d_act = dot_nt(d_branch, down_ref[...])
     d_lifted = (d_act * slope).astype(BF)
-    put(d_lifted_ref, d_lifted)
+    d_lifted_ref[0] = d_lifted
     d_normed2 = dot_nt(d_lifted, up_ref[...])
     grad = grad + norm_back(d_normed2, hat2, inverse2, mod[4:5])
     kept = keep * grad
-    put(kept4_ref, kept.astype(BF))
-    d_att_t = dot_nt(attn_ref[3], (kept * mod[2:3]).astype(BF))
-    d_query_t, d_keys, d_values = attend_back(
-        lambda head, at: exponent_ref[head, at, :],
-        lambda pair: pair_of(queries, pair),
-        lambda head, at: head_rows(keys_t, head)[:, at],
-        lambda pair, at: pair_of(values, pair)[at],
-        d_att_t,
-        att_t,
-        lambda head: inverses[head],
-        (rows, rows),
-    )
-    d_qkv = jnp.concatenate(
-        [(d_query_t.T * scale_by).astype(BF), d_keys.astype(BF), d_values.astype(BF)], axis=1
-    )
-    put(d_qkv_ref, d_qkv)
-    width = hat1.shape[1]
-    d_normed1 = (
-        dot_nt(d_qkv[:, :width], attn_ref[0])
-        + dot_nt(d_qkv[:, width : 2 * width], attn_ref[1])
-        + dot_nt(d_qkv[:, 2 * width :], attn_ref[2])
-    )
+    d_gate2 = row_sums(kept * branch2)
+    d_branch = (kept * mod[2:3]).astype(BF)
+    branch4_ref[0] = d_branch
+    d_query_parts, d_key_parts, d_value_parts = [], [], []
+    for r in range(runs):
+        d_att_t = dot_nt(attn_ref[3], run_of(d_branch, r))
+        query_run, value_run = run_of(queries, r), run_of(values, r)
+        d_query_t, d_keys, d_values = attend_back(
+            lambda head, at: exponent_ref[r, head, at, :],
+            lambda pair: pair_of(query_run, pair),
+            lambda head, at: head_rows(keys_t_parts[r], head)[:, at],
+            lambda pair, at: pair_of(value_run, pair)[at],
+            d_att_t,
+            att_t_parts[r],
+            lambda head: inverse_parts[r][head],
+            (run_rows, run_rows),
+        )
+        d_query_parts.append((d_query_t.T * scale_by).astype(BF))
+        d_key_parts.append(d_keys.astype(BF))
+        d_value_parts.append(d_values.astype(BF))
+    d_qkv = [jnp.concatenate(parts, axis=0) for parts in (d_query_parts, d_key_parts, d_value_parts)]
+    d_normed1 = None
+    for i in range(3):
+        d_qkv_ref[0, :, i * width : (i + 1) * width] = d_qkv[i]
+        part = dot_nt(d_qkv[i], attn_ref[i])
+        d_normed1 = part if d_normed1 is None else d_normed1 + part
     grad = grad + norm_back(d_normed1, hat1, inverse1, mod[1:2])
-    put(grad_ref, grad.astype(BF))
+    store(grad_ref, grad)
     mods_ref[0] = jnp.concatenate(
         [
             row_sums(d_normed1),
             row_sums(d_normed1 * hat1),
+            d_gate2,
             row_sums(d_normed2),
             row_sums(d_normed2 * hat2),
-            jnp.zeros((4, width), F32),
+            d_gate5,
+            jnp.zeros((2, width), F32),
         ],
         axis=0,
     )
+
+
+class Reducer:
+    def __init__(self, shapes, small_rows, sizes):
+        self.width = width = shapes[0][1]
+        self.shapes = shapes
+        bits = {name: [(name, 1 << i) for i in range(sizes[name].bit_length() - 1)] for name in ("ta", "pa")}
+        kinds = [bits["ta"] + bits["pa"], bits["ta"][::-1] + bits["pa"], bits["pa"] + bits["ta"]]
+        self.ways = [("dev", 1)] + kinds[0]
+        self.loads, row = [], 0
+        for i, shape in enumerate(shapes):
+            for column in range(shape[1] // width):
+                self.loads.append((i, row, column * width, shape[0]))
+                row += shape[0]
+        self.total = row
+        self.parts = next(n for n in PARTS if row % (2 * n * TILE) == 0)
+        self.part_rows = row // 2 // self.parts
+        self.half_rows = row // 2
+        self.orders = [[("dev", 1)] + kinds[PATTERN[p % len(PATTERN)]] for p in range(self.parts)]
+        self.steps = len(self.ways)
+        self.small_rows = small_rows
+        self.counts, self.halves, self.boxes, at = [self.part_rows], [True], [], 0
+        for _ in range(1, self.steps):
+            halve = (self.counts[-1] // 2) % TILE == 0
+            self.halves.append(halve)
+            self.counts.append(self.counts[-1] // 2 if halve else self.counts[-1])
+        for p in range(self.parts):
+            self.boxes.append([])
+            for count in self.counts:
+                self.boxes[p].append(at)
+                at += count
+        self.box_rows = at
+        self.phases = 2 * self.steps + 1
+
+    def scratch(self):
+        shapes = [
+            pltpu.VMEM((self.total, self.width), BF),
+            pltpu.VMEM((self.total, self.width), BF),
+            pltpu.VMEM((self.box_rows, self.width), BF),
+            pltpu.SemaphoreType.DMA((len(self.loads),)),
+            pltpu.SemaphoreType.DMA((self.parts, 2)),
+            pltpu.SemaphoreType.DMA((self.parts, 2 * self.steps)),
+            pltpu.SemaphoreType.DMA((self.parts, 2 * self.steps)),
+        ]
+        if self.small_rows:
+            shapes += [
+                pltpu.VMEM((self.steps, self.small_rows, self.width), F32),
+                pltpu.SemaphoreType.DMA((self.steps,)),
+                pltpu.SemaphoreType.DMA((self.steps,)),
+            ]
+        return shapes
+
+    def bind(self, sources, out, scratch, small_in=None, small_out=None):
+        self.sources, self.out = sources, out
+        self.work, self.whole, self.inbox, self.in_sem, self.out_sem, self.send_sem, self.recv_sem = scratch[:7]
+        self.small_in, self.small_out = small_in, small_out
+        if self.small_rows:
+            self.small_box, self.small_send, self.small_recv = scratch[7:]
+
+    def bit(self, way):
+        return (lax.axis_index(way[0]) // way[1]) % 2
+
+    def peer(self, way):
+        return {way[0]: lax.axis_index(way[0]) + way[1] - 2 * way[1] * self.bit(way)}
+
+    def greet(self):
+        barrier = pltpu.get_barrier_semaphore()
+        for way in self.ways:
+            pl.semaphore_signal(barrier, inc=1, device_id=self.peer(way), device_id_type=pl.DeviceIdType.MESH)
+        return len(self.ways)
+
+    def base(self, p, step):
+        row = self.bit(self.orders[p][0]) * self.half_rows + p * self.part_rows
+        for s in range(1, step + 1):
+            if self.halves[s]:
+                row = row + self.bit(self.orders[p][s]) * self.counts[s]
+        return row
+
+    def rows(self, ref, row, count):
+        return ref.at[pl.ds(pl.multiple_of(row, TILE), count)]
+
+    def load(self, i):
+        source, row, column, rows = self.loads[i]
+        view = self.sources[source].at[:, column : column + self.width]
+        return pltpu.make_async_copy(view, self.work.at[row : row + rows], self.in_sem.at[i])
+
+    def remote(self, src, dst, p, step, way):
+        return pltpu.make_async_remote_copy(
+            src_ref=src,
+            dst_ref=dst,
+            send_sem=self.send_sem.at[p, step],
+            recv_sem=self.recv_sem.at[p, step],
+            device_id=self.peer(way),
+            device_id_type=pl.DeviceIdType.MESH,
+        )
+
+    def down(self, p, step):
+        way, count = self.orders[p][step], self.counts[step]
+        if step == 0:
+            row = (1 - self.bit(way)) * self.half_rows + p * self.part_rows
+        else:
+            row = self.base(p, step - 1)
+            if self.halves[step]:
+                row = row + (1 - self.bit(way)) * count
+        box = self.boxes[p][step]
+        return self.remote(self.rows(self.work, row, count), self.inbox.at[box : box + count], p, step, way)
+
+    def end_down(self, p, step):
+        self.down(p, step).wait()
+        count, base, box = self.counts[step], self.base(p, step), self.boxes[p][step]
+        chunk = next(c for c in (96, 64, 48, 32, TILE) if count % c == 0)
+
+        def body(i, carry):
+            at = pl.ds(pl.multiple_of(base + i * chunk, TILE), chunk)
+            got = self.inbox[pl.ds(pl.multiple_of(box + i * chunk, TILE), chunk), :]
+            total = (self.work[at, :].astype(F32) + got.astype(F32)).astype(BF)
+            if step == self.steps - 1:
+                self.whole[at, :] = total
+            else:
+                self.work[at, :] = total
+            return carry
+
+        lax.fori_loop(0, count // chunk, body, 0)
+
+    def up(self, p, turn):
+        step = self.steps - 1 - turn
+        if not self.halves[step]:
+            return None
+        rows = self.rows(self.whole, self.base(p, step), self.counts[step])
+        return self.remote(rows, rows, p, self.steps + turn, self.orders[p][step])
+
+    def store(self, p, side):
+        rows = pl.ds(side * self.half_rows + p * self.part_rows, self.part_rows)
+        return pltpu.make_async_copy(self.whole.at[rows], self.out.at[rows], self.out_sem.at[p, side])
+
+    def small(self, step):
+        return pltpu.make_async_remote_copy(
+            src_ref=self.small_out,
+            dst_ref=self.small_box.at[step],
+            send_sem=self.small_send.at[step],
+            recv_sem=self.small_recv.at[step],
+            device_id=self.peer(self.ways[step]),
+            device_id_type=pl.DeviceIdType.MESH,
+        )
+
+    def prepare(self):
+        for i in range(len(self.loads)):
+            self.load(i).start()
+        if self.small_rows:
+            self.small_out[...] = self.small_in[...]
+
+    def phase(self, k):
+        n = self.steps
+        if k == 0:
+            for i in range(len(self.loads)):
+                self.load(i).wait()
+        for p in range(self.parts):
+            if 1 <= k <= n:
+                self.end_down(p, k - 1)
+            elif k > n:
+                before = self.up(p, k - n - 1)
+                if before is not None:
+                    before.wait()
+            if k < n:
+                self.down(p, k).start()
+            elif k < 2 * n:
+                after = self.up(p, k - n)
+                if after is not None:
+                    after.start()
+            else:
+                self.store(p, 0).start()
+                self.store(p, 1).start()
+        if k == 2 * n:
+            for p in range(self.parts):
+                self.store(p, 0).wait()
+                self.store(p, 1).wait()
+        if self.small_rows and k <= n:
+            if k > 0:
+                self.small(k - 1).wait()
+                self.small_out[...] = self.small_out[...] + self.small_box[k - 1]
+            if k < n:
+                self.small(k).start()
+
+    def unpack(self, reduced):
+        results, at = [], 0
+        for rows, columns in self.shapes:
+            turns = columns // self.width
+            blocks = [reduced[at + i * rows : at + (i + 1) * rows] for i in range(turns)]
+            at += turns * rows
+            results.append((blocks[0] if turns == 1 else jnp.concatenate(blocks, axis=1)).astype(F32))
+        return results
+
+
+def reduce_all(arrays, small, sizes):
+    reducer = Reducer([a.shape for a in arrays], small.shape[0], sizes)
+    n = len(arrays)
+
+    def kernel(*refs):
+        reducer.bind(refs[:n], refs[n + 1], refs[n + 3 :], refs[n], refs[n + 2])
+        reducer.prepare()
+        pl.semaphore_wait(pltpu.get_barrier_semaphore(), reducer.greet())
+        for k in range(reducer.phases):
+            reducer.phase(k)
+
+    any_spec, vmem_spec = pl.BlockSpec(memory_space=pl.ANY), pl.BlockSpec(memory_space=pltpu.VMEM)
+    reduced, small_sum = pl.pallas_call(
+        kernel,
+        in_specs=[any_spec] * n + [vmem_spec],
+        out_specs=[any_spec, vmem_spec],
+        out_shape=[shape_of((reducer.total, reducer.width), BF), shape_of(small.shape, F32)],
+        scratch_shapes=reducer.scratch(),
+        compiler_params=pltpu.CompilerParams(collective_id=0, has_side_effects=True, vmem_limit_bytes=VMEM_BYTES),
+        cost_estimate=pl.CostEstimate(
+            flops=8 * reducer.total * reducer.width, bytes_accessed=4 * reducer.total * reducer.width, transcendentals=0
+        ),
+    )(*arrays, small)
+    return reducer.unpack(reduced), small_sum
 
 
 def whole(array):
@@ -471,7 +734,9 @@
     )(*inputs)
 
 
-def make_per_device(n_ta, n_pa, n_dev):
+def make_per_device(sizes):
+    n_ta, n_pa, n_dev = sizes["ta"], sizes["pa"], sizes["dev"]
+
     def per_device(
         latents,
         context,
@@ -622,6 +887,8 @@
                 out(space_rows, width),
                 out(space_rows, hidden),
                 out(space_rows, hidden),
+                out(space_rows, width),
+                out(space_rows, width),
             )
             dense = 2 * count * space_rows * width * (6 * width + 2 * hidden) + 8 * count * key_rows * width * width
             return call(
@@ -641,11 +908,11 @@
                 return shape_of((count,) + shape, dtype)
 
             (_, _, query, keys_t, value, exponent, att_t, _, inverse, _, cross_query, cross_exponent, cross_att_t, _,
-             cross_inverse, middle, _, _, slope) = saved
+             cross_inverse, middle, _, _, slope, branch2, branch5) = saved
             inputs = (
                 counts, grad, space_mod, patch_attn, cross_ends, text_keys.T, text_values, patch_up, patch_down,
                 query, keys_t, value, exponent, att_t, inverse, cross_query, cross_exponent, cross_att_t,
-                cross_inverse, middle, slope,
+                cross_inverse, middle, slope, branch2, branch5,
             )
             hidden = patch_up.shape[1]
             outputs = (
@@ -693,13 +960,16 @@
                 count * space_rows * width * 30,
             )
 
-        owns, saves, states = [], [], []
-        for frame_ids in FRAME_GROUPS:
-            own, other = to_space(frame_ids)
-            saved = space_forward(frame_ids, own, other)
-            owns.append(own)
-            saves.append(saved)
-            states.append(saved[0])
+        near_frames = min(2, frames)
+        frame_groups = [tuple(range(near_frames)), tuple(range(near_frames, frames))]
+        frame_groups = [ids for ids in frame_groups if ids]
+        arrived = [to_space(ids) for ids in frame_groups]
+        owns = [own for own, _ in arrived]
+        cotangent, owns[-1] = lax.optimization_barrier((cotangent, owns[-1]))
+        saves = [
+            space_forward(ids, own, other) for ids, own, (_, other) in zip(frame_groups, owns, arrived)
+        ]
+        states = [saved[0] for saved in saves]
 
         n_steps = halves * clips_dev
         cot_parts = []
@@ -740,19 +1010,20 @@
         state = jnp.concatenate(state_groups, axis=1).reshape(all_frames, time_patches, width)
 
         block_rows = all_frames * BLOCK
-        ids = jnp.arange(block_rows, dtype=jnp.int32)
-        same = (ids[:, None] % BLOCK == ids[None, :] % BLOCK) & (ids[:, None] // BLOCK < counts[0])
+        run_rows = all_frames * SUB
+        ids = jnp.arange(run_rows, dtype=jnp.int32)
+        same = (ids[:, None] % SUB == ids[None, :] % SUB) & (ids[:, None] // SUB < counts[0])
         bias = jnp.where(same, 0.0, MASKED_SCORE).astype(F32)
         hidden = frame_up.shape[1]
         n_blocks = time_patches // BLOCK
 
         def tokens(features):
-            return shape_of((all_frames, time_patches, features), BF)
+            return shape_of((n_blocks, block_rows, features), BF)
 
         time_inputs = (counts, state, cot, frame_mod, bias, frame_attn, frame_turned, frame_up, frame_down)
         time_outputs = (
-            tokens(width),
-            tokens(width),
+            shape_of((all_frames, time_patches, width), BF),
+            shape_of((all_frames, time_patches, width), BF),
             tokens(width),
             tokens(3 * width),
             tokens(width),
@@ -767,17 +1038,20 @@
         def blocked(array):
             return pl.BlockSpec((all_frames, BLOCK, array.shape[2]), lambda at: (0, at, 0))
 
-        (out_t, grad_t, normed_t, d_qkv_t, att_tt, kept4, normed4, act4, d_lifted4, kept5, frame_mods) = call(
+        (out_t, grad_t, normed_t, d_qkv_t, att_tt, branch4, normed4, act4, d_lifted4, branch5, frame_six) = call(
             time_kernel,
             (n_blocks,),
             time_inputs,
             [SCALARS, blocked(state), blocked(cot)] + [whole(a) for a in time_inputs[3:]],
             time_outputs,
-            [blocked(a) for a in time_outputs[:-1]] + [framed(time_outputs[-1])],
+            [blocked(a) for a in time_outputs[:2]] + [framed(a) for a in time_outputs[2:]],
             all_frames * time_patches * width * (24 * width + 12 * hidden),
-            [pltpu.VMEM((HEADS, block_rows, block_rows), BF)],
+            [pltpu.VMEM((BLOCK // SUB, HEADS, run_rows, run_rows), BF)],
         )
 
+        grad_s = exchange(grad_t.reshape(n_ta, frames, time_patches, width))
+
+        out_t, grad_s = lax.optimization_barrier((out_t, grad_s))
         out_pieces = out_t.reshape(n_ta, frames, time_patches, width)
         out_parts = []
         for step in range(n_steps):
@@ -795,38 +1069,20 @@
             rows.append(jnp.concatenate(runs, axis=1))
         output = jnp.stack(rows)
 
-        grad_s = exchange(grad_t.reshape(n_ta, frames, time_patches, width))
-
         def weight_grad(left, right):
-            n = left.ndim - 1
-            axes = tuple(range(n))
-            return lax.dot_general(left, right, ((axes, axes), ((), ())), preferred_element_type=F32)
-
-        def gated(product, gate, weight):
-            return product * gate, jnp.sum(weight.astype(F32) * product, axis=0)
-
-        d_frame_qkv = weight_grad(normed_t, d_qkv_t).reshape(width, 3, width).swapaxes(0, 1)
-        d_frame_proj, d_gate2_t = gated(weight_grad(att_tt, kept4), frame_mod[2], frame_attn[3])
+            left, right = left.reshape(-1, left.shape[-1]), right.reshape(-1, right.shape[-1])
+            return lax.dot_general(left, right, (((0,), (0,)), ((), ())), preferred_element_type=F32).astype(BF)
+
+        d_frame_qkv = weight_grad(normed_t, d_qkv_t)
+        d_frame_proj = weight_grad(att_tt, branch4)
         d_frame_up = weight_grad(normed4, d_lifted4)
-        d_frame_down, d_gate5_t = gated(weight_grad(act4, kept5), frame_mod[5], frame_down)
-        frame_mods = jnp.sum(frame_mods, axis=0)
-
-        def summed(arrays):
-            flat = jnp.concatenate([a.reshape(-1).astype(BF) for a in arrays])
-            total = lax.psum(flat, whole_axes).astype(F32)
-            results, at = [], 0
-            for a in arrays:
-                results.append(total[at : at + a.size].reshape(a.shape))
-                at += a.size
-            return results
-
-        d_frame_attn = jnp.concatenate([d_frame_qkv, d_frame_proj[None]])
-        d_frame_attn, d_frame_up, d_frame_down = summed([d_frame_attn, d_frame_up, d_frame_down])
-
-        pieces = []
-        finished, first_mods, backs = [], [], []
-        for frame_ids, own, saved in zip(FRAME_GROUPS, owns, saves):
+        d_frame_down = weight_grad(act4, branch5)
+
+        pieces, backs, finish_six = [], [], []
+        for i, (frame_ids, own, saved) in enumerate(zip(frame_groups, owns, saves)):
             grad = grad_s[:, frame_ids[0] : frame_ids[-1] + 1]
+            if i == 1:
+                grad, output = lax.optimization_barrier((grad, output))
             backed = space_backward(frame_ids, grad, saved)
             backs.append(backed)
             other_grad = backed[2]
@@ -835,8 +1091,7 @@
                 sent = other_grad[:, (step - 1) * space_rows : step * space_rows]
                 parts.append(lax.ppermute(sent, pair_axes, back(group_pairs(step))))
             done, mods = space_finish(own, backed[0], backed[1], parts)
-            finished.append(done)
-            first_mods.append(jnp.sum(mods, axis=0))
+            finish_six.append(mods)
             got = []
             for step in range(clips_dev):
                 b = (clip - step) % clips_dev
@@ -857,39 +1112,43 @@
             picked = [entry[index] for entry in lists]
             return picked[0] if len(picked) == 1 else jnp.concatenate(picked)
 
-        normed1, att1, cross_in, cross_att, normed2, act2 = (
-            over_frames(saves, i) for i in (1, 7, 9, 13, 16, 17)
-        )
-        kept3, d_lifted2, kept2, d_cross_query, kept1, d_query, d_key, d_value, d_tk, d_tv, space_mods = (
-            over_frames(backs, i) for i in range(3, 14)
-        )
-        d_patch_up = weight_grad(normed2, d_lifted2)
-        d_patch_down, d_gate5 = gated(weight_grad(act2, kept3), space_mod[5], patch_down)
-        d_cross_proj = weight_grad(cross_att, kept2)
-        d_cross_q = weight_grad(cross_in, d_cross_query)
+        def grad_over(lists, index, others, other_index):
+            total = None
+            for one, two in zip(lists, others):
+                left, right = one[index], two[other_index]
+                left, right = left.reshape(-1, left.shape[-1]), right.reshape(-1, right.shape[-1])
+                part = lax.dot_general(left, right, (((0,), (0,)), ((), ())), preferred_element_type=F32)
+                total = part if total is None else total + part
+            return total.astype(BF)
+
+        d_patch_up = grad_over(saves, 16, backs, 4)
+        d_patch_down = grad_over(saves, 17, backs, 3)
+        d_cross_proj = grad_over(saves, 13, backs, 5)
+        d_cross_q = grad_over(saves, 9, backs, 6)
         text_t = text.astype(F32).T
-        d_cross_k = jnp.dot(text_t, jnp.sum(d_tk, axis=0)[:text_count], precision=HIGHEST)
-        d_cross_v = jnp.dot(text_t, jnp.sum(d_tv, axis=0)[:text_count], precision=HIGHEST)
-        d_cross = jnp.stack([d_cross_q, d_cross_k, d_cross_v, d_cross_proj])
-        d_patch_proj, d_gate2 = gated(weight_grad(att1, kept1), space_mod[2], patch_attn[3])
-        d_patch_attn = jnp.stack(
-            [
-                weight_grad(normed1[:, :space_rows], d_query),
-                weight_grad(normed1, d_key),
-                weight_grad(normed1, d_value),
-                d_patch_proj,
-            ]
-        )
-        space_mods = jnp.sum(space_mods, axis=0)
-        first_mods = sum(first_mods[1:], first_mods[0])
-        d_cross, d_patch_up, d_patch_down = summed([d_cross, d_patch_up, d_patch_down])
-        (d_patch_attn,) = summed([d_patch_attn])
-
-        space_six = jnp.stack([first_mods[0], first_mods[1], d_gate2, space_mods[0], space_mods[1], d_gate5])
-        frame_six = jnp.stack([frame_mods[0], frame_mods[1], d_gate2_t, frame_mods[2], frame_mods[3], d_gate5_t])
-        mine = jnp.stack([space_six, frame_six])
+        d_tk, d_tv = (over_frames(backs, i) for i in (11, 12))
+        d_cross_k = jnp.dot(text_t, jnp.sum(d_tk, axis=0)[:text_count], precision=HIGHEST).astype(BF)
+        d_cross_v = jnp.dot(text_t, jnp.sum(d_tv, axis=0)[:text_count], precision=HIGHEST).astype(BF)
+        d_patch_proj = grad_over(saves, 7, backs, 7)
+        near_saves = [(saved[1][:, :space_rows],) for saved in saves]
+        d_patch_q = grad_over(near_saves, 0, backs, 8)
+        d_patch_k = grad_over(saves, 1, backs, 9)
+        d_patch_v = grad_over(saves, 1, backs, 10)
+        six = jnp.sum(over_frames(backs, 13), axis=0) + jnp.sum(jnp.concatenate(finish_six), axis=0)
+        mine = jnp.stack([six, jnp.sum(frame_six, axis=0)])
         spread = jnp.where(jnp.arange(clips)[:, None, None, None] == clip, mine[None], 0.0)
-        by_clip = lax.psum(spread, whole_axes)
+        arrays = [
+            d_patch_q, d_patch_k, d_patch_v, d_patch_proj, d_cross_q, d_cross_k, d_cross_v, d_cross_proj,
+            d_patch_up, d_patch_down, d_frame_qkv, d_frame_proj, d_frame_up, d_frame_down,
+        ]
+        results, by_clip = reduce_all(arrays, spread.reshape(-1, width), sizes)
+        by_clip = by_clip.reshape(clips, 2, 8, width)[:, :, :6]
+        d_patch_attn = jnp.stack(results[0:4])
+        d_cross = jnp.stack(results[4:8])
+        d_patch_up, d_patch_down = results[8:10]
+        d_frame_qkv = results[10].reshape(width, 3, width).swapaxes(0, 1)
+        d_frame_attn = jnp.concatenate([d_frame_qkv, results[11][None]])
+        d_frame_up, d_frame_down = results[12:14]
         d_table = jnp.sum(by_clip, axis=0)
         d_step = lax.dot_general(
             embeddings,
@@ -920,7 +1179,7 @@
     in_specs = (tokens, P("dev", None, None), tokens, P("dev"), P("dev"), P("dev")) + (P(),) * 9
     out_specs = (tokens, tokens) + (P(),) * 9
     return jax.shard_map(
-        make_per_device(sizes["ta"], sizes["pa"], sizes["dev"]),
+        make_per_device(sizes),
         mesh=mesh,
         in_specs=in_specs,
         out_specs=out_specs,

time: 901 us -> 637 us (0.71)
  waiting for transfers between devices: 397 us -> 72 us
  Pallas kernels: 230 us -> 357 us
  other arithmetic: 72.8 us -> 42.9 us
  local copies, waits for them, and re-layouts: 60.7 us -> 33.8 us
  starting transfers between devices: 41.2 us -> 56.3 us
  between operations: 15.7 us -> 2.41 us
    psum x2 -> x0, waiting for transfers between devices: 291 us -> none  [the longest x1 176 us: summed(): total = lax.psum(flat, whole_axes).astype(F32)]
    pallas_call x0 -> x1, Pallas kernels: none -> 106 us  [reduce_all(): pl.pallas_call(kernel, in_specs=[any_spec] * n + [vmem_spec], out_specs=[...]
    ppermute x2 -> x4, waiting for transfers between devices: 52.4 us -> 13.5 us  [to_space(): parts.append(lax.ppermute(sent, pair_axes, space_pairs(step)))]
    ppermute x4, waiting for transfers between devices: 0.01 us -> 36.1 us  [per_device(): cot_parts.append(lax.ppermute(sent, whole_axes, time_pairs(step)))]
    ppermute x4, waiting for transfers between devices: 35.1 us -> 0.01 us  [per_device(): out_parts.append(lax.ppermute(sent, whole_axes, back(time_pairs(step))))]
    concatenate x3 -> x2, other arithmetic: 38 us -> 3.03 us  [the longest x1 1.56 us: per_device(): d_frame_attn = jnp.concatenate([d_frame_qkv, results[11][None]])]
    pallas_call x4 -> x7, Pallas kernels: 230 us -> 251 us  [call(): pl.pallas_call(kernel, grid=grid, in_specs=in_specs, out_specs=out_specs,...]
    ppermute x2 -> x4, waiting for transfers between devices: 0.01 us -> 19.1 us  [per_device(): got.append(lax.ppermute(sent, pair_axes, back(space_pairs(step))))]
  transfers between devices with their start and end apart: 22 -> 29, of which waited for: 10 -> 10; matrix products, arithmetic and copies ran while one was open for 14% -> 18% of each run, Pallas kernels for 8% -> 26%
where the time goes in v2:
time: 637 us; the launch traced here: 631 us
  Pallas kernels  357 us (56%)
  waiting for transfers between devices  72 us (11%)
  matrix products  60.6 us (10%)
  starting transfers between devices  56.3 us (9%)
  other arithmetic  42.9 us (7%)
  local copies, waits for them, and re-layouts  33.8 us (5%)
    pallas_call x7, Pallas kernels, call(): pl.pallas_call(kernel, grid=grid, in_specs=in_specs, out_specs=out_specs,...  251 us
    pallas_call x1, Pallas kernels, reduce_all(): pl.pallas_call(kernel, in_specs=[any_spec] * n + [vmem_spec], out_specs=[...  106 us
    ppermute x4, waiting for transfers between devices, per_device(): cot_parts.append(lax.ppermute(sent, whole_axes, time_pairs(step)))  36.1 us
    dot_general x16, matrix products, grad_over(): lax.dot_general(left, right, (((0,), (0,)), ((), ())), preferred_element_...  31 us
    dot_general x4, matrix products, weight_grad(): lax.dot_general(left, right, (((0,), (0,)), ((), ())), preferred_element_...  20.9 us
    ppermute x4, waiting for transfers between devices, per_device(): got.append(lax.ppermute(sent, pair_axes, back(space_pairs(step))))  19.1 us
    ppermute x4, starting transfers between devices, per_device(): out_parts.append(lax.ppermute(sent, whole_axes, back(time_pairs(step))))  14.6 us
    ppermute x4, waiting for transfers between devices, to_space(): parts.append(lax.ppermute(sent, pair_axes, space_pairs(step)))  13.5 us
  transfers between devices with their start and end apart: 29, of which 10 were waited for; matrix products, arithmetic and copies ran while one was open for 18% of the time, Pallas kernels for 26%

profile of v2, /device:TPU:1, one launch (start us, length us, event | category | flops | bytes accessed | tf_op | source)
XLA Modules:
  0.0 631.0 jit_solution(3327110034213732524)
XLA Ops:
  2.7 4.7 collective-permute-start.1
  7.5 2.1 collective-permute-start
  12.3 2.9 collective-permute-start.6
  15.4 3.7 all-gather
  19.3 2.1 all_gather.7
  36.8 13.5 %collective-permute-done.6 = bf16[3,256,384]{2,1,0:T(8,128)(2,1)} collective-permute-done((bf16[3,256,384]{2,1,0:T(8,128)(2,1)}, bf16[3,256,384]{2,1,0:T(8,128)(2,1)}, u32[]{:S(2)}, u32[]{:S(2)}) %collective-permute-start.6) | collective-permute-done | bytes 589856 | tf_op jit(solution)/shard_map/ppermute | solution.py:850
  52.7 1.9 collective-permute-start.12
  54.6 5.5 collective-permute-start.15
  65.4 19.4 %collective-permute-done.12 = bf16[5,128,384]{2,1,0:T(8,128)(2,1)S(1)} collective-permute-done((bf16[5,128,384]{2,1,0:T(8,128)(2,1)S(1)}, bf16[5,128,384]{2,1,0:T(8,128)(2,1)S(1)}, u32[]{:S(2)}, u32[]{:S(2)}) %collective-permute-start.12) | collective-permute-done | bytes 491552 | tf_op jit(solution)/shard_map/ppermute | solution.py:983
  84.8 5.8 collective-permute-done.15
  90.6 4.7 collective-permute-done.14
  95.4 6.2 collective-permute-done.13
  103.0 35.9 %shard_map.230 = (bf16[2,512,384]{2,1,0:T(8,128)(2,1)}, bf16[2,1024,384]{2,1,0:T(8,128)(2,1)}, bf16[2,512,384]{2,1,0:T(8,128)(2,1)}, bf16[2,384,1024]{2,1,0:T(8,...) custom-call(s32[4]{0:T(128)} %pad_add_fusion.1.refs_0_.counts_ref, ...), custom_call_target="tpu_custom_call" | custom-call | flops 13086228480 | bytes 41955344 | tf_op jit(solution)/shard_map/pallas_call | solution.py:725
  138.9 2.1 dynamic-slice_bitcast_fusion.34
  143.6 49.2 %shard_map.231 = (bf16[3,512,384]{2,1,0:T(8,128)(2,1)}, bf16[3,1024,384]{2,1,0:T(8,128)(2,1)}, bf16[3,512,384]{2,1,0:T(8,128)(2,1)}, bf16[3,384,1024]{2,1,0:T(8,...) custom-call(s32[4]{0:T(128)} %pad_add_fusion.1.refs_0_.counts_ref, ...), custom_call_target="tpu_custom_call" | custom-call | flops 19629342720 | bytes 60469264 | tf_op jit(solution)/shard_map/pallas_call | solution.py:725
  200.8 2.2 collective-permute-done.10
  204.9 77.6 %shard_map.232 = (bf16[20,128,384]{2,1,0:T(8,128)(2,1)}, bf16[20,128,384]{2,1,0:T(8,128)(2,1)}, bf16[8,320,384]{2,1,0:T(8,128)(2,1)}, bf16[8,320,1152]{2,1,0:T(8...) custom-call(s32[4]{0:T(128)} %pad_add_fusion.1.refs_0_.counts_ref, ...), custom_call_target="tpu_custom_call" | custom-call | flops 27179089920 | bytes 43663376 | tf_op jit(solution)/shard_map/pallas_call | solution.py:725
  287.2 7.7 %fusion.4.refs_12_ = bf16[384,1536]{1,0:T(8,128)(2,1)} fusion(bf16[8,320,384]{2,1,0:T(8,128)(2,1)S(1)} %copy-done.42, bf16[8,320,1536]{2,1,0:T(8,128)(2,1)} %get-tuple-element.187), kind=kOutput, calls=%fused_computation.11 | convolution fusion | flops 3020488704 | bytes 11010048 | tf_op jit(solution)/shard_map/dot_general | solution.py:1074
  294.9 5.4 fusion.5.refs_13_
  300.3 3.7 fusion.6.refs_10_
  304.1 4.1 fusion.19.refs_11_
  311.3 5.2 collective-permute-start.19
  317.5 4.7 collective-permute-start.21
  322.1 3.7 collective-permute-start.20
  326.8 33.2 %shard_map.233 = (f32[2,512,384]{2,1,0:T(8,128)}, f32[2,512,384]{2,1,0:T(8,128)}, bf16[2,512,384]{2,1,0:T(8,128)(2,1)}, bf16[2,512,384]{2,1,0:T(8,128)(2,1)}, bf...) custom-call(s32[4]{0:T(128)} %pad_add_fusion.1.refs_0_.counts_ref, ...), custom_call_target="tpu_custom_call" | custom-call | flops 19528679424 | bytes 46895120 | tf_op jit(solution)/shard_map/pallas_call | solution.py:725
  368.9 45.1 %shard_map.235 = (f32[3,512,384]{2,1,0:T(8,128)}, f32[3,512,384]{2,1,0:T(8,128)}, bf16[3,512,384]{2,1,0:T(8,128)(2,1)}, bf16[3,512,384]{2,1,0:T(8,128)(2,1)}, bf...) custom-call(s32[4]{0:T(128)} %pad_add_fusion.1.refs_0_.counts_ref, ...), custom_call_target="tpu_custom_call" | custom-call | flops 29293019136 | bytes 68173840 | tf_op jit(solution)/shard_map/pallas_call | solution.py:725
  415.8 2.2 convolution_bitcast_fusion.16
  422.1 4.7 convolution_bitcast_fusion.3
  430.9 2.0 convolution_bitcast_fusion.5
  433.0 2.9 fusion.2.refs_9_
  439.9 2.5 fusion.3.refs_8_
  446.1 3.1 fusion.13.refs_2_
  449.2 3.9 shard_map.234
  453.1 2.0 dynamic-slice_bitcast_fusion.23
  455.0 6.5 %collective-permute-start.25 = (bf16[2,256,384]{2,1,0:T(8,128)(2,1)}, bf16[2,256,384]{2,1,0:T(8,128)(2,1)S(1)}, u32[]{:S(2)}, u32[]{:S(2)}) collective-permute-start(bf16[2,256,384]{2,1,0:T(8,128)(2,1)} %get-tuple-element.275), channel_id=1, source_target_pairs={{2,0},{6,1},{0,2},{4,3},{3,4},{7,5},{1,6},{5,7},{10,8},{14,9},{8,1... | collective-permute-start | bytes 1179656 | tf_op jit(solution)/shard_map/ppermute | solution.py:1099
  461.5 1.9 collective-permute-start.24
  464.7 3.1 fusion.14.refs_1_
  467.8 3.0 collective-permute-done.25
  470.8 8.5 %collective-permute-done.24 = bf16[2,256,384]{2,1,0:T(8,128)(2,1)} collective-permute-done((bf16[2,256,384]{2,1,0:T(8,128)(2,1)S(1)}, bf16[2,256,384]{2,1,0:T(8,128)(2,1)}, u32[]{:S(2)}, u32[]{:S(2)}) %collective-permute-start.24) | collective-permute-done | bytes 393248 | tf_op jit(solution)/shard_map/ppermute | solution.py:1099
  480.7 6.0 shard_map.236
  488.2 106.4 %shard_map.237 = (bf16[10752,384]{1,0:T(8,128)(2,1)}, f32[64,384]{1,0:T(8,128)}) custom-call(bf16[384,384]{1,0:T(8,128)(2,1)} %fusion.18.refs_0_, bf16[384,384]{1,0:T(8,128)(2,1)} %fusion.14.refs_1_, bf16[384,384]{1,0:T(8,128)(2,1)} %fusion.13.refs_2_, bf16[384,384]{1,0:T(8,128)(2,1)} %fusion.17.refs_3_, bf16[384,384]{1,0:T(8,128)(2,1)} %fusion.16.refs_4_, ...), custom_call_target="tpu_custom_call" | custom-call | flops 33030144 | bytes 16515072 | tf_op jit(solution)/shard_map/pallas_call | solution.py:692
  595.6 3.3 fusion.55
  600.5 2.0 collective-permute-start.28
  602.5 1.9 collective-permute-start.27
  604.4 3.5 fusion.44
  616.2 4.1 slice_convert_fusion
  620.3 7.6 %collective-permute-done.27 = bf16[3,256,384]{2,1,0:T(8,128)(2,1)S(1)} collective-permute-done((bf16[3,256,384]{2,1,0:T(8,128)(2,1)S(1)}, bf16[3,256,384]{2,1,0:T(8,128)(2,1)S(1)}, u32[]{:S(2)}, u32[]{:S(2)}) %collective-permute-start.27) | collective-permute-done | bytes 589856 | tf_op jit(solution)/shard_map/ppermute | solution.py:1099
  628.4 2.2 maximum_convert_fusion
  (259 shorter events, 93.0 us)
Async XLA Ops:
  1.8 7.7 %slice-start.1 = ((bf16[2,5,256,384]{3,2,1,0:T(8,128)(2,1)}), bf16[2,3,256,384]{3,2,1,0:T(8,128)(2,1)S(1)}, s32[]{:S(2)}) async-start(bf16[2,5,256,384]{3,2,1,0:T(8,128)(2,1)} %param.15), calls=%async_computation.1 | async-start | bytes 2359296 | tf_op jit(solution)/shard_map/slice | solution.py:846
  2.7 32.6 %collective-permute-start.1 = (bf16[2,256,384]{2,1,0:T(8,128)(2,1)}, bf16[2,256,384]{2,1,0:T(8,128)(2,1)}, u32[]{:S(2)}, u32[]{:S(2)}) collective-permute-start(bf16[2,256,384]{2,1,0:T(8,128)(2,1)} %get-tuple-element.287), channel_id=1, source_target_pairs={{0,2},{1,6},{2,0},{3,4},{4,3},{5,7},{6,1},{7,5},{8,10},{9,14},{10,... | collective-permute-start | bytes 1179656 | tf_op jit(solution)/shard_map/ppermute | solution.py:850
  7.4 7.8 %copy-start.32 = (s32[2]{0:T(128)S(1)}, s32[2]{0:T(128)}, u32[]{:S(2)}) copy-start(s32[2]{0:T(128)} %param.20) | copy-start | bytes 28
  7.4 7.8 %copy-start.33 = (s32[2]{0:T(128)S(1)}, s32[2]{0:T(128)}, u32[]{:S(2)}) copy-start(s32[2]{0:T(128)} %param.19) | copy-start | bytes 28
  7.5 7.8 %copy-start.34 = (s32[2]{0:T(128)S(1)}, s32[2]{0:T(128)}, u32[]{:S(2)}) copy-start(s32[2]{0:T(128)} %param.18) | copy-start | bytes 28
  7.5 11.8 %copy-start.19 = (bf16[2,120,384]{2,1,0:T(8,128)(2,1)S(1)}, bf16[2,120,384]{2,1,0:T(8,128)(2,1)}, u32[]{:S(2)}) copy-start(bf16[2,120,384]{2,1,0:T(8,128)(2,1)} %param.16) | copy-start | bytes 552964
  7.5 27.9 %collective-permute-start = (bf16[2,256,384]{2,1,0:T(8,128)(2,1)}, bf16[2,256,384]{2,1,0:T(8,128)(2,1)}, u32[]{:S(2)}, u32[]{:S(2)}) collective-permute-start(bf16[2,256,384]{2,1,0:T(8,128)(2,1)} %get-tuple-element.288), channel_id=1, source_target_pairs={{0,0},{1,4},{2,2},{3,6},{4,1},{5,5},{6,3},{7,7},{8,8},{9,12},{10,1... | collective-permute-start | bytes 1179656 | tf_op jit(solution)/shard_map/ppermute | solution.py:850
  9.5 11.9 %copy-start.13 = (bf16[4,384,384]{2,1,0:T(8,128)(2,1)S(1)}, bf16[4,384,384]{2,1,0:T(8,128)(2,1)}, u32[]{:S(2)}) copy-start(bf16[4,384,384]{2,1,0:T(8,128)(2,1)} %param.24) | copy-start | bytes 3538948
  9.5 14.2 %copy-start.30 = (bf16[2,6,384]{2,0,1:T(2,128)(2,1)S(1)}, bf16[2,6,384]{2,0,1:T(2,128)(2,1)}, u32[]{:S(2)}) copy-start(bf16[2,6,384]{2,0,1:T(2,128)(2,1)} %param.22) | copy-start | bytes 27652
  9.6 14.8 %copy-start.11 = (bf16[256,2304]{1,0:T(8,128)(2,1)S(1)}, bf16[256,2304]{1,0:T(8,128)(2,1)}, u32[]{:S(2)}) copy-start(bf16[256,2304]{1,0:T(8,128)(2,1)} %param.21) | copy-start | bytes 3538948
  10.7 26.1 %collective-permute-start.7 = (bf16[3,256,384]{2,1,0:T(8,128)(2,1)}, bf16[3,256,384]{2,1,0:T(8,128)(2,1)}, u32[]{:S(2)}, u32[]{:S(2)}) collective-permute-start(bf16[3,256,384]{2,1,0:T(8,128)(2,1)} %get-tuple-element.271), channel_id=1, source_target_pairs={{0,2},{1,6},{2,0},{3,4},{4,3},{5,7},{6,1},{7,5},{8,10},{9,14},{10,... | collective-permute-start | bytes 1769480 | tf_op jit(solution)/shard_map/ppermute | solution.py:850
  12.3 38.0 %collective-permute-start.6 = (bf16[3,256,384]{2,1,0:T(8,128)(2,1)}, bf16[3,256,384]{2,1,0:T(8,128)(2,1)}, u32[]{:S(2)}, u32[]{:S(2)}) collective-permute-start(bf16[3,256,384]{2,1,0:T(8,128)(2,1)} %get-tuple-element.272), channel_id=1, source_target_pairs={{0,0},{1,4},{2,2},{3,6},{4,1},{5,5},{6,3},{7,7},{8,8},{9,12},{10,1... | collective-permute-start | bytes 1769480 | tf_op jit(solution)/shard_map/ppermute | solution.py:850
  25.0 6.9 %slice-start.4 = ((bf16[4,384,384]{2,1,0:T(8,128)(2,1)}), bf16[2,384,384]{2,1,0:T(8,128)(2,1)S(1)}, s32[]{:S(2)}) async-start(bf16[4,384,384]{2,1,0:T(8,128)(2,1)} %attn_ref.1), calls=%async_computation.4 | async-start | bytes 1179648 | tf_op jit(solution)/shard_map/slice | solution.py:843
  52.4 32.4 %copy-start.2 = (bf16[3,512,384]{2,1,0:T(8,128)(2,1)}, bf16[3,512,384]{2,1,0:T(8,128)(2,1)S(1)}, u32[]{:S(2)}) copy-start(bf16[3,512,384]{2,1,0:T(8,128)(2,1)S(1)} %pad_maximum_fusion.6.refs_1_.refs_0_) | copy-start | bytes 3538948
  52.7 32.2 %collective-permute-start.12 = (bf16[5,128,384]{2,1,0:T(8,128)(2,1)S(1)}, bf16[5,128,384]{2,1,0:T(8,128)(2,1)S(1)}, u32[]{:S(2)}, u32[]{:S(2)}) collective-permute-start(bf16[5,128,384]{2,1,0:T(8,128)(2,1)S(1)} %get-tuple-element.251), channel_id=1, source_target_pairs={{0,0},{1,4},{2,16},{3,20},{4,1},{5,5},{6,17},{7,21},{8,8},{9,12},{... | collective-permute-start | bytes 1474568 | tf_op jit(solution)/shard_map/ppermute | solution.py:983
  54.6 36.0 %collective-permute-start.15 = (bf16[5,128,384]{2,1,0:T(8,128)(2,1)S(1)}, bf16[5,128,384]{2,1,0:T(8,128)(2,1)S(1)}, u32[]{:S(2)}, u32[]{:S(2)}) collective-permute-start(bf16[5,128,384]{2,1,0:T(8,128)(2,1)S(1)} %get-tuple-element.252), channel_id=1, source_target_pairs={{0,10},{1,14},{2,26},{3,30},{4,11},{5,15},{6,27},{7,31},{8,2},{9,6... | collective-permute-start | bytes 1474568 | tf_op jit(solution)/shard_map/ppermute | solution.py:983
  60.1 35.3 %collective-permute-start.14 = (bf16[5,128,384]{2,1,0:T(8,128)(2,1)S(1)}, bf16[5,128,384]{2,1,0:T(8,128)(2,1)S(1)}, u32[]{:S(2)}, u32[]{:S(2)}) collective-permute-start(bf16[5,128,384]{2,1,0:T(8,128)(2,1)S(1)} %get-tuple-element.253), channel_id=1, source_target_pairs={{0,2},{1,6},{2,18},{3,22},{4,3},{5,7},{6,19},{7,23},{8,10},{9,14},... | collective-permute-start | bytes 1474568 | tf_op jit(solution)/shard_map/ppermute | solution.py:983
  61.7 39.8 %collective-permute-start.13 = (bf16[5,128,384]{2,1,0:T(8,128)(2,1)S(1)}, bf16[5,128,384]{2,1,0:T(8,128)(2,1)S(1)}, u32[]{:S(2)}, u32[]{:S(2)}) collective-permute-start(bf16[5,128,384]{2,1,0:T(8,128)(2,1)S(1)} %get-tuple-element.254), channel_id=1, source_target_pairs={{0,8},{1,12},{2,24},{3,28},{4,9},{5,13},{6,25},{7,29},{8,0},{9,4},... | collective-permute-start | bytes 1474568 | tf_op jit(solution)/shard_map/ppermute | solution.py:983
  61.8 40.1 %copy-start.6 = (bf16[2,512,384]{2,1,0:T(8,128)(2,1)}, bf16[2,512,384]{2,1,0:T(8,128)(2,1)S(1)}, u32[]{:S(2)}) copy-start(bf16[2,512,384]{2,1,0:T(8,128)(2,1)S(1)} %pad_maximum_fusion.8.refs_1_.refs_0_) | copy-start | bytes 2359300
  61.8 40.3 %collective-permute-start.2 = (bf16[2,512,384]{2,1,0:T(8,128)(2,1)S(1)}, bf16[2,512,384]{2,1,0:T(8,128)(2,1)S(1)}, u32[]{:S(2)}, u32[]{:S(2)}) collective-permute-start(bf16[2,512,384]{2,1,0:T(8,128)(2,1)S(1)} %pad_maximum_fusion.8.refs_1_.refs_0_), channel_id=1, source_target_pairs={{0,1},{1,0},{2,3},{3,2},{4,5},{5,4},{6,7},{7,6},{8,9},{9,8},{10,11... | collective-permute-start | bytes 2359304 | tf_op jit(solution)/shard_map/ppermute | solution.py:856
  84.8 58.8 %collective-permute-start.8 = (bf16[3,512,384]{2,1,0:T(8,128)(2,1)S(1)}, bf16[3,512,384]{2,1,0:T(8,128)(2,1)}, u32[]{:S(2)}, u32[]{:S(2)}) collective-permute-start(bf16[3,512,384]{2,1,0:T(8,128)(2,1)S(1)} %pad_maximum_fusion.6.refs_1_.refs_0_), channel_id=1, source_target_pairs={{0,1},{1,0},{2,3},{3,2},{4,5},{5,4},{6,7},{7,6},{8,9},{9,8},{10,11... | collective-permute-start | bytes 3538952 | tf_op jit(solution)/shard_map/ppermute | solution.py:856
  141.0 54.8 %collective-permute-start.5 = (bf16[2,128,384]{2,1,0:T(8,128)(2,1)}, bf16[2,128,384]{2,1,0:T(8,128)(2,1)}, u32[]{:S(2)}, u32[]{:S(2)}) collective-permute-start(bf16[2,128,384]{2,1,0:T(8,128)(2,1)} %get-tuple-element.282), channel_id=1, source_target_pairs={{0,24},{8,16},{16,8},{24,0},{1,25},{9,17},{17,9},{25,1},{2,26},{10... | collective-permute-start | bytes 589832 | tf_op jit(solution)/shard_map/ppermute | solution.py:1000
  141.0 57.5 %collective-permute-start.4 = (bf16[2,128,384]{2,1,0:T(8,128)(2,1)}, bf16[2,128,384]{2,1,0:T(8,128)(2,1)}, u32[]{:S(2)}, u32[]{:S(2)}) collective-permute-start(bf16[2,128,384]{2,1,0:T(8,128)(2,1)} %get-tuple-element.283), channel_id=1, source_target_pairs={{0,16},{8,24},{16,0},{24,8},{1,17},{9,25},{17,1},{25,9},{2,18},{10... | collective-permute-start | bytes 589832 | tf_op jit(solution)/shard_map/ppermute | solution.py:1000
  142.4 56.1 %collective-permute-start.3 = (bf16[2,128,384]{2,1,0:T(8,128)(2,1)}, bf16[2,128,384]{2,1,0:T(8,128)(2,1)}, u32[]{:S(2)}, u32[]{:S(2)}) collective-permute-start(bf16[2,128,384]{2,1,0:T(8,128)(2,1)} %get-tuple-element.284), channel_id=1, source_target_pairs={{0,8},{8,0},{16,24},{24,16},{1,9},{9,1},{17,25},{25,17},{2,10},{10... | collective-permute-start | bytes 589832 | tf_op jit(solution)/shard_map/ppermute | solution.py:1000
  194.2 6.6 %collective-permute-start.11 = (bf16[3,128,384]{2,1,0:T(8,128)(2,1)S(1)}, bf16[3,128,384]{2,1,0:T(8,128)(2,1)S(1)}, u32[]{:S(2)}, u32[]{:S(2)}) collective-permute-start(bf16[3,128,384]{2,1,0:T(8,128)(2,1)S(1)} %get-tuple-element.264), channel_id=1, source_target_pairs={{0,24},{8,16},{16,8},{24,0},{1,25},{9,17},{17,9},{25,1},{2,26},{10... | collective-permute-start | bytes 884744 | tf_op jit(solution)/shard_map/ppermute | solution.py:1000
  194.3 8.8 %collective-permute-start.10 = (bf16[3,128,384]{2,1,0:T(8,128)(2,1)S(1)}, bf16[3,128,384]{2,1,0:T(8,128)(2,1)S(1)}, u32[]{:S(2)}, u32[]{:S(2)}) collective-permute-start(bf16[3,128,384]{2,1,0:T(8,128)(2,1)S(1)} %get-tuple-element.265), channel_id=1, source_target_pairs={{0,16},{8,24},{16,0},{24,8},{1,17},{9,25},{17,1},{25,9},{2,18},{10... | collective-permute-start | bytes 884744 | tf_op jit(solution)/shard_map/ppermute | solution.py:1000
  195.7 7.4 %collective-permute-start.9 = (bf16[3,128,384]{2,1,0:T(8,128)(2,1)S(1)}, bf16[3,128,384]{2,1,0:T(8,128)(2,1)S(1)}, u32[]{:S(2)}, u32[]{:S(2)}) collective-permute-start(bf16[3,128,384]{2,1,0:T(8,128)(2,1)S(1)} %get-tuple-element.266), channel_id=1, source_target_pairs={{0,8},{8,0},{16,24},{24,16},{1,9},{9,1},{17,25},{25,17},{2,10},{10... | collective-permute-start | bytes 884744 | tf_op jit(solution)/shard_map/ppermute | solution.py:1000
  282.5 12.3 %copy-start.54 = (bf16[8,320,1536]{2,1,0:T(8,128)(2,1)S(1)}, bf16[8,320,1536]{2,1,0:T(8,128)(2,1)}, u32[]{:S(2)}) copy-start(bf16[8,320,1536]{2,1,0:T(8,128)(2,1)} %get-tuple-element.188) | copy-start | bytes 23592964
  282.5 12.3 %copy-start.55 = (bf16[8,320,384]{2,1,0:T(8,128)(2,1)S(1)}, bf16[8,320,384]{2,1,0:T(8,128)(2,1)}, u32[]{:S(2)}) copy-start(bf16[8,320,384]{2,1,0:T(8,128)(2,1)} %get-tuple-element.189) | copy-start | bytes 5898244
  284.4 23.7 %collective-permute-start.18 = (bf16[5,128,384]{2,1,0:T(8,128)(2,1)S(1)}, bf16[5,128,384]{2,1,0:T(8,128)(2,1)S(1)}, u32[]{:S(2)}, u32[]{:S(2)}) collective-permute-start(bf16[5,128,384]{2,1,0:T(8,128)(2,1)S(1)} %get-tuple-element.244), channel_id=1, source_target_pairs={{0,24},{8,16},{16,8},{24,0},{1,25},{9,17},{17,9},{25,1},{2,26},{10... | collective-permute-start | bytes 1474568 | tf_op jit(solution)/shard_map/ppermute | solution.py:1000
  285.6 22.5 %collective-permute-start.17 = (bf16[5,128,384]{2,1,0:T(8,128)(2,1)S(1)}, bf16[5,128,384]{2,1,0:T(8,128)(2,1)S(1)}, u32[]{:S(2)}, u32[]{:S(2)}) collective-permute-start(bf16[5,128,384]{2,1,0:T(8,128)(2,1)S(1)} %get-tuple-element.245), channel_id=1, source_target_pairs={{0,16},{8,24},{16,0},{24,8},{1,17},{9,25},{17,1},{25,9},{2,18},{10... | collective-permute-start | bytes 1474568 | tf_op jit(solution)/shard_map/ppermute | solution.py:1000
  286.8 21.4 %collective-permute-start.16 = (bf16[5,128,384]{2,1,0:T(8,128)(2,1)S(1)}, bf16[5,128,384]{2,1,0:T(8,128)(2,1)S(1)}, u32[]{:S(2)}, u32[]{:S(2)}) collective-permute-start(bf16[5,128,384]{2,1,0:T(8,128)(2,1)S(1)} %get-tuple-element.246), channel_id=1, source_target_pairs={{0,8},{8,0},{16,24},{24,16},{1,9},{9,1},{17,25},{25,17},{2,10},{10... | collective-permute-start | bytes 1474568 | tf_op jit(solution)/shard_map/ppermute | solution.py:1000
  287.1 13.2 %slice-start.6 = ((s8[5898240]{0:T(1024)(128)(4,1)}), s8[4194304]{0:T(1024)(128)(4,1)S(1)}, s32[]{:S(2)}) async-start(s8[5898240]{0:T(1024)(128)(4,1)} %bitcast.346), calls=%async_computation.6 | async-start | bytes 8388608
  311.3 53.9 %collective-permute-start.19 = (bf16[5,128,384]{2,1,0:T(8,128)(2,1)}, bf16[5,128,384]{2,1,0:T(8,128)(2,1)S(1)}, u32[]{:S(2)}, u32[]{:S(2)}) collective-permute-start(bf16[5,128,384]{2,1,0:T(8,128)(2,1)} %get-tuple-element.235), channel_id=1, source_target_pairs={{0,0},{4,1},{16,2},{20,3},{1,4},{5,5},{17,6},{21,7},{8,8},{12,9},{... | collective-permute-start | bytes 1474568 | tf_op jit(solution)/shard_map/ppermute | solution.py:1061
  316.5 48.6 %collective-permute-start.22 = (bf16[5,128,384]{2,1,0:T(8,128)(2,1)S(1)}, bf16[5,128,384]{2,1,0:T(8,128)(2,1)}, u32[]{:S(2)}, u32[]{:S(2)}) collective-permute-start(bf16[5,128,384]{2,1,0:T(8,128)(2,1)S(1)} %get-tuple-element.236), channel_id=1, source_target_pairs={{10,0},{14,1},{26,2},{30,3},{11,4},{15,5},{27,6},{31,7},{2,8},{6,9... | collective-permute-start | bytes 1474568 | tf_op jit(solution)/shard_map/ppermute | solution.py:1061
  317.5 47.7 %collective-permute-start.21 = (bf16[5,128,384]{2,1,0:T(8,128)(2,1)S(1)}, bf16[5,128,384]{2,1,0:T(8,128)(2,1)}, u32[]{:S(2)}, u32[]{:S(2)}) collective-permute-start(bf16[5,128,384]{2,1,0:T(8,128)(2,1)S(1)} %get-tuple-element.237), channel_id=1, source_target_pairs={{2,0},{6,1},{18,2},{22,3},{3,4},{7,5},{19,6},{23,7},{10,8},{14,9},... | collective-permute-start | bytes 1474568 | tf_op jit(solution)/shard_map/ppermute | solution.py:1061
  322.1 43.1 %collective-permute-start.20 = (bf16[5,128,384]{2,1,0:T(8,128)(2,1)S(1)}, bf16[5,128,384]{2,1,0:T(8,128)(2,1)}, u32[]{:S(2)}, u32[]{:S(2)}) collective-permute-start(bf16[5,128,384]{2,1,0:T(8,128)(2,1)S(1)} %get-tuple-element.238), channel_id=1, source_target_pairs={{8,0},{12,1},{24,2},{28,3},{9,4},{13,5},{25,6},{29,7},{0,8},{4,9},... | collective-permute-start | bytes 1474568 | tf_op jit(solution)/shard_map/ppermute | solution.py:1061
  365.2 84.0 %collective-permute-start.23 = (bf16[2,512,384]{2,1,0:T(8,128)(2,1)}, bf16[2,512,384]{2,1,0:T(8,128)(2,1)}, u32[]{:S(2)}, u32[]{:S(2)}) collective-permute-start(bf16[2,512,384]{2,1,0:T(8,128)(2,1)} %get-tuple-element.129), channel_id=1, source_target_pairs={{1,0},{0,1},{3,2},{2,3},{5,4},{4,5},{7,6},{6,7},{9,8},{8,9},{11,10... | collective-permute-start | bytes 2359304 | tf_op jit(solution)/shard_map/ppermute | solution.py:1092
  368.9 46.9 %copy-start = (bf16[3,1024,384]{2,1,0:T(8,128)(2,1)S(1)}, bf16[3,1024,384]{2,1,0:T(8,128)(2,1)}, u32[]{:S(2)}) copy-start(bf16[3,1024,384]{2,1,0:T(8,128)(2,1)} %get-tuple-element.152) | copy-start | bytes 7077892
  421.1 59.6 %collective-permute-start.26 = (bf16[3,512,384]{2,1,0:T(8,128)(2,1)}, bf16[3,512,384]{2,1,0:T(8,128)(2,1)}, u32[]{:S(2)}, u32[]{:S(2)}) collective-permute-start(bf16[3,512,384]{2,1,0:T(8,128)(2,1)} %get-tuple-element.148), channel_id=1, source_target_pairs={{1,0},{0,1},{3,2},{2,3},{5,4},{4,5},{7,6},{6,7},{9,8},{8,9},{11,10... | collective-permute-start | bytes 3538952 | tf_op jit(solution)/shard_map/ppermute | solution.py:1092
  449.2 14.2 %copy-start.16 = (f32[128,384]{1,0:T(8,128)S(1)}, f32[128,384]{1,0:T(8,128)}, u32[]{:S(2)}) copy-start(f32[128,384]{1,0:T(8,128)} %reduce_sum.112) | copy-start | bytes 589828
  453.1 11.6 %copy-start.23 = (f32[3,8,384]{2,1,0:T(8,128)S(1)}, f32[3,8,384]{2,1,0:T(8,128)}, u32[]{:S(2)}) copy-start(f32[3,8,384]{2,1,0:T(8,128)} %get-tuple-element.191) | copy-start | bytes 110596
  455.0 15.8 %collective-permute-start.25 = (bf16[2,256,384]{2,1,0:T(8,128)(2,1)}, bf16[2,256,384]{2,1,0:T(8,128)(2,1)S(1)}, u32[]{:S(2)}, u32[]{:S(2)}) collective-permute-start(bf16[2,256,384]{2,1,0:T(8,128)(2,1)} %get-tuple-element.275), channel_id=1, source_target_pairs={{2,0},{6,1},{0,2},{4,3},{3,4},{7,5},{1,6},{5,7},{10,8},{14,9},{8,1... | collective-permute-start | bytes 1179656 | tf_op jit(solution)/shard_map/ppermute | solution.py:1099
  461.5 17.8 %collective-permute-start.24 = (bf16[2,256,384]{2,1,0:T(8,128)(2,1)S(1)}, bf16[2,256,384]{2,1,0:T(8,128)(2,1)}, u32[]{:S(2)}, u32[]{:S(2)}) collective-permute-start(bf16[2,256,384]{2,1,0:T(8,128)(2,1)S(1)} %get-tuple-element.276), channel_id=1, source_target_pairs={{0,0},{4,1},{2,2},{6,3},{1,4},{5,5},{3,6},{7,7},{8,8},{12,9},{10,1... | collective-permute-start | bytes 1179656 | tf_op jit(solution)/shard_map/ppermute | solution.py:1099
  480.7 6.8 %copy-start.22 = (f32[8,384]{1,0:T(8,128)S(1)}, f32[8,384]{1,0:T(8,128)}, u32[]{:S(2)}) copy-start(f32[8,384]{1,0:T(8,128)} %reduce_sum.115) | copy-start | bytes 36868
  480.7 6.8 %copy-start.31 = (pred[64]{0:T(512)(128)(4,1)S(1)}, pred[64]{0:T(512)(128)(4,1)}, u32[]{:S(2)}) copy-start(pred[64]{0:T(512)(128)(4,1)} %broadcast_in_dim.49) | copy-start | bytes 196
  600.5 19.8 %collective-permute-start.28 = (bf16[3,256,384]{2,1,0:T(8,128)(2,1)S(1)}, bf16[3,256,384]{2,1,0:T(8,128)(2,1)S(1)}, u32[]{:S(2)}, u32[]{:S(2)}) collective-permute-start(bf16[3,256,384]{2,1,0:T(8,128)(2,1)S(1)} %get-tuple-element.257), channel_id=1, source_target_pairs={{2,0},{6,1},{0,2},{4,3},{3,4},{7,5},{1,6},{5,7},{10,8},{14,9},{8,1... | collective-permute-start | bytes 1769480 | tf_op jit(solution)/shard_map/ppermute | solution.py:1099
  602.5 25.4 %collective-permute-start.27 = (bf16[3,256,384]{2,1,0:T(8,128)(2,1)S(1)}, bf16[3,256,384]{2,1,0:T(8,128)(2,1)S(1)}, u32[]{:S(2)}, u32[]{:S(2)}) collective-permute-start(bf16[3,256,384]{2,1,0:T(8,128)(2,1)S(1)} %get-tuple-element.258), channel_id=1, source_target_pairs={{0,0},{4,1},{2,2},{6,3},{1,4},{5,5},{3,6},{7,7},{8,8},{12,9},{10,1... | collective-permute-start | bytes 1769480 | tf_op jit(solution)/shard_map/ppermute | solution.py:1099
  (45 other events, 128.5 us)

commit v3 on v2

--- a/solution.py
+++ b/solution.py
@@ -141,11 +141,112 @@
     return value.reshape(-1, value.shape[-1])
 
 
+class Layout:
+    def __init__(self, sizes, latents_shape):
+        self.clips_dev, self.frames, self.patches, self.width = latents_shape
+        self.n_ta, self.n_pa, self.n_dev = sizes["ta"], sizes["pa"], sizes["dev"]
+        self.clips = self.clips_dev * self.n_dev
+        self.run = self.n_pa // self.clips
+        self.group = self.run * self.n_dev
+        self.near = self.n_pa // self.group
+        self.halves = self.n_ta // self.near
+        self.space_rows = self.near * self.patches
+        self.time_patches = self.space_rows // self.n_ta
+        self.other_rows = (self.group - 1) * self.space_rows
+        self.key_rows = self.group * self.space_rows
+        self.all_frames = self.n_ta * self.frames
+
+    def here(self):
+        return {name: lax.axis_index(name) for name in ("ta", "pa", "dev")}
+
+    def clip(self, me):
+        return me["pa"] // self.run
+
+    def member(self, me):
+        return me["dev"] * self.run + me["pa"] % self.run
+
+    def space_place(self, ta, clip, member):
+        return {"ta": ta, "pa": clip * self.run + member % self.run, "dev": member // self.run}
+
+    def space_target(self, me, j):
+        return self.space_place(me["ta"], me["dev"] * self.clips_dev + j, me["pa"] // self.near)
+
+    def owner(self, me, ta, slot):
+        return {"ta": ta, "pa": self.near * self.member(me) + slot, "dev": self.clip(me) // self.clips_dev}
+
+    def time_target(self, me, j, s):
+        place = self.space_target(me, j)
+        return {**place, "ta": (me["pa"] % self.near) * self.halves + s}
+
+    def fellow(self, me, step):
+        return self.space_place(me["ta"], self.clip(me), (self.member(me) + step) % self.group)
+
+    def across(self, me, step):
+        return {**me, "ta": (me["ta"] + step) % self.n_ta}
+
+
+def is_me(me, place):
+    same = None
+    for name, index in place.items():
+        if index is not me[name]:
+            equal = index == me[name]
+            same = equal if same is None else same & equal
+    return same
+
+
+def greet(me, place):
+    @pl.when(jnp.logical_not(is_me(me, place)))
+    def _():
+        pl.semaphore_signal(
+            pltpu.get_barrier_semaphore(), inc=1, device_id=place, device_id_type=pl.DeviceIdType.MESH
+        )
+
+
+def await_greetings(me, places):
+    amount = jnp.int32(0)
+    for place in places:
+        amount = amount + jnp.logical_not(is_me(me, place)).astype(jnp.int32)
+    pl.semaphore_wait(pltpu.get_barrier_semaphore(), amount)
+
+
+def push(src, dst, send_sem, recv_sem, place):
+    return pltpu.make_async_remote_copy(
+        src_ref=src,
+        dst_ref=dst,
+        send_sem=send_sem,
+        recv_sem=recv_sem,
+        device_id=place,
+        device_id_type=pl.DeviceIdType.MESH,
+    )
+
+
+def start_push(me, src, dst, send_sem, recv_sem, place):
+    same = is_me(me, place)
+
+    @pl.when(same)
+    def _():
+        pltpu.make_async_copy(src, dst, recv_sem).start()
+
+    @pl.when(jnp.logical_not(same))
+    def _():
+        push(src, dst, send_sem, recv_sem, place).start()
+
+
+def end_push(me, src, dst, send_sem, recv_sem, place):
+    @pl.when(jnp.logical_not(is_me(me, place)))
+    def _():
+        push(src, dst, send_sem, recv_sem, place).wait_send()
+
+
+def arrived(dst, recv_sem):
+    pltpu.make_async_copy(dst, dst, recv_sem).wait()
+
+
 def space_forward_kernel(
-    first_frame,
+    lay,
     counts_ref,
-    own_ref,
-    other_ref,
+    latents_ref,
+    cot_ref,
     mod_ref,
     attn_ref,
     turned_ref,
@@ -155,6 +256,8 @@
     up_ref,
     down_ref,
     state_ref,
+    moved_ref,
+    own_ref,
     normed_ref,
     query_ref,
     keys_t_ref,
@@ -175,15 +278,101 @@
     slope_ref,
     branch2_ref,
     branch5_ref,
+    own_buf,
+    other_buf,
+    sent_buf,
+    lat_send,
+    lat_recv,
+    fellow_send,
+    fellow_recv,
+    state_send,
+    state_recv,
+    cot_send,
+    cot_recv,
 ):
     scale_by = HDIM ** (-0.5)
-    frame = counts_ref[2] + first_frame + pl.program_id(0)
+    me = lay.here()
+    step = pl.program_id(0)
+    frames, near = lay.frames, lay.near
+    last = step == frames - 1
+
+    def latent_copy(j, f):
+        slot = me["pa"] % near
+        return (
+            latents_ref.at[j, f], own_buf.at[f, slot], lat_send.at[j, f], lat_recv.at[f, slot], lay.space_target(me, j),
+        )
+
+    def fellow_copy(turn, f):
+        return (
+            own_buf.at[f], other_buf.at[f, turn - 1], fellow_send.at[turn - 1, f], fellow_recv.at[turn - 1, f],
+            lay.fellow(me, turn),
+        )
+
+    def state_copy(turn, f):
+        place = lay.across(me, turn)
+        row = pl.multiple_of(place["ta"] * lay.time_patches, TILE)
+        return (
+            sent_buf.at[f, pl.ds(row, lay.time_patches)], state_ref.at[me["ta"] * frames + f], state_send.at[turn, f],
+            state_recv.at[turn, f], place,
+        )
+
+    def cot_copy(j, s):
+        return (
+            cot_ref.at[j, :, pl.ds(s * lay.time_patches, lay.time_patches)],
+            moved_ref.at[pl.ds(me["ta"] * frames, frames)],
+            cot_send.at[j, s], cot_recv.at[me["ta"]], lay.time_target(me, j, s),
+        )
+
+    def start_latents(f):
+        for j in range(lay.clips_dev):
+            start_push(me, *latent_copy(j, f))
+
+    def pass_on(f):
+        for slot in range(near):
+            arrived(own_buf.at[f, slot], lat_recv.at[f, slot])
+        for turn in range(1, lay.group):
+            push(*fellow_copy(turn, f)).start()
+
+    @pl.when(step == 0)
+    def _():
+        for slot in range(near):
+            greet(me, lay.owner(me, me["ta"], slot))
+        for t in range(lay.n_ta):
+            greet(me, lay.owner(me, t, me["ta"] // lay.halves))
+        friends = [lay.fellow(me, turn) for turn in range(1, lay.group)]
+        friends += [lay.across(me, turn) for turn in range(1, lay.n_ta)]
+        for friend in friends:
+            greet(me, friend)
+        targets = [lay.space_target(me, j) for j in range(lay.clips_dev)]
+        targets += [lay.time_target(me, j, s) for j in range(lay.clips_dev) for s in range(lay.halves)]
+        await_greetings(me, targets + friends)
+        start_latents(0)
+        if frames > 1:
+            start_latents(1)
+        pass_on(0)
+
+    @pl.when(step + 2 < frames)
+    def _():
+        start_latents(step + 2)
+
+    @pl.when(step == min(1, frames - 1))
+    def _():
+        for j in range(lay.clips_dev):
+            for s in range(lay.halves):
+                start_push(me, *cot_copy(j, s))
+
+    for turn in range(1, lay.group):
+        arrived(other_buf.at[step, turn - 1], fellow_recv.at[turn - 1, step])
+    frame = counts_ref[2] + step
     keep = (frame < counts_ref[0]).astype(F32)
     mod = mod_ref[...]
-    own = fold(own_ref).astype(F32)
-    rows = own.shape[0]
+    own_low = own_buf[step].reshape(lay.space_rows, lay.width)
+    own_ref[0] = own_low
+    own = own_low.astype(F32)
+    rows = lay.space_rows
     normed_own = (norm_parts(own)[0] * (1.0 + mod[1:2]) + mod[0:1]).astype(BF)
-    normed_other = (norm_parts(fold(other_ref).astype(F32))[0] * (1.0 + mod[1:2]) + mod[0:1]).astype(BF)
+    other = other_buf[step].reshape(lay.other_rows, lay.width).astype(F32)
+    normed_other = (norm_parts(other)[0] * (1.0 + mod[1:2]) + mod[0:1]).astype(BF)
     normed = jnp.concatenate([normed_own, normed_other], axis=0)
     normed_ref[0] = normed
     queries = (dot(normed_own, attn_ref[0]).astype(BF) * scale_by).astype(BF)
@@ -203,9 +392,14 @@
     att_t_ref[0] = att_t.astype(BF)
     att = att_t.T.astype(BF)
     att_ref[0] = att
-    branch = dot(att, attn_ref[3])
+
+    @pl.when(jnp.logical_not(last))
+    def _():
+        pass_on(step + 1)
+
+    branch = dot(att_ref[0], attn_ref[3])
     branch2_ref[0] = branch.astype(BF)
-    state = own + (keep * mod[2:3]) * branch
+    state = own_ref[0].astype(F32) + (keep * mod[2:3]) * branch
     cross_in = state.astype(BF)
     cross_in_ref[0] = cross_in
     cross_queries = (dot(cross_in, cross_ref[0]).astype(BF) * scale_by).astype(BF)
@@ -233,7 +427,29 @@
     branch = dot(act, down_ref[...])
     branch5_ref[0] = branch.astype(BF)
     state = state + (keep * mod[5:6]) * branch
-    state_ref[0] = state.astype(BF)
+    sent_buf[step] = state.astype(BF)
+    src, dst, _, sem, _ = state_copy(0, step)
+    pltpu.make_async_copy(src, dst, sem).start()
+    for turn in range(1, lay.n_ta):
+        push(*state_copy(turn, step)).start()
+
+    @pl.when(last)
+    def _():
+        for f in range(frames):
+            for j in range(lay.clips_dev):
+                end_push(me, *latent_copy(j, f))
+            for turn in range(1, lay.group):
+                push(*fellow_copy(turn, f)).wait_send()
+            for turn in range(1, lay.n_ta):
+                push(*state_copy(turn, f)).wait_send()
+            for turn in range(lay.n_ta):
+                src, dst, _, sem, _ = state_copy(turn, f)
+                arrived(dst, sem)
+        for j in range(lay.clips_dev):
+            for s in range(lay.halves):
+                end_push(me, *cot_copy(j, s))
+        for t in range(lay.n_ta):
+            arrived(moved_ref.at[pl.ds(t * frames, frames)], cot_recv.at[t])
 
 
 def space_backward_kernel(
@@ -714,13 +930,14 @@
 
 
 SCALARS = pl.BlockSpec(memory_space=pltpu.SMEM)
+HBM = pl.BlockSpec(memory_space=pl.ANY)
 
 
 def shape_of(shape, dtype):
     return jax.ShapeDtypeStruct(shape, dtype)
 
 
-def call(kernel, grid, inputs, in_specs, outputs, out_specs, flops, scratch=()):
+def call(kernel, grid, inputs, in_specs, outputs, out_specs, flops, scratch=(), collective_id=None):
     moved = sum(math.prod(a.shape) * a.dtype.itemsize for a in (*inputs, *outputs))
     return pl.pallas_call(
         kernel,
@@ -729,7 +946,9 @@
         out_specs=out_specs,
         out_shape=outputs,
         scratch_shapes=list(scratch),
-        compiler_params=pltpu.CompilerParams(vmem_limit_bytes=VMEM_BYTES),
+        compiler_params=pltpu.CompilerParams(
+            vmem_limit_bytes=VMEM_BYTES, collective_id=collective_id, has_side_effects=collective_id is not None
+        ),
         cost_estimate=pl.CostEstimate(flops=int(flops), bytes_accessed=int(moved), transcendentals=0),
     )(*inputs)
 
@@ -754,19 +973,13 @@
         frame_up,
         frame_down,
     ):
+        lay = Layout(sizes, latents.shape)
         clips_dev, frames, patches, width = latents.shape
-        clips = clips_dev * n_dev
-        run = n_pa // clips
-        group = run * n_dev
-        near = n_pa // group
-        space_rows = near * patches
-        time_patches = space_rows // n_ta
-        other_rows = (group - 1) * space_rows
-        key_rows = group * space_rows
-        all_frames = n_ta * frames
+        clips, run, group, near, halves = lay.clips, lay.run, lay.group, lay.near, lay.halves
+        space_rows, other_rows, key_rows = lay.space_rows, lay.other_rows, lay.key_rows
+        time_patches, all_frames = lay.time_patches, lay.all_frames
         ta, pa, dev = (lax.axis_index(name) for name in ("ta", "pa", "dev"))
-        clip = pa // run
-        member = dev * run + pa % run
+        clip, member = lay.clip(lay.here()), lay.member(lay.here())
 
         def place(clip_id, member_id):
             return (clip_id * run + member_id % run) * n_dev + member_id // run
@@ -778,8 +991,6 @@
                     k = d * clips_dev + (p + step) % clips_dev
                     pairs.append((p * n_dev + d, place(k, p // near)))
             return pairs
-
-        halves = n_ta // near
 
         def time_pairs(step):
             u, w = step % halves, step // halves
@@ -842,73 +1053,82 @@
         patch_turned = jnp.swapaxes(patch_attn[1:3], 1, 2)
         frame_turned = jnp.swapaxes(frame_attn[1:3], 1, 2)
 
-        def to_space(frame_ids):
-            picked = latents[:, frame_ids[0] : frame_ids[-1] + 1]
-            parts = []
-            for step in range(clips_dev):
-                sent = lax.dynamic_index_in_dim(picked, (pa + step) % clips_dev, 0, keepdims=False)
-                parts.append(lax.ppermute(sent, pair_axes, space_pairs(step)))
-            stacked = jnp.stack(parts)
-            slots = [
-                lax.dynamic_index_in_dim(stacked, (clip - b) % clips_dev, 0, keepdims=False) for b in range(near)
-            ]
-            own = jnp.concatenate(slots, axis=1)
-            others = [lax.ppermute(own, pair_axes, group_pairs(step)) for step in range(1, group)]
-            return own, jnp.concatenate(others, axis=1)
-
-        def space_forward(frame_ids, own, other):
+        def out(*shape, dtype=BF):
+            return shape_of((frames,) + shape, dtype)
+
+        def moved_tokens():
+            return shape_of((all_frames, time_patches, width), BF)
+
+        hidden = patch_up.shape[1]
+        inputs = (
+            counts, latents, cotangent, space_mod, patch_attn, patch_turned, cross_ends, text_keys, text_values.T,
+            patch_up, patch_down,
+        )
+        outputs = (
+            moved_tokens(),
+            moved_tokens(),
+            out(space_rows, width),
+            out(key_rows, width),
+            out(space_rows, width),
+            out(width, key_rows),
+            out(key_rows, width),
+            out(HEADS, key_rows, space_rows),
+            out(width, space_rows),
+            out(space_rows, width),
+            out(8, space_rows, dtype=F32),
+            out(space_rows, width),
+            out(space_rows, width),
+            out(HEADS, text_rows, space_rows),
+            out(width, space_rows),
+            out(space_rows, width),
+            out(8, space_rows, dtype=F32),
+            out(space_rows, width, dtype=F32),
+            out(space_rows, width),
+            out(space_rows, hidden),
+            out(space_rows, hidden),
+            out(space_rows, width),
+            out(space_rows, width),
+        )
+        dense = 2 * frames * space_rows * width * (6 * width + 2 * hidden) + 8 * frames * key_rows * width * width
+        dma = pltpu.SemaphoreType.DMA
+        state, cot, *saved = call(
+            lambda *refs: space_forward_kernel(lay, *refs),
+            (frames,),
+            inputs,
+            [SCALARS, HBM, HBM] + [whole(a) for a in inputs[3:]],
+            outputs,
+            [HBM, HBM] + [framed(a) for a in outputs[2:]],
+            dense + 16 * frames * space_rows * key_rows * width,
+            [
+                pltpu.VMEM((frames, near, patches, width), BF),
+                pltpu.VMEM((frames, group - 1, near, patches, width), BF),
+                pltpu.VMEM((frames, space_rows, width), BF),
+                dma((clips_dev, frames)),
+                dma((frames, near)),
+                dma((group - 1, frames)),
+                dma((group - 1, frames)),
+                dma((n_ta, frames)),
+                dma((n_ta, frames)),
+                dma((clips_dev, halves)),
+                dma((n_ta,)),
+            ],
+            collective_id=1,
+        )
+
+        def space_backward(frame_ids, grad, saved):
             count = len(frame_ids)
 
             def out(*shape, dtype=BF):
                 return shape_of((count,) + shape, dtype)
 
-            inputs = (
-                counts, own, other, space_mod, patch_attn, patch_turned, cross_ends, text_keys, text_values.T,
-                patch_up, patch_down,
-            )
-            hidden = patch_up.shape[1]
-            outputs = (
-                out(space_rows, width),
-                out(key_rows, width),
-                out(space_rows, width),
-                out(width, key_rows),
-                out(key_rows, width),
-                out(HEADS, key_rows, space_rows),
-                out(width, space_rows),
-                out(space_rows, width),
-                out(8, space_rows, dtype=F32),
-                out(space_rows, width),
-                out(space_rows, width),
-                out(HEADS, text_rows, space_rows),
-                out(width, space_rows),
-                out(space_rows, width),
-                out(8, space_rows, dtype=F32),
-                out(space_rows, width, dtype=F32),
-                out(space_rows, width),
-                out(space_rows, hidden),
-                out(space_rows, hidden),
-                out(space_rows, width),
-                out(space_rows, width),
-            )
-            dense = 2 * count * space_rows * width * (6 * width + 2 * hidden) + 8 * count * key_rows * width * width
-            return call(
-                lambda *refs: space_forward_kernel(frame_ids[0], *refs),
-                (count,),
-                inputs,
-                [SCALARS, framed(own), framed(other)] + [whole(a) for a in inputs[3:]],
-                outputs,
-                [framed(a) for a in outputs],
-                dense + 16 * count * space_rows * key_rows * width,
-            )
-
-        def space_backward(frame_ids, grad, saved):
-            count = len(frame_ids)
-
-            def out(*shape, dtype=BF):
-                return shape_of((count,) + shape, dtype)
-
             (_, _, query, keys_t, value, exponent, att_t, _, inverse, _, cross_query, cross_exponent, cross_att_t, _,
              cross_inverse, middle, _, _, slope, branch2, branch5) = saved
+            start = frame_ids[0]
+
+            def framed_from(array):
+                tail = (0,) * (array.ndim - 1)
+                return pl.BlockSpec((1,) + tuple(array.shape[1:]), lambda frame: (frame + start,) + tail)
+
             inputs = (
                 counts, grad, space_mod, patch_attn, cross_ends, text_keys.T, text_values, patch_up, patch_down,
                 query, keys_t, value, exponent, att_t, inverse, cross_query, cross_exponent, cross_att_t,
@@ -937,7 +1157,7 @@
                 lambda *refs: space_backward_kernel(frame_ids[0], *refs),
                 (count,),
                 inputs,
-                [SCALARS, grad_spec] + [whole(a) for a in inputs[2:9]] + [framed(a) for a in inputs[9:]],
+                [SCALARS, grad_spec] + [whole(a) for a in inputs[2:9]] + [framed_from(a) for a in inputs[9:]],
                 outputs,
                 [framed(a) for a in outputs],
                 dense + 32 * count * space_rows * key_rows * width,
@@ -960,38 +1180,9 @@
                 count * space_rows * width * 30,
             )
 
-        near_frames = min(2, frames)
-        frame_groups = [tuple(range(near_frames)), tuple(range(near_frames, frames))]
-        frame_groups = [ids for ids in frame_groups if ids]
-        arrived = [to_space(ids) for ids in frame_groups]
-        owns = [own for own, _ in arrived]
-        cotangent, owns[-1] = lax.optimization_barrier((cotangent, owns[-1]))
-        saves = [
-            space_forward(ids, own, other) for ids, own, (_, other) in zip(frame_groups, owns, arrived)
-        ]
-        states = [saved[0] for saved in saves]
-
+        frame_groups = [ids for ids in (tuple(range(min(2, frames))), tuple(range(min(2, frames), frames))) if ids]
+        slot = ta % halves
         n_steps = halves * clips_dev
-        cot_parts = []
-        for step in range(n_steps):
-            u, w = step % halves, step // halves
-            s = (ta % halves + u) % halves
-            j = (ta // halves + w) % clips_dev
-            sent = lax.dynamic_slice(
-                cotangent, (j, 0, s * time_patches, 0), (1, frames, time_patches, width)
-            )[0]
-            cot_parts.append(lax.ppermute(sent, whole_axes, time_pairs(step)))
-        cot_stack = jnp.stack(cot_parts)
-        slot = ta % halves
-
-        def step_from(source):
-            u = (slot - source % halves) % halves
-            w = (clip % clips_dev - source // halves) % clips_dev
-            return w * halves + u
-
-        cot = jnp.concatenate(
-            [lax.dynamic_index_in_dim(cot_stack, step_from(t), 0, keepdims=False) for t in range(n_ta)]
-        )
 
         def exchange(pieces):
             got = [lax.dynamic_index_in_dim(pieces, ta, 0, keepdims=False)]
@@ -1002,12 +1193,6 @@
             return jnp.stack(
                 [lax.dynamic_index_in_dim(stacked, ta ^ t, 0, keepdims=False) for t in range(n_ta)]
             )
-
-        state_groups = []
-        for state in states:
-            pieces = state.reshape(state.shape[0], n_ta, time_patches, width).swapaxes(0, 1)
-            state_groups.append(exchange(pieces))
-        state = jnp.concatenate(state_groups, axis=1).reshape(all_frames, time_patches, width)
 
         block_rows = all_frames * BLOCK
         run_rows = all_frames * SUB
@@ -1079,7 +1264,8 @@
         d_frame_down = weight_grad(act4, branch5)
 
         pieces, backs, finish_six = [], [], []
-        for i, (frame_ids, own, saved) in enumerate(zip(frame_groups, owns, saves)):
+        for i, frame_ids in enumerate(frame_groups):
+            own = saved[0][frame_ids[0] : frame_ids[-1] + 1]
             grad = grad_s[:, frame_ids[0] : frame_ids[-1] + 1]
             if i == 1:
                 grad, output = lax.optimization_barrier((grad, output))
@@ -1114,26 +1300,25 @@
 
         def grad_over(lists, index, others, other_index):
             total = None
-            for one, two in zip(lists, others):
-                left, right = one[index], two[other_index]
+            for ids, two in zip(frame_groups, others):
+                left, right = lists[index][ids[0] : ids[-1] + 1], two[other_index]
                 left, right = left.reshape(-1, left.shape[-1]), right.reshape(-1, right.shape[-1])
                 part = lax.dot_general(left, right, (((0,), (0,)), ((), ())), preferred_element_type=F32)
                 total = part if total is None else total + part
             return total.astype(BF)
 
-        d_patch_up = grad_over(saves, 16, backs, 4)
-        d_patch_down = grad_over(saves, 17, backs, 3)
-        d_cross_proj = grad_over(saves, 13, backs, 5)
-        d_cross_q = grad_over(saves, 9, backs, 6)
+        d_patch_up = grad_over(saved, 16, backs, 4)
+        d_patch_down = grad_over(saved, 17, backs, 3)
+        d_cross_proj = grad_over(saved, 13, backs, 5)
+        d_cross_q = grad_over(saved, 9, backs, 6)
         text_t = text.astype(F32).T
         d_tk, d_tv = (over_frames(backs, i) for i in (11, 12))
         d_cross_k = jnp.dot(text_t, jnp.sum(d_tk, axis=0)[:text_count], precision=HIGHEST).astype(BF)
         d_cross_v = jnp.dot(text_t, jnp.sum(d_tv, axis=0)[:text_count], precision=HIGHEST).astype(BF)
-        d_patch_proj = grad_over(saves, 7, backs, 7)
-        near_saves = [(saved[1][:, :space_rows],) for saved in saves]
-        d_patch_q = grad_over(near_saves, 0, backs, 8)
-        d_patch_k = grad_over(saves, 1, backs, 9)
-        d_patch_v = grad_over(saves, 1, backs, 10)
+        d_patch_proj = grad_over(saved, 7, backs, 7)
+        d_patch_q = grad_over([saved[1][:, :space_rows]], 0, backs, 8)
+        d_patch_k = grad_over(saved, 1, backs, 9)
+        d_patch_v = grad_over(saved, 1, backs, 10)
         six = jnp.sum(over_frames(backs, 13), axis=0) + jnp.sum(jnp.concatenate(finish_six), axis=0)
         mine = jnp.stack([six, jnp.sum(frame_six, axis=0)])
         spread = jnp.where(jnp.arange(clips)[:, None, None, None] == clip, mine[None], 0.0)

time: 637 us -> 602 us (0.945)
  waiting for transfers between devices: 72 us -> 19.4 us
  Pallas kernels: 357 us -> 403 us
  starting transfers between devices: 56.3 us -> 39.8 us
  local copies, waits for them, and re-layouts: 33.8 us -> 24.5 us
    ppermute x10 -> x0, waiting for transfers between devices: 49.7 us -> none  [the longest x4 36.1 us: per_device(): cot_parts.append(lax.ppermute(sent, whole_axes, time_pairs(step)))]
    pallas_call x7 -> x6, Pallas kernels: 251 us -> 297 us  [call(): pl.pallas_call(kernel, grid=grid, in_specs=in_specs, out_specs=out_specs,...]
    ppermute x10 -> x0, starting transfers between devices: 20.4 us -> none  [the longest x4 11.3 us: to_space(): parts.append(lax.ppermute(sent, pair_axes, space_pairs(step)))]
  transfers between devices with their start and end apart: 29 -> 13, of which waited for: 10 -> 3; matrix products, arithmetic and copies ran while one was open for 18% -> 16% of each run, Pallas kernels for 26% -> 14%
where the time goes in v3:
time: 602 us; the launch traced here: 598 us
  Pallas kernels  403 us (67%)
  matrix products  66.6 us (11%)
  starting transfers between devices  39.8 us (7%)
  other arithmetic  38.6 us (6%)
  local copies, waits for them, and re-layouts  24.5 us (4%)
  waiting for transfers between devices  19.4 us (3%)
    pallas_call x6, Pallas kernels, call(): pl.pallas_call(kernel, grid=grid, in_specs=in_specs, out_specs=out_specs,...  297 us
    pallas_call x1, Pallas kernels, reduce_all(): pl.pallas_call(kernel, in_specs=[any_spec] * n + [vmem_spec], out_specs=[...  107 us
    dot_general x16, matrix products, grad_over(): lax.dot_general(left, right, (((0,), (0,)), ((), ())), preferred_element_...  36.9 us
    dot_general x4, matrix products, weight_grad(): lax.dot_general(left, right, (((0,), (0,)), ((), ())), preferred_element_...  20.3 us
    ppermute x4, waiting for transfers between devices, per_device(): got.append(lax.ppermute(sent, pair_axes, back(space_pairs(step))))  19.4 us
    ppermute x4, starting transfers between devices, per_device(): got.append(lax.ppermute(sent, pair_axes, back(space_pairs(step))))  15.6 us
    ppermute x4, starting transfers between devices, per_device(): out_parts.append(lax.ppermute(sent, whole_axes, back(time_pairs(step))))  15.1 us
  transfers between devices with their start and end apart: 13, of which 3 were waited for; matrix products, arithmetic and copies ran while one was open for 16% of the time, Pallas kernels for 14%

profile of v3, /device:TPU:1, one launch (start us, length us, event | category | flops | bytes accessed | tf_op | source)
XLA Modules:
  0.0 597.8 jit_solution(1253940045917820372)
XLA Ops:
  1.6 1.8 all-gather
  3.5 2.3 all_gather.7
  19.5 1.8 pad_add_fusion.1.refs_0_.counts_ref
  21.3 131.3 %shard_map.230 = (bf16[20,128,384]{2,1,0:T(8,128)(2,1)}, bf16[20,128,384]{2,1,0:T(8,128)(2,1)}, bf16[5,512,384]{2,1,0:T(8,128)(2,1)}, bf16[5,1024,384]{2,1,0:T(8...) custom-call(s32[4]{0:T(128)} %pad_add_fusion.1.refs_0_.counts_ref, ...), custom_call_target="tpu_custom_call" | custom-call | flops 32715571200 | bytes 101429264 | tf_op jit(solution)/shard_map/pallas_call | solution.py:942
  152.7 77.9 %shard_map.231 = (bf16[20,128,384]{2,1,0:T(8,128)(2,1)}, bf16[20,128,384]{2,1,0:T(8,128)(2,1)}, bf16[8,320,384]{2,1,0:T(8,128)(2,1)}, bf16[8,320,1152]{2,1,0:T(8...) custom-call(s32[4]{0:T(128)} %pad_add_fusion.1.refs_0_.counts_ref, ...), custom_call_target="tpu_custom_call" | custom-call | flops 27179089920 | bytes 43663376 | tf_op jit(solution)/shard_map/pallas_call | solution.py:942
  230.5 2.8 constant_dynamic-slice_fusion.5
  234.5 2.2 collective-permute-start.1
  236.8 6.5 %fusion.6.refs_10_ = bf16[384,1152]{1,0:T(8,128)(2,1)} fusion(bf16[8,320,384]{2,1,0:T(8,128)(2,1)S(1)} %copy-done.41, bf16[8,320,1152]{2,1,0:T(8,128)(2,1)} %get-tuple-element.141), kind=kOutput, calls=%fused_computation.13 | convolution fusion | flops 2265366528 | bytes 8749056 | tf_op jit(solution)/shard_map/dot_general | solution.py:1259
  243.3 4.3 fusion.2.refs_12_
  247.6 5.4 fusion.3.refs_13_
  256.5 4.0 fusion.14.refs_11_
  265.0 7.6 %collective-permute-start.3 = (bf16[5,128,384]{2,1,0:T(8,128)(2,1)S(1)}, bf16[5,128,384]{2,1,0:T(8,128)(2,1)S(1)}, u32[]{:S(2)}, u32[]{:S(2)}) collective-permute-start(bf16[5,128,384]{2,1,0:T(8,128)(2,1)S(1)} %get-tuple-element.193), channel_id=1, source_target_pairs={{0,0},{4,1},{16,2},{20,3},{1,4},{5,5},{17,6},{21,7},{8,8},{12,9},{... | collective-permute-start | bytes 1474568 | tf_op jit(solution)/shard_map/ppermute | solution.py:1246
  272.9 4.3 collective-permute-start.5
  277.2 2.8 collective-permute-start.4
  280.1 32.6 %shard_map.232 = (f32[2,512,384]{2,1,0:T(8,128)}, f32[2,512,384]{2,1,0:T(8,128)}, bf16[2,512,384]{2,1,0:T(8,128)(2,1)}, bf16[2,512,384]{2,1,0:T(8,128)(2,1)}, bf...) custom-call(s32[4]{0:T(128)} %pad_add_fusion.1.refs_0_.counts_ref, ...), custom_call_target="tpu_custom_call" | custom-call | flops 19528679424 | bytes 87101456 | tf_op jit(solution)/shard_map/pallas_call | solution.py:942
  314.0 1.7 reduce_sum.109
  316.9 5.3 convolution_bitcast_fusion.5
  325.7 45.1 %shard_map.234 = (f32[3,512,384]{2,1,0:T(8,128)}, f32[3,512,384]{2,1,0:T(8,128)}, bf16[3,512,384]{2,1,0:T(8,128)(2,1)}, bf16[3,512,384]{2,1,0:T(8,128)(2,1)}, bf...) custom-call(s32[4]{0:T(128)} %pad_add_fusion.1.refs_0_.counts_ref, ...), custom_call_target="tpu_custom_call" | custom-call | flops 29293019136 | bytes 94978064 | tf_op jit(solution)/shard_map/pallas_call | solution.py:942
  372.2 1.8 reduce_sum.110
  374.0 1.8 reduce_sum.113
  375.8 2.6 convolution_bitcast_fusion.16
  378.7 3.2 convolution_bitcast_fusion.14
  381.9 2.3 convolution_bitcast_fusion.13
  384.2 5.7 collective-permute-start.10
  392.2 1.8 fusion.19.refs_1_
  401.7 6.3 %fusion.5.refs_9_ = bf16[1536,384]{1,0:T(8,128)(2,1)} fusion(f32[1536,384]{1,0:T(8,128)S(1)} %copy-done.46, bf16[5,512,1536]{2,1,0:T(8,128)(2,1)} %get-tuple-element.137, bf16[3,512,384]{2,1,0:T(8,128)(2,1)S(1)} %copy-done.47), kind=kOutput, calls=%fused_computation.12 | convolution fusion | flops 1813118976 | bytes 12582912 | tf_op jit(solution)/shard_map/dot_general | solution.py:1306
  408.1 2.0 convolution_bitcast_fusion.6
  411.4 2.7 fusion.4.refs_8_
  414.1 3.9 shard_map.233
  418.0 2.1 dynamic-slice_bitcast_fusion.13
  420.1 11.0 %collective-permute-start.9 = (bf16[2,256,384]{2,1,0:T(8,128)(2,1)}, bf16[2,256,384]{2,1,0:T(8,128)(2,1)}, u32[]{:S(2)}, u32[]{:S(2)}) collective-permute-start(bf16[2,256,384]{2,1,0:T(8,128)(2,1)} %get-tuple-element.213), channel_id=1, source_target_pairs={{2,0},{6,1},{0,2},{4,3},{3,4},{7,5},{1,6},{5,7},{10,8},{14,9},{8,1... | collective-permute-start | bytes 1179656 | tf_op jit(solution)/shard_map/ppermute | solution.py:1285
  431.1 1.9 collective-permute-start.8
  433.1 3.1 fusion.18.refs_2_
  436.2 4.3 collective-permute-done.9
  440.5 7.0 %collective-permute-done.8 = bf16[2,256,384]{2,1,0:T(8,128)(2,1)} collective-permute-done((bf16[2,256,384]{2,1,0:T(8,128)(2,1)}, bf16[2,256,384]{2,1,0:T(8,128)(2,1)}, u32[]{:S(2)}, u32[]{:S(2)}) %collective-permute-start.8) | collective-permute-done | bytes 393248 | tf_op jit(solution)/shard_map/ppermute | solution.py:1285
  449.1 5.8 shard_map.235
  456.4 106.7 %shard_map.236 = (bf16[10752,384]{1,0:T(8,128)(2,1)}, f32[64,384]{1,0:T(8,128)}) custom-call(bf16[384,384]{1,0:T(8,128)(2,1)} %fusion.13.refs_0_, bf16[384,384]{1,0:T(8,128)(2,1)} %fusion.19.refs_1_, bf16[384,384]{1,0:T(8,128)(2,1)} %fusion.18.refs_2_, bf16[384,384]{1,0:T(8,128)(2,1)} %fusion.17.refs_3_, bf16[384,384]{1,0:T(8,128)(2,1)} %fusion.16.refs_4_, ...), custom_call_target="tpu_custom_call" | custom-call | flops 33030144 | bytes 16515072 | tf_op jit(solution)/shard_map/pallas_call | solution.py:908
  564.1 3.3 fusion.47
  568.3 2.0 collective-permute-start.11
  571.0 3.5 fusion.36
  574.5 1.6 maximum_convert_fusion.4
  576.1 1.7 maximum_convert_fusion.5
  577.8 1.6 maximum_convert_fusion.1
  579.4 1.7 maximum_convert_fusion.3
  581.1 1.6 maximum_convert_fusion.2
  582.7 4.1 slice_convert_fusion
  586.8 8.1 %collective-permute-done.11 = bf16[3,256,384]{2,1,0:T(8,128)(2,1)S(1)} collective-permute-done((bf16[3,256,384]{2,1,0:T(8,128)(2,1)S(1)}, bf16[3,256,384]{2,1,0:T(8,128)(2,1)S(1)}, u32[]{:S(2)}, u32[]{:S(2)}) %collective-permute-start.11) | collective-permute-done | bytes 589856 | tf_op jit(solution)/shard_map/ppermute | solution.py:1285
  595.4 2.2 maximum_convert_fusion
  (190 shorter events, 49.1 us)
Async XLA Ops:
  0.6 7.7 %copy-start.12 = (bf16[4,384,384]{2,1,0:T(8,128)(2,1)S(1)}, bf16[4,384,384]{2,1,0:T(8,128)(2,1)}, u32[]{:S(2)}) copy-start(bf16[4,384,384]{2,1,0:T(8,128)(2,1)} %param.24) | copy-start | bytes 3538948
  0.7 9.8 %copy-start.37 = (bf16[2,6,384]{2,0,1:T(2,128)(2,1)S(1)}, bf16[2,6,384]{2,0,1:T(2,128)(2,1)}, u32[]{:S(2)}) copy-start(bf16[2,6,384]{2,0,1:T(2,128)(2,1)} %param.22) | copy-start | bytes 27652
  5.8 6.8 %slice-start.2 = ((bf16[4,384,384]{2,1,0:T(8,128)(2,1)}), bf16[2,384,384]{2,1,0:T(8,128)(2,1)S(1)}, s32[]{:S(2)}) async-start(bf16[4,384,384]{2,1,0:T(8,128)(2,1)} %attn_ref.1), calls=%async_computation.2 | async-start | bytes 1179648 | tf_op jit(solution)/shard_map/slice | solution.py:1054
  7.0 5.6 copy-start.24
  8.4 4.3 copy-start.25
  14.8 3.8 copy-start.13
  14.8 3.8 copy-start.14
  230.5 6.3 %copy-start.41 = (bf16[8,320,384]{2,1,0:T(8,128)(2,1)S(1)}, bf16[8,320,384]{2,1,0:T(8,128)(2,1)}, u32[]{:S(2)}) copy-start(bf16[8,320,384]{2,1,0:T(8,128)(2,1)} %get-tuple-element.140) | copy-start | bytes 5898244
  233.4 27.1 %collective-permute-start.2 = (bf16[5,128,384]{2,1,0:T(8,128)(2,1)}, bf16[5,128,384]{2,1,0:T(8,128)(2,1)S(1)}, u32[]{:S(2)}, u32[]{:S(2)}) collective-permute-start(bf16[5,128,384]{2,1,0:T(8,128)(2,1)} %get-tuple-element.202), channel_id=1, source_target_pairs={{0,24},{8,16},{16,8},{24,0},{1,25},{9,17},{17,9},{25,1},{2,26},{10... | collective-permute-start | bytes 1474568 | tf_op jit(solution)/shard_map/ppermute | solution.py:1191
  234.5 26.0 %collective-permute-start.1 = (bf16[5,128,384]{2,1,0:T(8,128)(2,1)}, bf16[5,128,384]{2,1,0:T(8,128)(2,1)}, u32[]{:S(2)}, u32[]{:S(2)}) collective-permute-start(bf16[5,128,384]{2,1,0:T(8,128)(2,1)} %get-tuple-element.203), channel_id=1, source_target_pairs={{0,16},{8,24},{16,0},{24,8},{1,17},{9,25},{17,1},{25,9},{2,18},{10... | collective-permute-start | bytes 1474568 | tf_op jit(solution)/shard_map/ppermute | solution.py:1191
  236.8 23.7 %collective-permute-start = (bf16[5,128,384]{2,1,0:T(8,128)(2,1)S(1)}, bf16[5,128,384]{2,1,0:T(8,128)(2,1)}, u32[]{:S(2)}, u32[]{:S(2)}) collective-permute-start(bf16[5,128,384]{2,1,0:T(8,128)(2,1)S(1)} %get-tuple-element.204), channel_id=1, source_target_pairs={{0,8},{8,0},{16,24},{24,16},{1,9},{9,1},{17,25},{25,17},{2,10},{10... | collective-permute-start | bytes 1474568 | tf_op jit(solution)/shard_map/ppermute | solution.py:1191
  236.8 6.5 %copy-start.39 = (bf16[8,320,1536]{2,1,0:T(8,128)(2,1)S(1)}, bf16[8,320,1536]{2,1,0:T(8,128)(2,1)}, u32[]{:S(2)}) copy-start(bf16[8,320,1536]{2,1,0:T(8,128)(2,1)} %get-tuple-element.145) | copy-start | bytes 23592964
  236.8 6.5 %copy-start.40 = (bf16[8,320,384]{2,1,0:T(8,128)(2,1)S(1)}, bf16[8,320,384]{2,1,0:T(8,128)(2,1)}, u32[]{:S(2)}) copy-start(bf16[8,320,384]{2,1,0:T(8,128)(2,1)} %get-tuple-element.144) | copy-start | bytes 5898244
  243.3 4.3 copy-start.48
  243.3 4.3 copy-start.49
  247.6 5.4 copy-start.7
  253.0 2.8 copy-start.26
  265.0 57.2 %collective-permute-start.3 = (bf16[5,128,384]{2,1,0:T(8,128)(2,1)S(1)}, bf16[5,128,384]{2,1,0:T(8,128)(2,1)S(1)}, u32[]{:S(2)}, u32[]{:S(2)}) collective-permute-start(bf16[5,128,384]{2,1,0:T(8,128)(2,1)S(1)} %get-tuple-element.193), channel_id=1, source_target_pairs={{0,0},{4,1},{16,2},{20,3},{1,4},{5,5},{17,6},{21,7},{8,8},{12,9},{... | collective-permute-start | bytes 1474568 | tf_op jit(solution)/shard_map/ppermute | solution.py:1246
  272.6 49.6 %collective-permute-start.6 = (bf16[5,128,384]{2,1,0:T(8,128)(2,1)S(1)}, bf16[5,128,384]{2,1,0:T(8,128)(2,1)S(1)}, u32[]{:S(2)}, u32[]{:S(2)}) collective-permute-start(bf16[5,128,384]{2,1,0:T(8,128)(2,1)S(1)} %get-tuple-element.194), channel_id=1, source_target_pairs={{10,0},{14,1},{26,2},{30,3},{11,4},{15,5},{27,6},{31,7},{2,8},{6,9... | collective-permute-start | bytes 1474568 | tf_op jit(solution)/shard_map/ppermute | solution.py:1246
  272.9 49.3 %collective-permute-start.5 = (bf16[5,128,384]{2,1,0:T(8,128)(2,1)S(1)}, bf16[5,128,384]{2,1,0:T(8,128)(2,1)}, u32[]{:S(2)}, u32[]{:S(2)}) collective-permute-start(bf16[5,128,384]{2,1,0:T(8,128)(2,1)S(1)} %get-tuple-element.195), channel_id=1, source_target_pairs={{2,0},{6,1},{18,2},{22,3},{3,4},{7,5},{19,6},{23,7},{10,8},{14,9},... | collective-permute-start | bytes 1474568 | tf_op jit(solution)/shard_map/ppermute | solution.py:1246
  277.2 45.0 %collective-permute-start.4 = (bf16[5,128,384]{2,1,0:T(8,128)(2,1)S(1)}, bf16[5,128,384]{2,1,0:T(8,128)(2,1)}, u32[]{:S(2)}, u32[]{:S(2)}) collective-permute-start(bf16[5,128,384]{2,1,0:T(8,128)(2,1)S(1)} %get-tuple-element.196), channel_id=1, source_target_pairs={{8,0},{12,1},{24,2},{28,3},{9,4},{13,5},{25,6},{29,7},{0,8},{4,9},... | collective-permute-start | bytes 1474568 | tf_op jit(solution)/shard_map/ppermute | solution.py:1246
  316.8 97.3 %collective-permute-start.7 = (bf16[2,512,384]{2,1,0:T(8,128)(2,1)}, bf16[2,512,384]{2,1,0:T(8,128)(2,1)}, u32[]{:S(2)}, u32[]{:S(2)}) collective-permute-start(bf16[2,512,384]{2,1,0:T(8,128)(2,1)} %get-tuple-element.107), channel_id=1, source_target_pairs={{1,0},{0,1},{3,2},{2,3},{5,4},{4,5},{7,6},{6,7},{9,8},{8,9},{11,10... | collective-permute-start | bytes 2359304 | tf_op jit(solution)/shard_map/ppermute | solution.py:1278
  375.8 2.8 copy-start
  378.7 3.2 copy-start.1
  381.9 8.0 %copy-start.5 = (bf16[120,384]{1,0:T(8,128)(2,1)S(1)}, bf16[120,384]{1,0:T(8,128)(2,1)}, u32[]{:S(2)}) copy-start(bf16[120,384]{1,0:T(8,128)(2,1)} %copy-done.4) | copy-start | bytes 276484
  381.9 8.0 %copy-start.18 = (f32[128,384]{1,0:T(8,128)S(1)}, f32[128,384]{1,0:T(8,128)}, u32[]{:S(2)}) copy-start(f32[128,384]{1,0:T(8,128)} %reduce_sum.109) | copy-start | bytes 589828
  381.9 8.0 %copy-start.20 = (f32[128,384]{1,0:T(8,128)S(1)}, f32[128,384]{1,0:T(8,128)}, u32[]{:S(2)}) copy-start(f32[128,384]{1,0:T(8,128)} %reduce_sum.110) | copy-start | bytes 589828
  381.9 9.1 %copy-start.19 = (f32[128,384]{1,0:T(8,128)S(1)}, f32[128,384]{1,0:T(8,128)}, u32[]{:S(2)}) copy-start(f32[128,384]{1,0:T(8,128)} %reduce_sum.113) | copy-start | bytes 589828
  381.9 10.3 %copy-start.9 = (bf16[2,1024,384]{2,1,0:T(8,128)(2,1)S(1)}, bf16[2,1024,384]{2,1,0:T(8,128)(2,1)}, u32[]{:S(2)}) copy-start(bf16[2,1024,384]{2,1,0:T(8,128)(2,1)} %get-tuple-element.117) | copy-start | bytes 4718596
  384.2 64.8 %collective-permute-start.10 = (bf16[3,512,384]{2,1,0:T(8,128)(2,1)}, bf16[3,512,384]{2,1,0:T(8,128)(2,1)}, u32[]{:S(2)}, u32[]{:S(2)}) collective-permute-start(bf16[3,512,384]{2,1,0:T(8,128)(2,1)} %get-tuple-element.112), channel_id=1, source_target_pairs={{1,0},{0,1},{3,2},{2,3},{5,4},{4,5},{7,6},{6,7},{9,8},{8,9},{11,10... | collective-permute-start | bytes 3538952 | tf_op jit(solution)/shard_map/ppermute | solution.py:1278
  400.2 7.8 %slice-start = ((s8[4718592]{0:T(1024)(128)(4,1)}), s8[4194304]{0:T(1024)(128)(4,1)S(1)}, s32[]{:S(2)}) async-start(s8[4718592]{0:T(1024)(128)(4,1)} %bitcast.244), calls=%async_computation | async-start | bytes 8388608
  401.7 6.3 %slice-start.1 = ((s8[4718592]{0:T(1024)(128)(4,1)}), s8[524288]{0:T(1024)(128)(4,1)S(1)}, s32[]{:S(2)}) async-start(s8[4718592]{0:T(1024)(128)(4,1)} %bitcast.244), calls=%async_computation.1 | async-start | bytes 1048576
  401.7 6.3 %copy-start.8 = (bf16[5,512,384]{2,1,0:T(8,128)(2,1)S(1)}, bf16[5,512,384]{2,1,0:T(8,128)(2,1)}, u32[]{:S(2)}) copy-start(bf16[5,512,384]{2,1,0:T(8,128)(2,1)} %get-tuple-element.134) | copy-start | bytes 5898244
  408.1 3.4 copy-start.2
  418.0 15.0 %copy-start.3 = (f32[384,384]{1,0:T(8,128)S(1)}, f32[384,384]{1,0:T(8,128)}, u32[]{:S(2)}) copy-start(f32[384,384]{1,0:T(8,128)} %convolution_bitcast_fusion.13) | copy-start | bytes 1769476
  420.1 20.4 %collective-permute-start.9 = (bf16[2,256,384]{2,1,0:T(8,128)(2,1)}, bf16[2,256,384]{2,1,0:T(8,128)(2,1)}, u32[]{:S(2)}, u32[]{:S(2)}) collective-permute-start(bf16[2,256,384]{2,1,0:T(8,128)(2,1)} %get-tuple-element.213), channel_id=1, source_target_pairs={{2,0},{6,1},{0,2},{4,3},{3,4},{7,5},{1,6},{5,7},{10,8},{14,9},{8,1... | collective-permute-start | bytes 1179656 | tf_op jit(solution)/shard_map/ppermute | solution.py:1285
  431.1 16.4 %collective-permute-start.8 = (bf16[2,256,384]{2,1,0:T(8,128)(2,1)}, bf16[2,256,384]{2,1,0:T(8,128)(2,1)}, u32[]{:S(2)}, u32[]{:S(2)}) collective-permute-start(bf16[2,256,384]{2,1,0:T(8,128)(2,1)} %get-tuple-element.214), channel_id=1, source_target_pairs={{0,0},{4,1},{2,2},{6,3},{1,4},{5,5},{3,6},{7,7},{8,8},{12,9},{10,1... | collective-permute-start | bytes 1179656 | tf_op jit(solution)/shard_map/ppermute | solution.py:1285
  433.0 3.2 copy-start.32
  449.0 6.6 %copy-start.30 = (f32[8,384]{1,0:T(8,128)S(1)}, f32[8,384]{1,0:T(8,128)}, u32[]{:S(2)}) copy-start(f32[8,384]{1,0:T(8,128)} %reduce_sum.115) | copy-start | bytes 36868
  449.0 6.6 %copy-start.31 = (f32[8,384]{1,0:T(8,128)S(1)}, f32[8,384]{1,0:T(8,128)}, u32[]{:S(2)}) copy-start(f32[8,384]{1,0:T(8,128)} %reduce_sum.116) | copy-start | bytes 36868
  449.0 6.6 %copy-start.29 = (f32[8,384]{1,0:T(8,128)S(1)}, f32[8,384]{1,0:T(8,128)}, u32[]{:S(2)}) copy-start(f32[8,384]{1,0:T(8,128)} %reduce_sum.121) | copy-start | bytes 36868
  449.0 6.6 %copy-start.38 = (pred[64]{0:T(512)(128)(4,1)S(1)}, pred[64]{0:T(512)(128)(4,1)}, u32[]{:S(2)}) copy-start(pred[64]{0:T(512)(128)(4,1)} %broadcast_in_dim.49) | copy-start | bytes 196
  564.0 3.4 copy-start.11
  567.4 2.9 copy-start.28
  567.4 3.5 copy-start.34
  567.4 3.5 copy-start.36
  567.6 19.3 %collective-permute-start.12 = (bf16[3,256,384]{2,1,0:T(8,128)(2,1)S(1)}, bf16[3,256,384]{2,1,0:T(8,128)(2,1)S(1)}, u32[]{:S(2)}, u32[]{:S(2)}) collective-permute-start(bf16[3,256,384]{2,1,0:T(8,128)(2,1)S(1)} %get-tuple-element.207), channel_id=1, source_target_pairs={{2,0},{6,1},{0,2},{4,3},{3,4},{7,5},{1,6},{5,7},{10,8},{14,9},{8,1... | collective-permute-start | bytes 1769480 | tf_op jit(solution)/shard_map/ppermute | solution.py:1285
  568.3 26.6 %collective-permute-start.11 = (bf16[3,256,384]{2,1,0:T(8,128)(2,1)S(1)}, bf16[3,256,384]{2,1,0:T(8,128)(2,1)S(1)}, u32[]{:S(2)}, u32[]{:S(2)}) collective-permute-start(bf16[3,256,384]{2,1,0:T(8,128)(2,1)S(1)} %get-tuple-element.208), channel_id=1, source_target_pairs={{0,0},{4,1},{2,2},{6,3},{1,4},{5,5},{3,6},{7,7},{8,8},{12,9},{10,1... | collective-permute-start | bytes 1769480 | tf_op jit(solution)/shard_map/ppermute | solution.py:1285
  (19 other events, 35.0 us)

commit v4 on v3

--- a/solution.py
+++ b/solution.py
@@ -18,9 +18,17 @@
 BF = jnp.bfloat16
 VMEM_BYTES = 60 * 2**20
 SUM_ROWS = 16
-BLOCK = 16
+BLOCK = 32
+STREAM_RUNS = 2
+TIME_LAG = 1
 SUB = 8
 TILE = 16
+TIME_STAGE = 8
+SPACE_STAGE = 1
+BACK_STAGE = 1
+CROSS_AHEAD = 2
+SPAN = 512
+KEY_CHUNK = 256
 PARTS = (7, 5, 4, 3, 2, 1)
 PATTERN = (0, 1, 2, 0, 1, 0, 1)
 
@@ -81,59 +89,114 @@
     return jnp.concatenate([rows, blank] if head % 2 == 0 else [blank, rows], axis=0)
 
 
-def attend(queries, keys, values_t, bias, keep_exponent):
-    ones = jnp.ones((SUM_ROWS, values_t.shape[1]), BF)
-    parts, inverses = [], []
-    for head in range(HEADS):
-        pair = head // 2
-        scores = dot_nt(pair_of(keys, pair), head_lanes(pair_of(queries, pair), head))
+def spans(count, size):
+    return [slice(at, min(at + size, count)) for at in range(0, count, size)]
+
+
+def attend(jobs, ahead, keep_exponent):
+    units = [
+        (i, head, span) for i, job in enumerate(jobs) for head in range(HEADS) for span in spans(job[0].shape[0], SPAN)
+    ]
+    scores, tops, sums, inverses = {}, {}, {}, {}
+
+    def score(unit, keys_span):
+        i, head, span = unit
+        queries, keys, _, bias = jobs[i]
+        lone = head_lanes(pair_of(queries, head // 2)[span], head)
+        value = dot_nt(pair_of(keys, head // 2)[keys_span], lone)
         if bias is not None:
-            scores = scores + bias
-        largest = jnp.max(scores, axis=0, keepdims=True)
-        exponent = jnp.exp(scores - largest).astype(BF)
-        keep_exponent(head, exponent)
-        lifted = jnp.concatenate([head_rows(values_t, head), ones], axis=0)
-        summed = dot(lifted, exponent)
-        inverse = 1.0 / summed[HDIM : HDIM + 1, :]
-        parts.append(summed[:HDIM, :] * inverse)
-        inverses.append(inverse)
-    return jnp.concatenate(parts, axis=0), inverses
-
-
-def attend_back(exponent_of, queries_of, keys_t_of, values_of, d_att_t, att_t, inverse_of, keys_chunk):
-    n_keys, chunk = keys_chunk
-    d_query_parts, d_key_pairs, d_value_pairs = [], [], []
-    for pair in range(PAIRS):
-        d_keys = [None] * (n_keys // chunk)
-        d_values = [None] * (n_keys // chunk)
-        for head in (2 * pair, 2 * pair + 1):
+            value = value + bias[keys_span, span]
+        scores.setdefault((i, head, span.start), []).append(value)
+        top = jnp.max(value, axis=0, keepdims=True)
+        old = tops.get((i, head, span.start))
+        tops[i, head, span.start] = top if old is None else jnp.maximum(old, top)
+
+    def weigh(unit, index, keys_span):
+        i, head, span = unit
+        name = (i, head, span.start)
+        exponent = jnp.exp(scores[name][index] - tops[name]).astype(BF)
+        scores[name][index] = None
+        keep_exponent(i, head, keys_span, span, exponent)
+        values_t = jobs[i][2]
+        count = keys_span.stop - keys_span.start
+        lifted = jnp.concatenate([head_rows(values_t, head)[:, keys_span], jnp.ones((SUM_ROWS, count), BF)], axis=0)
+        part = dot(lifted, exponent)
+        sums[name] = part if name not in sums else sums[name] + part
+
+    def finish(unit):
+        i, head, span = unit
+        name = (i, head, span.start)
+        total = sums[name]
+        inverse = 1.0 / total[HDIM : HDIM + 1, :]
+        sums[name] = total[:HDIM, :] * inverse
+        inverses[name] = inverse
+
+    for turn in range(len(units) + ahead):
+        later = units[turn] if turn < len(units) else None
+        now = units[turn - ahead] if turn >= ahead else None
+        later_spans = spans(jobs[later[0]][1].shape[0], SPAN) if later else []
+        now_spans = spans(jobs[now[0]][1].shape[0], SPAN) if now else []
+        for index in range(max(len(later_spans), len(now_spans))):
+            if index < len(later_spans):
+                score(later, later_spans[index])
+            if index < len(now_spans):
+                weigh(now, index, now_spans[index])
+        if now:
+            finish(now)
+
+    def joined(parts, i, head):
+        starts = [span.start for span in spans(jobs[i][0].shape[0], SPAN)]
+        return jnp.concatenate([parts[i, head, start] for start in starts], axis=1)
+
+    return (
+        [jnp.concatenate([joined(sums, i, head) for head in range(HEADS)], axis=0) for i in range(len(jobs))],
+        [[joined(inverses, i, head) for head in range(HEADS)] for i in range(len(jobs))],
+    )
+
+
+def added(total, part):
+    return part if total is None else total + part
+
+
+def attend_back(jobs, ahead, chunk):
+    scaled, centres = {}, {}
+    for i, (_, _, _, _, d_att_t, att_t, inverse_of, _) in enumerate(jobs):
+        for head in range(HEADS):
             inverse = inverse_of(head)
             d_att_head = head_rows(d_att_t, head)
-            centre = row_sums(d_att_head * head_rows(att_t, head)) * inverse
-            scaled = (d_att_head * inverse).astype(BF)
-            blank = jnp.zeros_like(scaled)
-            scaled_pair = jnp.concatenate([scaled, blank] if head % 2 == 0 else [blank, scaled], axis=0)
-            query_pair = head_lanes(queries_of(pair), head)
-            d_query = None
-            for at in range(n_keys // chunk):
-                rows = slice(at * chunk, (at + 1) * chunk)
-                exponent = exponent_of(head, rows)
-                d_chance = dot(values_of(pair, rows), scaled_pair)
-                d_score = (exponent.astype(F32) * (d_chance - centre)).astype(BF)
-                d_value = dot_nt(exponent, scaled_pair)
-                d_key = dot(d_score, query_pair)
-                part = dot(keys_t_of(head, rows), d_score)
-                d_query = part if d_query is None else d_query + part
-                d_keys[at] = d_key if d_keys[at] is None else d_keys[at] + d_key
-                d_values[at] = d_value if d_values[at] is None else d_values[at] + d_value
-            d_query_parts.append(d_query)
-        d_key_pairs.append(jnp.concatenate(d_keys, axis=0))
-        d_value_pairs.append(jnp.concatenate(d_values, axis=0))
-    return (
-        jnp.concatenate(d_query_parts, axis=0),
-        jnp.concatenate(d_key_pairs, axis=1),
-        jnp.concatenate(d_value_pairs, axis=1),
-    )
+            centres[i, head] = row_sums(d_att_head * head_rows(att_t, head)) * inverse
+            part = (d_att_head * inverse).astype(BF)
+            blank = jnp.zeros_like(part)
+            scaled[i, head] = jnp.concatenate([part, blank] if head % 2 == 0 else [blank, part], axis=0)
+    units = [
+        (i, head, rows) for i, job in enumerate(jobs) for head in range(HEADS) for rows in spans(job[7], chunk)
+    ]
+    d_queries, d_keys, d_values, chances = {}, {}, {}, {}
+    for turn in range(len(units) + ahead):
+        if turn < len(units):
+            i, head, rows = units[turn]
+            chances[turn] = dot(jobs[i][3](head // 2, rows), scaled[i, head])
+        if turn < ahead:
+            continue
+        i, head, rows = units[turn - ahead]
+        key = (i, head // 2, rows.start)
+        exponent = jobs[i][0](head, rows)
+        chance = chances.pop(turn - ahead)
+        d_values[key] = added(d_values.get(key), dot_nt(exponent, scaled[i, head]))
+        score = (exponent.astype(F32) * (chance - centres[i, head])).astype(BF)
+        d_keys[key] = added(d_keys.get(key), dot(score, head_lanes(jobs[i][1](head // 2), head)))
+        d_queries[i, head] = added(d_queries.get((i, head)), dot(jobs[i][2](head, rows), score))
+    results = []
+    for i, job in enumerate(jobs):
+        starts = [rows.start for rows in spans(job[7], chunk)]
+        joined = [
+            jnp.concatenate(
+                [jnp.concatenate([parts[i, pair, at] for at in starts], axis=0) for pair in range(PAIRS)], axis=1
+            )
+            for parts in (d_keys, d_values)
+        ]
+        results.append((jnp.concatenate([d_queries[i, head] for head in range(HEADS)], axis=0), *joined))
+    return results
 
 
 def fold(ref):
@@ -346,16 +409,11 @@
         targets = [lay.space_target(me, j) for j in range(lay.clips_dev)]
         targets += [lay.time_target(me, j, s) for j in range(lay.clips_dev) for s in range(lay.halves)]
         await_greetings(me, targets + friends)
-        start_latents(0)
-        if frames > 1:
-            start_latents(1)
+        for f in range(frames):
+            start_latents(f)
         pass_on(0)
 
-    @pl.when(step + 2 < frames)
-    def _():
-        start_latents(step + 2)
-
-    @pl.when(step == min(1, frames - 1))
+    @pl.when(step == min(2, frames - 1))
     def _():
         for j in range(lay.clips_dev):
             for s in range(lay.halves):
@@ -383,10 +441,10 @@
     keys_t_ref[0] = dot_nt(turned_ref[0], normed).astype(BF)
     values_t = dot_nt(turned_ref[1], normed).astype(BF)
 
-    def keep_exponent(head, exponent):
-        exponent_ref[0, head] = exponent
-
-    att_t, inverses = attend(queries, keys, values_t, None, keep_exponent)
+    def keep_exponent(_, head, keys_span, span, exponent):
+        exponent_ref[0, head, keys_span, span] = exponent
+
+    (att_t,), (inverses,) = attend([(queries, keys, values_t, None)], SPACE_STAGE, keep_exponent)
     for head in range(HEADS):
         inverse_ref[0, head : head + 1, :] = inverses[head]
     att_t_ref[0] = att_t.astype(BF)
@@ -407,10 +465,12 @@
     text_id = lax.broadcasted_iota(jnp.int32, (text_keys_ref.shape[0], rows), 0)
     bias = jnp.where(text_id < counts_ref[1], 0.0, MASKED_SCORE)
 
-    def keep_cross(head, exponent):
-        cross_exponent_ref[0, head] = exponent
-
-    cross_t, inverses = attend(cross_queries, text_keys_ref[...], text_values_t_ref[...], bias, keep_cross)
+    def keep_cross(_, head, keys_span, span, exponent):
+        cross_exponent_ref[0, head, keys_span, span] = exponent
+
+    (cross_t,), (inverses,) = attend(
+        [(cross_queries, text_keys_ref[...], text_values_t_ref[...], bias)], CROSS_AHEAD, keep_cross
+    )
     for head in range(HEADS):
         cross_inverse_ref[0, head : head + 1, :] = inverses[head]
     cross_att_t_ref[0] = cross_t.astype(BF)
@@ -512,7 +572,7 @@
     kept = (keep * grad).astype(BF)
     kept2_ref[0] = kept
     d_att_t = dot_nt(cross_ref[1], kept)
-    d_query_t, d_keys, d_values = attend_back(
+    job = (
         lambda head, at: cross_exponent_ref[0, head, at, :],
         lambda pair: cross_query_ref[0, :, pair * LANES : (pair + 1) * LANES],
         lambda head, at: text_keys_t_ref[head * HDIM : (head + 1) * HDIM, at],
@@ -520,8 +580,9 @@
         d_att_t,
         cross_att_t_ref[0].astype(F32),
         lambda head: cross_inverse_ref[0, head : head + 1, :],
-        (text_values_ref.shape[0], text_values_ref.shape[0]),
+        text_values_ref.shape[0],
     )
+    ((d_query_t, d_keys, d_values),) = attend_back([job], CROSS_AHEAD, KEY_CHUNK)
     d_text_keys_ref[0] = d_keys
     d_text_values_ref[0] = d_values
     d_query = (d_query_t.T * scale_by).astype(BF)
@@ -537,8 +598,7 @@
     d_branch = (kept * mod[2:3]).astype(BF)
     kept1_ref[0] = d_branch
     d_att_t = dot_nt(attn_ref[3], d_branch)
-    n_keys = value_ref.shape[1]
-    d_query_t, d_keys, d_values = attend_back(
+    job = (
         lambda head, at: exponent_ref[0, head, at, :],
         lambda pair: query_ref[0, :, pair * LANES : (pair + 1) * LANES],
         lambda head, at: keys_t_ref[0, head * HDIM : (head + 1) * HDIM, at],
@@ -546,8 +606,9 @@
         d_att_t,
         att_t_ref[0].astype(F32),
         lambda head: inverse_ref[0, head : head + 1, :],
-        (n_keys, min(n_keys, 256)),
+        value_ref.shape[1],
     )
+    ((d_query_t, d_keys, d_values),) = attend_back([job], BACK_STAGE, KEY_CHUNK)
     d_query = (d_query_t.T * scale_by).astype(BF)
     d_keys, d_values = d_keys.astype(BF), d_values.astype(BF)
     d_query_ref[0] = d_query
@@ -571,14 +632,27 @@
     )
 
 
+def interleave(streams, lag):
+    live, turn = list(enumerate(streams)), 0
+    while live:
+        left = []
+        for i, stream in live:
+            if turn < i * lag or next(stream, DONE) is not DONE:
+                left.append((i, stream))
+        live, turn = left, turn + 1
+
+
+DONE = object()
+
+
 def time_kernel(
     counts_ref,
     state_ref,
     cot_ref,
     mod_ref,
     bias_ref,
-    attn_ref,
-    turned_ref,
+    qkv_ref,
+    proj_ref,
     up_ref,
     down_ref,
     out_ref,
@@ -597,109 +671,131 @@
     scale_by = HDIM ** (-0.5)
     frames, block, width = state_ref.shape
     run_rows = frames * SUB
-    runs = block // SUB
+    runs = min(STREAM_RUNS, block // SUB)
     mod = mod_ref[...]
-
-    def load(ref):
-        cube = ref[...].astype(F32)
-        parts = [cube[:, r * SUB : (r + 1) * SUB].reshape(run_rows, width) for r in range(runs)]
-        return jnp.concatenate(parts, axis=0)
-
-    def store(ref, value):
-        parts = [value[r * run_rows : (r + 1) * run_rows].reshape(frames, SUB, width) for r in range(runs)]
-        ref[...] = jnp.concatenate(parts, axis=1).astype(ref.dtype)
-
-    def run_of(value, r):
-        return value[r * run_rows : (r + 1) * run_rows]
-
-    state = load(state_ref)
-    rows = state.shape[0]
-    frame = (lax.broadcasted_iota(jnp.int32, (rows, 1), 0) // SUB) % frames
-    keep = (frame < counts_ref[0]).astype(F32)
-    hat1, inverse1 = norm_parts(state)
-    normed = (hat1 * (1.0 + mod[1:2]) + mod[0:1]).astype(BF)
-    normed_ref[0] = normed
-    queries = (dot(normed, attn_ref[0]).astype(BF) * scale_by).astype(BF)
-    keys = dot(normed, attn_ref[1]).astype(BF)
-    values = dot(normed, attn_ref[2]).astype(BF)
-    att_parts, att_t_parts, inverse_parts, keys_t_parts = [], [], [], []
-    for r in range(runs):
-        normed_run = run_of(normed, r)
-        keys_t_parts.append(dot_nt(turned_ref[0], normed_run).astype(BF))
-        values_t = dot_nt(turned_ref[1], normed_run).astype(BF)
-
-        def keep_exponent(head, exponent):
-            exponent_ref[r, head] = exponent
-
-        att_t, inverses = attend(
-            run_of(queries, r), run_of(keys, r), values_t, bias_ref[...], keep_exponent
-        )
-        att_t_parts.append(att_t)
-        inverse_parts.append(inverses)
-        att_parts.append(att_t.T.astype(BF))
-    att = jnp.concatenate(att_parts, axis=0)
-    att_ref[0] = att
-    branch2 = dot(att, attn_ref[3])
-    state = state + (keep * mod[2:3]) * branch2
-    hat2, inverse2 = norm_parts(state)
-    normed2 = (hat2 * (1.0 + mod[4:5]) + mod[3:4]).astype(BF)
-    normed2_ref[0] = normed2
-    act, slope = gelu_parts(dot(normed2, up_ref[...]))
-    act = act.astype(BF)
-    act_ref[0] = act
-    branch5 = dot(act, down_ref[...])
-    store(out_ref, state + (keep * mod[5:6]) * branch5)
-    grad = load(cot_ref)
-    kept = keep * grad
-    d_gate5 = row_sums(kept * branch5)
-    d_branch = (kept * mod[5:6]).astype(BF)
-    branch5_ref[0] = d_branch
-    d_act = dot_nt(d_branch, down_ref[...])
-    d_lifted = (d_act * slope).astype(BF)
-    d_lifted_ref[0] = d_lifted
-    d_normed2 = dot_nt(d_lifted, up_ref[...])
-    grad = grad + norm_back(d_normed2, hat2, inverse2, mod[4:5])
-    kept = keep * grad
-    d_gate2 = row_sums(kept * branch2)
-    d_branch = (kept * mod[2:3]).astype(BF)
-    branch4_ref[0] = d_branch
-    d_query_parts, d_key_parts, d_value_parts = [], [], []
-    for r in range(runs):
-        d_att_t = dot_nt(attn_ref[3], run_of(d_branch, r))
-        query_run, value_run = run_of(queries, r), run_of(values, r)
-        d_query_t, d_keys, d_values = attend_back(
-            lambda head, at: exponent_ref[r, head, at, :],
-            lambda pair: pair_of(query_run, pair),
-            lambda head, at: head_rows(keys_t_parts[r], head)[:, at],
-            lambda pair, at: pair_of(value_run, pair)[at],
-            d_att_t,
-            att_t_parts[r],
-            lambda head: inverse_parts[r][head],
-            (run_rows, run_rows),
-        )
-        d_query_parts.append((d_query_t.T * scale_by).astype(BF))
-        d_key_parts.append(d_keys.astype(BF))
-        d_value_parts.append(d_values.astype(BF))
-    d_qkv = [jnp.concatenate(parts, axis=0) for parts in (d_query_parts, d_key_parts, d_value_parts)]
-    d_normed1 = None
-    for i in range(3):
-        d_qkv_ref[0, :, i * width : (i + 1) * width] = d_qkv[i]
-        part = dot_nt(d_qkv[i], attn_ref[i])
-        d_normed1 = part if d_normed1 is None else d_normed1 + part
-    grad = grad + norm_back(d_normed1, hat1, inverse1, mod[1:2])
-    store(grad_ref, grad)
-    mods_ref[0] = jnp.concatenate(
-        [
-            row_sums(d_normed1),
-            row_sums(d_normed1 * hat1),
-            d_gate2,
-            row_sums(d_normed2),
-            row_sums(d_normed2 * hat2),
-            d_gate5,
-            jnp.zeros((2, width), F32),
-        ],
-        axis=0,
-    )
+    totals = []
+
+    def stream(first_run):
+        patches = slice(first_run * SUB, (first_run + runs) * SUB)
+        mine = slice(first_run * run_rows, (first_run + runs) * run_rows)
+
+        def load(ref):
+            cube = ref[:, patches, :].astype(F32)
+            parts = [cube[:, r * SUB : (r + 1) * SUB].reshape(run_rows, width) for r in range(runs)]
+            return jnp.concatenate(parts, axis=0)
+
+        def store(ref, value):
+            parts = [value[r * run_rows : (r + 1) * run_rows].reshape(frames, SUB, width) for r in range(runs)]
+            ref[:, patches, :] = jnp.concatenate(parts, axis=1).astype(ref.dtype)
+
+        def run_of(value, r):
+            return value[r * run_rows : (r + 1) * run_rows]
+
+        state = load(state_ref)
+        frame = (lax.broadcasted_iota(jnp.int32, (runs * run_rows, 1), 0) // SUB) % frames
+        keep = (frame < counts_ref[0]).astype(F32)
+        hat1, inverse1 = norm_parts(state)
+        normed = (hat1 * (1.0 + mod[1:2]) + mod[0:1]).astype(BF)
+        normed_ref[0, mine] = normed
+        yield
+        qkv = dot(normed, qkv_ref[...])
+        queries = (qkv[:, :width].astype(BF) * scale_by).astype(BF)
+        keys = qkv[:, width : 2 * width].astype(BF)
+        values = qkv[:, 2 * width :].astype(BF)
+        yield
+        keys_t_runs, jobs = [], []
+        for r in range(runs):
+            keys_t_runs.append(run_of(keys, r).T)
+            jobs.append((run_of(queries, r), run_of(keys, r), run_of(values, r).T, bias_ref[...]))
+
+        def keep_exponent(r, head, keys_span, span, exponent):
+            exponent_ref[first_run + r, head, keys_span, span] = exponent
+
+        att_t_runs, inverse_runs = attend(jobs, TIME_STAGE, keep_exponent)
+        yield
+        att = jnp.concatenate([att_t.T.astype(BF) for att_t in att_t_runs], axis=0)
+        att_ref[0, mine] = att
+        branch2 = dot(att, proj_ref[...])
+        yield
+        state = state + (keep * mod[2:3]) * branch2
+        hat2, inverse2 = norm_parts(state)
+        normed2 = (hat2 * (1.0 + mod[4:5]) + mod[3:4]).astype(BF)
+        normed2_ref[0, mine] = normed2
+        yield
+        lifted = dot(normed2, up_ref[...])
+        yield
+        act, slope = gelu_parts(lifted)
+        act = act.astype(BF)
+        act_ref[0, mine] = act
+        grad = load(cot_ref)
+        kept = keep * grad
+        d_branch = (kept * mod[5:6]).astype(BF)
+        branch5_ref[0, mine] = d_branch
+        yield
+        d_act = dot_nt(d_branch, down_ref[...])
+        yield
+        d_lifted = (d_act * slope).astype(BF)
+        d_lifted_ref[0, mine] = d_lifted
+        branch5 = dot(act, down_ref[...])
+        yield
+        store(out_ref, state + (keep * mod[5:6]) * branch5)
+        d_gate5 = row_sums(kept * branch5)
+        d_normed2 = dot_nt(d_lifted, up_ref[...])
+        yield
+        grad = grad + norm_back(d_normed2, hat2, inverse2, mod[4:5])
+        kept = keep * grad
+        d_gate2 = row_sums(kept * branch2)
+        d_branch = (kept * mod[2:3]).astype(BF)
+        branch4_ref[0, mine] = d_branch
+        yield
+        d_att_t_runs = [dot_nt(proj_ref[...], run_of(d_branch, r)) for r in range(runs)]
+        yield
+
+        def job(r):
+            query_run, value_run = run_of(queries, r), run_of(values, r)
+            return (
+                lambda head, at: exponent_ref[first_run + r, head, at, :],
+                lambda pair: pair_of(query_run, pair),
+                lambda head, at: head_rows(keys_t_runs[r], head)[:, at],
+                lambda pair, at: pair_of(value_run, pair)[at],
+                d_att_t_runs[r],
+                att_t_runs[r],
+                lambda head: inverse_runs[r][head],
+                run_rows,
+            )
+
+        backs = attend_back([job(r) for r in range(runs)], TIME_STAGE, run_rows)
+        yield
+        d_qkv = jnp.concatenate(
+            [
+                jnp.concatenate([(d_query_t.T * scale_by).astype(BF) for d_query_t, _, _ in backs], axis=0),
+                jnp.concatenate([d_keys.astype(BF) for _, d_keys, _ in backs], axis=0),
+                jnp.concatenate([d_values.astype(BF) for _, _, d_values in backs], axis=0),
+            ],
+            axis=1,
+        )
+        d_qkv_ref[0, mine] = d_qkv
+        d_normed1 = dot_nt(d_qkv, qkv_ref[...])
+        yield
+        grad = grad + norm_back(d_normed1, hat1, inverse1, mod[1:2])
+        store(grad_ref, grad)
+        totals.append(
+            jnp.concatenate(
+                [
+                    row_sums(d_normed1),
+                    row_sums(d_normed1 * hat1),
+                    d_gate2,
+                    row_sums(d_normed2),
+                    row_sums(d_normed2 * hat2),
+                    d_gate5,
+                    jnp.zeros((2, width), F32),
+                ],
+                axis=0,
+            )
+        )
+
+    interleave([stream(first) for first in range(0, block // SUB, runs)], TIME_LAG)
+    mods_ref[0] = sum(totals[1:], totals[0])
 
 
 class Reducer:
@@ -1051,7 +1147,6 @@
         text_values = dot(text_wide, cross_attn[2]).astype(BF)
         cross_ends = jnp.stack([cross_attn[0], cross_attn[3]])
         patch_turned = jnp.swapaxes(patch_attn[1:3], 1, 2)
-        frame_turned = jnp.swapaxes(frame_attn[1:3], 1, 2)
 
         def out(*shape, dtype=BF):
             return shape_of((frames,) + shape, dtype)
@@ -1205,7 +1300,8 @@
         def tokens(features):
             return shape_of((n_blocks, block_rows, features), BF)
 
-        time_inputs = (counts, state, cot, frame_mod, bias, frame_attn, frame_turned, frame_up, frame_down)
+        frame_wide = frame_attn[:3].swapaxes(0, 1).reshape(width, 3 * width)
+        time_inputs = (counts, state, cot, frame_mod, bias, frame_wide, frame_attn[3], frame_up, frame_down)
         time_outputs = (
             shape_of((all_frames, time_patches, width), BF),
             shape_of((all_frames, time_patches, width), BF),

time: 602 us -> 553 us (0.919)
  Pallas kernels: 403 us -> 345 us
  local copies, waits for them, and re-layouts: 24.5 us -> 31.2 us
    pallas_call x6, Pallas kernels: 297 us -> 239 us  [call(): pl.pallas_call(kernel, grid=grid, in_specs=in_specs, out_specs=out_specs,...]
    ppermute x4, starting transfers between devices: 15.1 us -> 23.8 us  [per_device(): out_parts.append(lax.ppermute(sent, whole_axes, back(time_pairs(step))))]
  transfers between devices with their start and end apart: 13 -> 13, of which waited for: 3 -> 3; matrix products, arithmetic and copies ran while one was open for 16% -> 18% of each run, Pallas kernels for 14% -> 15%
where the time goes in v4:
time: 553 us; the launch traced here: 549 us
  Pallas kernels  345 us (62%)
  matrix products  66.5 us (12%)
  starting transfers between devices  41.2 us (7%)
  other arithmetic  38.7 us (7%)
  local copies, waits for them, and re-layouts  31.2 us (6%)
  waiting for transfers between devices  20.3 us (4%)
    pallas_call x6, Pallas kernels, call(): pl.pallas_call(kernel, grid=grid, in_specs=in_specs, out_specs=out_specs,...  239 us
    pallas_call x1, Pallas kernels, reduce_all(): pl.pallas_call(kernel, in_specs=[any_spec] * n + [vmem_spec], out_specs=[...  107 us
    dot_general x16, matrix products, grad_over(): lax.dot_general(left, right, (((0,), (0,)), ((), ())), preferred_element_...  36.8 us
    ppermute x4, starting transfers between devices, per_device(): out_parts.append(lax.ppermute(sent, whole_axes, back(time_pairs(step))))  23.8 us
    dot_general x4, matrix products, weight_grad(): lax.dot_general(left, right, (((0,), (0,)), ((), ())), preferred_element_...  20.3 us
    ppermute x4, waiting for transfers between devices, per_device(): got.append(lax.ppermute(sent, pair_axes, back(space_pairs(step))))  20.3 us
    ppermute x4, starting transfers between devices, per_device(): got.append(lax.ppermute(sent, pair_axes, back(space_pairs(step))))  11.5 us
  transfers between devices with their start and end apart: 13, of which 3 were waited for; matrix products, arithmetic and copies ran while one was open for 18% of the time, Pallas kernels for 15%

profile of v4, /device:TPU:1, one launch (start us, length us, event | category | flops | bytes accessed | tf_op | source)
XLA Modules:
  0.0 549.0 jit_solution(15677544866277748074)
XLA Ops:
  1.7 1.8 all-gather
  3.6 2.3 all_gather.7
  14.4 2.3 copy.135
  23.6 1.9 pad_add_fusion.1.refs_0_.counts_ref
  25.5 99.2 %shard_map.230 = (bf16[20,128,384]{2,1,0:T(8,128)(2,1)}, bf16[20,128,384]{2,1,0:T(8,128)(2,1)}, bf16[5,512,384]{2,1,0:T(8,128)(2,1)}, bf16[5,1024,384]{2,1,0:T(8...) custom-call(s32[4]{0:T(128)} %pad_add_fusion.1.refs_0_.counts_ref, ...), custom_call_target="tpu_custom_call" | custom-call | flops 32715571200 | bytes 101429264 | tf_op jit(solution)/shard_map/pallas_call | solution.py:1038
  124.7 53.9 %shard_map.231 = (bf16[20,128,384]{2,1,0:T(8,128)(2,1)}, bf16[20,128,384]{2,1,0:T(8,128)(2,1)}, bf16[4,640,384]{2,1,0:T(8,128)(2,1)}, bf16[4,640,1152]{2,1,0:T(8...) custom-call(s32[4]{0:T(128)} %pad_add_fusion.1.refs_0_.counts_ref, ...), custom_call_target="tpu_custom_call" | custom-call | flops 27179089920 | bytes 43024400 | tf_op jit(solution)/shard_map/pallas_call | solution.py:1038
  178.6 2.8 constant_dynamic-slice_fusion.5
  181.4 3.1 collective-permute-start.2
  184.8 7.7 %fusion.2.refs_12_ = bf16[384,1536]{1,0:T(8,128)(2,1)} fusion(bf16[4,640,384]{2,1,0:T(8,128)(2,1)S(1)} %copy-done.40, bf16[4,640,1536]{2,1,0:T(8,128)(2,1)} %get-tuple-element.145), kind=kOutput, calls=%fused_computation.9 | convolution fusion | flops 3020488704 | bytes 11010048 | tf_op jit(solution)/shard_map/dot_general | solution.py:1355
  192.6 5.4 fusion.3.refs_13_
  198.0 3.7 fusion.6.refs_10_
  201.7 2.3 slice.191.refs_0_
  204.0 2.4 slice.193.refs_0_
  207.7 3.5 fusion.14.refs_11_
  215.7 12.8 %collective-permute-start.3 = (bf16[5,128,384]{2,1,0:T(8,128)(2,1)S(1)}, bf16[5,128,384]{2,1,0:T(8,128)(2,1)S(1)}, u32[]{:S(2)}, u32[]{:S(2)}) collective-permute-start(bf16[5,128,384]{2,1,0:T(8,128)(2,1)S(1)} %get-tuple-element.193), channel_id=1, source_target_pairs={{0,0},{4,1},{16,2},{20,3},{1,4},{5,5},{17,6},{21,7},{8,8},{12,9},{... | collective-permute-start | bytes 1474568 | tf_op jit(solution)/shard_map/ppermute | solution.py:1342
  228.5 5.4 collective-permute-start.6
  233.9 5.2 collective-permute-start.5
  239.5 32.0 %shard_map.232 = (f32[2,512,384]{2,1,0:T(8,128)}, f32[2,512,384]{2,1,0:T(8,128)}, bf16[2,512,384]{2,1,0:T(8,128)(2,1)}, bf16[2,512,384]{2,1,0:T(8,128)(2,1)}, bf...) custom-call(s32[4]{0:T(128)} %pad_add_fusion.1.refs_0_.counts_ref, ...), custom_call_target="tpu_custom_call" | custom-call | flops 19528679424 | bytes 87101456 | tf_op jit(solution)/shard_map/pallas_call | solution.py:1038
  272.9 1.7 reduce_sum.109
  275.7 5.3 convolution_bitcast_fusion.5
  284.6 44.1 %shard_map.234 = (f32[3,512,384]{2,1,0:T(8,128)}, f32[3,512,384]{2,1,0:T(8,128)}, bf16[3,512,384]{2,1,0:T(8,128)(2,1)}, bf16[3,512,384]{2,1,0:T(8,128)(2,1)}, bf...) custom-call(s32[4]{0:T(128)} %pad_add_fusion.1.refs_0_.counts_ref, ...), custom_call_target="tpu_custom_call" | custom-call | flops 29293019136 | bytes 94978064 | tf_op jit(solution)/shard_map/pallas_call | solution.py:1038
  330.0 1.8 reduce_sum.110
  331.8 1.8 reduce_sum.113
  333.6 2.6 convolution_bitcast_fusion.16
  336.4 3.2 convolution_bitcast_fusion.14
  339.7 2.2 convolution_bitcast_fusion.13
  341.9 2.4 collective-permute-start.10
  346.7 1.7 fusion.19.refs_1_
  356.2 6.3 %fusion.5.refs_9_ = bf16[1536,384]{1,0:T(8,128)(2,1)} fusion(f32[1536,384]{1,0:T(8,128)S(1)} %copy-done.45, bf16[5,512,1536]{2,1,0:T(8,128)(2,1)} %get-tuple-element.137, bf16[3,512,384]{2,1,0:T(8,128)(2,1)S(1)} %copy-done.47), kind=kOutput, calls=%fused_computation.12 | convolution fusion | flops 1813118976 | bytes 12582912 | tf_op jit(solution)/shard_map/dot_general | solution.py:1402
  362.5 2.0 convolution_bitcast_fusion.6
  365.9 2.7 fusion.4.refs_8_
  368.6 3.8 shard_map.233
  372.4 2.1 dynamic-slice_bitcast_fusion.13
  374.6 5.7 %collective-permute-start.9 = (bf16[2,256,384]{2,1,0:T(8,128)(2,1)}, bf16[2,256,384]{2,1,0:T(8,128)(2,1)}, u32[]{:S(2)}, u32[]{:S(2)}) collective-permute-start(bf16[2,256,384]{2,1,0:T(8,128)(2,1)} %get-tuple-element.213), channel_id=1, source_target_pairs={{2,0},{6,1},{0,2},{4,3},{3,4},{7,5},{1,6},{5,7},{10,8},{14,9},{8,1... | collective-permute-start | bytes 1179656 | tf_op jit(solution)/shard_map/ppermute | solution.py:1381
  380.3 2.1 collective-permute-start.8
  382.4 3.1 fusion.18.refs_2_
  385.5 4.2 collective-permute-done.9
  389.7 9.1 %collective-permute-done.8 = bf16[2,256,384]{2,1,0:T(8,128)(2,1)} collective-permute-done((bf16[2,256,384]{2,1,0:T(8,128)(2,1)}, bf16[2,256,384]{2,1,0:T(8,128)(2,1)}, u32[]{:S(2)}, u32[]{:S(2)}) %collective-permute-start.8) | collective-permute-done | bytes 393248 | tf_op jit(solution)/shard_map/ppermute | solution.py:1381
  400.3 5.7 %shard_map.235 = (bf16[3,2,256,384]{3,2,1,0:T(8,128)(2,1)}, f32[3,8,384]{2,1,0:T(8,128)}) custom-call(bf16[3,512,384]{2,1,0:T(8,128)(2,1)} %slice.193.refs_0_, f32[3,512,384]{2,1,0:T(8,128)} %get-tuple-element.110.refs_1_, f32[3,512,384]{2,1,0:T(8,128)} %get-tuple-element.111.refs_2_, bf16[3,512,384]{2,1,0:T(8,128)(2,1)} %collective-permute-done.10.refs_3_, ...), custom_call_target="tpu_custom_call" | custom-call | flops 17694720 | bytes 8306688 | tf_op jit(solution)/shard_map/pallas_call | solution.py:1038
  407.5 106.7 %shard_map.236 = (bf16[10752,384]{1,0:T(8,128)(2,1)}, f32[64,384]{1,0:T(8,128)}) custom-call(bf16[384,384]{1,0:T(8,128)(2,1)} %fusion.13.refs_0_, bf16[384,384]{1,0:T(8,128)(2,1)} %fusion.19.refs_1_, bf16[384,384]{1,0:T(8,128)(2,1)} %fusion.18.refs_2_, bf16[384,384]{1,0:T(8,128)(2,1)} %fusion.17.refs_3_, bf16[384,384]{1,0:T(8,128)(2,1)} %fusion.16.refs_4_, ...), custom_call_target="tpu_custom_call" | custom-call | flops 33030144 | bytes 16515072 | tf_op jit(solution)/shard_map/pallas_call | solution.py:1004
  515.2 3.3 fusion.47
  518.7 1.8 collective-permute-start.12
  520.5 1.9 collective-permute-start.11
  523.1 3.5 fusion.36
  528.3 1.7 maximum_convert_fusion.5
  534.9 4.1 slice_convert_fusion
  539.0 7.1 %collective-permute-done.11 = bf16[3,256,384]{2,1,0:T(8,128)(2,1)S(1)} collective-permute-done((bf16[3,256,384]{2,1,0:T(8,128)(2,1)S(1)}, bf16[3,256,384]{2,1,0:T(8,128)(2,1)S(1)}, u32[]{:S(2)}, u32[]{:S(2)}) %collective-permute-start.11) | collective-permute-done | bytes 589856 | tf_op jit(solution)/shard_map/ppermute | solution.py:1381
  546.6 2.2 maximum_convert_fusion
  (195 shorter events, 53.7 us)
Async XLA Ops:
  0.6 7.8 %copy-start.14 = (bf16[4,384,384]{2,1,0:T(8,128)(2,1)S(1)}, bf16[4,384,384]{2,1,0:T(8,128)(2,1)}, u32[]{:S(2)}) copy-start(bf16[4,384,384]{2,1,0:T(8,128)(2,1)} %param.24) | copy-start | bytes 3538948
  0.7 8.5 %copy-start.3 = (bf16[4,384,384]{2,1,0:T(8,128)(2,1)S(1)}, bf16[4,384,384]{2,1,0:T(8,128)(2,1)}, u32[]{:S(2)}) copy-start(bf16[4,384,384]{2,1,0:T(8,128)(2,1)} %param.27) | copy-start | bytes 3538948
  7.1 5.5 %copy-start.25 = (bf16[128,384]{1,0:T(8,128)(2,1)}, bf16[128,384]{1,0:T(8,128)(2,1)S(1)}, u32[]{:S(2)}) copy-start(bf16[128,384]{1,0:T(8,128)(2,1)S(1)} %convolution_convert_fusion.2.refs_6_) | copy-start | bytes 294916
  7.1 4.1 copy-start.38
  8.4 4.9 copy-start.26
  9.2 4.1 slice-start.5
  9.9 4.5 slice-start.4
  14.4 3.8 copy-start.12
  18.3 4.4 copy-start.15
  178.6 6.3 %copy-start.40 = (bf16[4,640,384]{2,1,0:T(8,128)(2,1)S(1)}, bf16[4,640,384]{2,1,0:T(8,128)(2,1)}, u32[]{:S(2)}) copy-start(bf16[4,640,384]{2,1,0:T(8,128)(2,1)} %get-tuple-element.144) | copy-start | bytes 5898244
  178.6 14.0 %copy-start.46 = (bf16[4,640,1536]{2,1,0:T(8,128)(2,1)S(1)}, bf16[4,640,1536]{2,1,0:T(8,128)(2,1)}, u32[]{:S(2)}) copy-start(bf16[4,640,1536]{2,1,0:T(8,128)(2,1)} %get-tuple-element.146) | copy-start | bytes 23592964
  178.6 14.0 %copy-start.48 = (bf16[4,640,384]{2,1,0:T(8,128)(2,1)S(1)}, bf16[4,640,384]{2,1,0:T(8,128)(2,1)}, u32[]{:S(2)}) copy-start(bf16[4,640,384]{2,1,0:T(8,128)(2,1)} %get-tuple-element.147) | copy-start | bytes 5898244
  181.4 29.7 %collective-permute-start.2 = (bf16[5,128,384]{2,1,0:T(8,128)(2,1)}, bf16[5,128,384]{2,1,0:T(8,128)(2,1)S(1)}, u32[]{:S(2)}, u32[]{:S(2)}) collective-permute-start(bf16[5,128,384]{2,1,0:T(8,128)(2,1)} %get-tuple-element.202), channel_id=1, source_target_pairs={{0,24},{8,16},{16,8},{24,0},{1,25},{9,17},{17,9},{25,1},{2,26},{10... | collective-permute-start | bytes 1474568 | tf_op jit(solution)/shard_map/ppermute | solution.py:1286
  184.6 26.6 %collective-permute-start.1 = (bf16[5,128,384]{2,1,0:T(8,128)(2,1)}, bf16[5,128,384]{2,1,0:T(8,128)(2,1)}, u32[]{:S(2)}, u32[]{:S(2)}) collective-permute-start(bf16[5,128,384]{2,1,0:T(8,128)(2,1)} %get-tuple-element.203), channel_id=1, source_target_pairs={{0,16},{8,24},{16,0},{24,8},{1,17},{9,25},{17,1},{25,9},{2,18},{10... | collective-permute-start | bytes 1474568 | tf_op jit(solution)/shard_map/ppermute | solution.py:1286
  184.6 26.6 %collective-permute-start = (bf16[5,128,384]{2,1,0:T(8,128)(2,1)S(1)}, bf16[5,128,384]{2,1,0:T(8,128)(2,1)}, u32[]{:S(2)}, u32[]{:S(2)}) collective-permute-start(bf16[5,128,384]{2,1,0:T(8,128)(2,1)S(1)} %get-tuple-element.204), channel_id=1, source_target_pairs={{0,8},{8,0},{16,24},{24,16},{1,9},{9,1},{17,25},{25,17},{2,10},{10... | collective-permute-start | bytes 1474568 | tf_op jit(solution)/shard_map/ppermute | solution.py:1286
  184.8 13.1 %slice-start = ((s8[5898240]{0:T(1024)(128)(4,1)}), s8[4194304]{0:T(1024)(128)(4,1)S(1)}, s32[]{:S(2)}) async-start(s8[5898240]{0:T(1024)(128)(4,1)} %bitcast.247), calls=%async_computation | async-start | bytes 8388608
  192.6 5.4 slice-start.1
  192.6 5.4 copy-start.10
  201.7 5.3 copy-start.29
  201.7 5.9 %copy-start.1 = (bf16[4,640,384]{2,1,0:T(8,128)(2,1)S(1)}, bf16[4,640,384]{2,1,0:T(8,128)(2,1)}, u32[]{:S(2)}) copy-start(bf16[4,640,384]{2,1,0:T(8,128)(2,1)} %get-tuple-element.142) | copy-start | bytes 5898244
  215.7 65.4 %collective-permute-start.3 = (bf16[5,128,384]{2,1,0:T(8,128)(2,1)S(1)}, bf16[5,128,384]{2,1,0:T(8,128)(2,1)S(1)}, u32[]{:S(2)}, u32[]{:S(2)}) collective-permute-start(bf16[5,128,384]{2,1,0:T(8,128)(2,1)S(1)} %get-tuple-element.193), channel_id=1, source_target_pairs={{0,0},{4,1},{16,2},{20,3},{1,4},{5,5},{17,6},{21,7},{8,8},{12,9},{... | collective-permute-start | bytes 1474568 | tf_op jit(solution)/shard_map/ppermute | solution.py:1342
  228.5 52.6 %collective-permute-start.6 = (bf16[5,128,384]{2,1,0:T(8,128)(2,1)S(1)}, bf16[5,128,384]{2,1,0:T(8,128)(2,1)S(1)}, u32[]{:S(2)}, u32[]{:S(2)}) collective-permute-start(bf16[5,128,384]{2,1,0:T(8,128)(2,1)S(1)} %get-tuple-element.194), channel_id=1, source_target_pairs={{10,0},{14,1},{26,2},{30,3},{11,4},{15,5},{27,6},{31,7},{2,8},{6,9... | collective-permute-start | bytes 1474568 | tf_op jit(solution)/shard_map/ppermute | solution.py:1342
  233.9 47.2 %collective-permute-start.5 = (bf16[5,128,384]{2,1,0:T(8,128)(2,1)S(1)}, bf16[5,128,384]{2,1,0:T(8,128)(2,1)}, u32[]{:S(2)}, u32[]{:S(2)}) collective-permute-start(bf16[5,128,384]{2,1,0:T(8,128)(2,1)S(1)} %get-tuple-element.195), channel_id=1, source_target_pairs={{2,0},{6,1},{18,2},{22,3},{3,4},{7,5},{19,6},{23,7},{10,8},{14,9},... | collective-permute-start | bytes 1474568 | tf_op jit(solution)/shard_map/ppermute | solution.py:1342
  239.1 42.0 %collective-permute-start.4 = (bf16[5,128,384]{2,1,0:T(8,128)(2,1)S(1)}, bf16[5,128,384]{2,1,0:T(8,128)(2,1)}, u32[]{:S(2)}, u32[]{:S(2)}) collective-permute-start(bf16[5,128,384]{2,1,0:T(8,128)(2,1)S(1)} %get-tuple-element.196), channel_id=1, source_target_pairs={{8,0},{12,1},{24,2},{28,3},{9,4},{13,5},{25,6},{29,7},{0,8},{4,9},... | collective-permute-start | bytes 1474568 | tf_op jit(solution)/shard_map/ppermute | solution.py:1342
  275.7 92.9 %collective-permute-start.7 = (bf16[2,512,384]{2,1,0:T(8,128)(2,1)}, bf16[2,512,384]{2,1,0:T(8,128)(2,1)}, u32[]{:S(2)}, u32[]{:S(2)}) collective-permute-start(bf16[2,512,384]{2,1,0:T(8,128)(2,1)} %get-tuple-element.107), channel_id=1, source_target_pairs={{1,0},{0,1},{3,2},{2,3},{5,4},{4,5},{7,6},{6,7},{9,8},{8,9},{11,10... | collective-permute-start | bytes 2359304 | tf_op jit(solution)/shard_map/ppermute | solution.py:1374
  339.6 4.7 copy-start.7
  339.7 4.7 copy-start.19
  339.7 4.7 copy-start.21
  339.7 5.9 %copy-start.20 = (f32[128,384]{1,0:T(8,128)S(1)}, f32[128,384]{1,0:T(8,128)}, u32[]{:S(2)}) copy-start(f32[128,384]{1,0:T(8,128)} %reduce_sum.113) | copy-start | bytes 589828
  339.7 7.0 %copy-start.11 = (bf16[2,1024,384]{2,1,0:T(8,128)(2,1)S(1)}, bf16[2,1024,384]{2,1,0:T(8,128)(2,1)}, u32[]{:S(2)}) copy-start(bf16[2,1024,384]{2,1,0:T(8,128)(2,1)} %get-tuple-element.117) | copy-start | bytes 4718596
  341.9 58.3 %collective-permute-start.10 = (bf16[3,512,384]{2,1,0:T(8,128)(2,1)}, bf16[3,512,384]{2,1,0:T(8,128)(2,1)}, u32[]{:S(2)}, u32[]{:S(2)}) collective-permute-start(bf16[3,512,384]{2,1,0:T(8,128)(2,1)} %get-tuple-element.112), channel_id=1, source_target_pairs={{1,0},{0,1},{3,2},{2,3},{5,4},{4,5},{7,6},{6,7},{9,8},{8,9},{11,10... | collective-permute-start | bytes 3538952 | tf_op jit(solution)/shard_map/ppermute | solution.py:1374
  354.7 7.8 %slice-start.2 = ((s8[4718592]{0:T(1024)(128)(4,1)}), s8[4194304]{0:T(1024)(128)(4,1)S(1)}, s32[]{:S(2)}) async-start(s8[4718592]{0:T(1024)(128)(4,1)} %bitcast.250), calls=%async_computation.2 | async-start | bytes 8388608
  356.2 6.3 %slice-start.3 = ((s8[4718592]{0:T(1024)(128)(4,1)}), s8[524288]{0:T(1024)(128)(4,1)S(1)}, s32[]{:S(2)}) async-start(s8[4718592]{0:T(1024)(128)(4,1)} %bitcast.250), calls=%async_computation.3 | async-start | bytes 1048576
  356.2 6.3 %copy-start.9 = (bf16[5,512,384]{2,1,0:T(8,128)(2,1)S(1)}, bf16[5,512,384]{2,1,0:T(8,128)(2,1)}, u32[]{:S(2)}) copy-start(bf16[5,512,384]{2,1,0:T(8,128)(2,1)} %get-tuple-element.134) | copy-start | bytes 5898244
  362.5 3.4 copy-start.4
  372.4 9.9 %copy-start.5 = (f32[384,384]{1,0:T(8,128)S(1)}, f32[384,384]{1,0:T(8,128)}, u32[]{:S(2)}) copy-start(f32[384,384]{1,0:T(8,128)} %convolution_bitcast_fusion.13) | copy-start | bytes 1769476
  374.6 15.1 %collective-permute-start.9 = (bf16[2,256,384]{2,1,0:T(8,128)(2,1)}, bf16[2,256,384]{2,1,0:T(8,128)(2,1)}, u32[]{:S(2)}, u32[]{:S(2)}) collective-permute-start(bf16[2,256,384]{2,1,0:T(8,128)(2,1)} %get-tuple-element.213), channel_id=1, source_target_pairs={{2,0},{6,1},{0,2},{4,3},{3,4},{7,5},{1,6},{5,7},{10,8},{14,9},{8,1... | collective-permute-start | bytes 1179656 | tf_op jit(solution)/shard_map/ppermute | solution.py:1381
  380.3 18.5 %collective-permute-start.8 = (bf16[2,256,384]{2,1,0:T(8,128)(2,1)}, bf16[2,256,384]{2,1,0:T(8,128)(2,1)}, u32[]{:S(2)}, u32[]{:S(2)}) collective-permute-start(bf16[2,256,384]{2,1,0:T(8,128)(2,1)} %get-tuple-element.214), channel_id=1, source_target_pairs={{0,0},{4,1},{2,2},{6,3},{1,4},{5,5},{3,6},{7,7},{8,8},{12,9},{10,1... | collective-permute-start | bytes 1179656 | tf_op jit(solution)/shard_map/ppermute | solution.py:1381
  400.2 6.5 %copy-start.31 = (f32[8,384]{1,0:T(8,128)S(1)}, f32[8,384]{1,0:T(8,128)}, u32[]{:S(2)}) copy-start(f32[8,384]{1,0:T(8,128)} %reduce_sum.115) | copy-start | bytes 36868
  400.2 6.5 %copy-start.32 = (f32[8,384]{1,0:T(8,128)S(1)}, f32[8,384]{1,0:T(8,128)}, u32[]{:S(2)}) copy-start(f32[8,384]{1,0:T(8,128)} %reduce_sum.116) | copy-start | bytes 36868
  400.2 6.5 %copy-start.30 = (f32[8,384]{1,0:T(8,128)S(1)}, f32[8,384]{1,0:T(8,128)}, u32[]{:S(2)}) copy-start(f32[8,384]{1,0:T(8,128)} %reduce_sum.121) | copy-start | bytes 36868
  400.3 6.6 %copy-start.39 = (pred[64]{0:T(512)(128)(4,1)S(1)}, pred[64]{0:T(512)(128)(4,1)}, u32[]{:S(2)}) copy-start(pred[64]{0:T(512)(128)(4,1)} %broadcast_in_dim.49) | copy-start | bytes 196
  515.2 3.4 copy-start.13
  518.6 3.9 copy-start.28
  518.6 4.5 copy-start.35
  518.6 4.5 copy-start.37
  518.7 20.3 %collective-permute-start.12 = (bf16[3,256,384]{2,1,0:T(8,128)(2,1)S(1)}, bf16[3,256,384]{2,1,0:T(8,128)(2,1)S(1)}, u32[]{:S(2)}, u32[]{:S(2)}) collective-permute-start(bf16[3,256,384]{2,1,0:T(8,128)(2,1)S(1)} %get-tuple-element.207), channel_id=1, source_target_pairs={{2,0},{6,1},{0,2},{4,3},{3,4},{7,5},{1,6},{5,7},{10,8},{14,9},{8,1... | collective-permute-start | bytes 1769480 | tf_op jit(solution)/shard_map/ppermute | solution.py:1381
  520.5 25.6 %collective-permute-start.11 = (bf16[3,256,384]{2,1,0:T(8,128)(2,1)S(1)}, bf16[3,256,384]{2,1,0:T(8,128)(2,1)S(1)}, u32[]{:S(2)}, u32[]{:S(2)}) collective-permute-start(bf16[3,256,384]{2,1,0:T(8,128)(2,1)S(1)} %get-tuple-element.208), channel_id=1, source_target_pairs={{0,0},{4,1},{2,2},{6,3},{1,4},{5,5},{3,6},{7,7},{8,8},{12,9},{10,1... | collective-permute-start | bytes 1769480 | tf_op jit(solution)/shard_map/ppermute | solution.py:1381
  (20 other events, 37.7 us)

commit v5 on v4

--- a/solution.py
+++ b/solution.py
@@ -29,7 +29,8 @@
 CROSS_AHEAD = 2
 SPAN = 512
 KEY_CHUNK = 256
-PARTS = (7, 5, 4, 3, 2, 1)
+PARTS = (7, 6, 5, 4, 3, 2)
+HIDDEN_PARTS = (3, 2)
 PATTERN = (0, 1, 2, 0, 1, 0, 1)
 
 
@@ -39,6 +40,10 @@
 
 def dot_nt(a, b):
     return lax.dot_general(a, b, (((1,), (1,)), ((), ())), preferred_element_type=F32)
+
+
+def dot_tn(a, b):
+    return lax.dot_general(a, b, (((0,), (0,)), ((), ())), preferred_element_type=F32)
 
 
 def norm_parts(values):
@@ -160,7 +165,7 @@
 
 def attend_back(jobs, ahead, chunk):
     scaled, centres = {}, {}
-    for i, (_, _, _, _, d_att_t, att_t, inverse_of, _) in enumerate(jobs):
+    for i, (_, _, _, _, d_att_t, att_t, inverse_of, _, _) in enumerate(jobs):
         for head in range(HEADS):
             inverse = inverse_of(head)
             d_att_head = head_rows(d_att_t, head)
@@ -186,6 +191,8 @@
         score = (exponent.astype(F32) * (chance - centres[i, head])).astype(BF)
         d_keys[key] = added(d_keys.get(key), dot(score, head_lanes(jobs[i][1](head // 2), head)))
         d_queries[i, head] = added(d_queries.get((i, head)), dot(jobs[i][2](head, rows), score))
+        if rows.stop == jobs[i][7] and jobs[i][8] is not None:
+            jobs[i][8](head)
     results = []
     for i, job in enumerate(jobs):
         starts = [rows.start for rows in spans(job[7], chunk)]
@@ -265,8 +272,8 @@
         )
 
 
-def await_greetings(me, places):
-    amount = jnp.int32(0)
+def await_greetings(me, places, amount=0):
+    amount = jnp.int32(amount)
     for place in places:
         amount = amount + jnp.logical_not(is_me(me, place)).astype(jnp.int32)
     pl.semaphore_wait(pltpu.get_barrier_semaphore(), amount)
@@ -513,123 +520,196 @@
 
 
 def space_backward_kernel(
-    first_frame,
+    lay,
+    reducer,
     counts_ref,
     grad_ref,
-    mod_ref,
-    attn_ref,
-    cross_ref,
-    text_keys_t_ref,
-    text_values_ref,
-    up_ref,
-    down_ref,
-    query_ref,
-    keys_t_ref,
-    value_ref,
+    out_t_ref,
     exponent_ref,
-    att_t_ref,
-    inverse_ref,
-    cross_query_ref,
-    cross_exponent_ref,
-    cross_att_t_ref,
-    cross_inverse_ref,
-    middle_ref,
-    slope_ref,
-    branch2_ref,
-    branch5_ref,
-    state_grad_ref,
-    own_grad_ref,
-    other_grad_ref,
-    kept3_ref,
-    d_lifted_ref,
-    kept2_ref,
-    d_cross_query_ref,
-    kept1_ref,
-    d_query_ref,
-    d_key_ref,
-    d_value_ref,
-    d_text_keys_ref,
-    d_text_values_ref,
-    mods_ref,
+    *refs,
 ):
+    n_sources = len(reducer.shapes)
+    sources, refs = refs[:n_sources], refs[n_sources:]
+    (mod_ref, attn_ref, cross_ref, text_keys_t_ref, text_values_ref, up_ref, down_ref, own_ref, query_ref, keys_t_ref,
+     value_ref, att_t_ref, inverse_ref, cross_query_ref, cross_exponent_ref, cross_att_t_ref, cross_inverse_ref,
+     middle_ref, slope_ref, branch2_ref, branch5_ref) = refs[:21]
+    (output_ref, lat_grad_ref, reduced_ref, kept3_ref, d_lifted_ref, kept2_ref, d_cross_query_ref, kept1_ref,
+     d_query_ref, d_key_ref, d_value_ref, d_text_keys_ref, d_text_values_ref, mods_ref) = refs[21:35]
+    (exponent_buf, other_buf, fellow_buf, state_buf, own_buf, done_buf, exponent_sem, fellow_send, fellow_recv,
+     out_send, out_recv, grad_send, grad_recv) = refs[35:48]
+    reducer.bind(sources, reduced_ref, refs[48:])
     scale_by = HDIM ** (-0.5)
-    frame = counts_ref[2] + first_frame + pl.program_id(0)
-    keep = (frame < counts_ref[0]).astype(F32)
+    me = lay.here()
+    step = pl.program_id(0)
+    frames = lay.frames
+    rows = lay.space_rows
     mod = mod_ref[...]
-    grad = fold(grad_ref).astype(F32)
-    rows = grad.shape[0]
-    kept = keep * grad
-    d_gate5 = row_sums(kept * branch5_ref[0].astype(F32))
-    d_branch = (kept * mod[5:6]).astype(BF)
-    kept3_ref[0] = d_branch
-    d_act = dot_nt(d_branch, down_ref[...])
-    d_lifted = (d_act * slope_ref[0].astype(F32)).astype(BF)
-    d_lifted_ref[0] = d_lifted
-    d_normed = dot_nt(d_lifted, up_ref[...])
-    hat, inverse = norm_parts(middle_ref[0])
-    grad = grad + norm_back(d_normed, hat, inverse, mod[4:5])
-    d_shift, d_scale = row_sums(d_normed), row_sums(d_normed * hat)
-    kept = (keep * grad).astype(BF)
-    kept2_ref[0] = kept
-    d_att_t = dot_nt(cross_ref[1], kept)
-    job = (
-        lambda head, at: cross_exponent_ref[0, head, at, :],
-        lambda pair: cross_query_ref[0, :, pair * LANES : (pair + 1) * LANES],
-        lambda head, at: text_keys_t_ref[head * HDIM : (head + 1) * HDIM, at],
-        lambda pair, at: text_values_ref[at, pair * LANES : (pair + 1) * LANES],
-        d_att_t,
-        cross_att_t_ref[0].astype(F32),
-        lambda head: cross_inverse_ref[0, head : head + 1, :],
-        text_values_ref.shape[0],
-    )
-    ((d_query_t, d_keys, d_values),) = attend_back([job], CROSS_AHEAD, KEY_CHUNK)
-    d_text_keys_ref[0] = d_keys
-    d_text_values_ref[0] = d_values
-    d_query = (d_query_t.T * scale_by).astype(BF)
-    d_cross_query_ref[0] = d_query
-    grad = grad + dot_nt(d_query, cross_ref[0])
-    state_grad_ref[0] = grad
-    kept = keep * grad
-    d_gate2 = row_sums(kept * branch2_ref[0].astype(F32))
-    mods_ref[0] = jnp.concatenate(
-        [jnp.zeros((2, hat.shape[1]), F32), d_gate2, d_shift, d_scale, d_gate5, jnp.zeros((2, hat.shape[1]), F32)],
-        axis=0,
-    )
-    d_branch = (kept * mod[2:3]).astype(BF)
-    kept1_ref[0] = d_branch
-    d_att_t = dot_nt(attn_ref[3], d_branch)
-    job = (
-        lambda head, at: exponent_ref[0, head, at, :],
-        lambda pair: query_ref[0, :, pair * LANES : (pair + 1) * LANES],
-        lambda head, at: keys_t_ref[0, head * HDIM : (head + 1) * HDIM, at],
-        lambda pair, at: value_ref[0, at, pair * LANES : (pair + 1) * LANES],
-        d_att_t,
-        att_t_ref[0].astype(F32),
-        lambda head: inverse_ref[0, head : head + 1, :],
-        value_ref.shape[1],
-    )
-    ((d_query_t, d_keys, d_values),) = attend_back([job], BACK_STAGE, KEY_CHUNK)
-    d_query = (d_query_t.T * scale_by).astype(BF)
-    d_keys, d_values = d_keys.astype(BF), d_values.astype(BF)
-    d_query_ref[0] = d_query
-    d_key_ref[0] = d_keys
-    d_value_ref[0] = d_values
-    d_normed = dot_nt(d_keys, attn_ref[1]) + dot_nt(d_values, attn_ref[2])
-    own_grad_ref[0] = d_normed[:rows] + dot_nt(d_query, attn_ref[0])
-    other_grad_ref[0] = d_normed[rows:].astype(BF)
-
-
-def space_finish_kernel(n_parts, own_ref, state_grad_ref, own_grad_ref, *rest):
-    parts, (mod_ref, out_ref, mods_ref) = rest[:n_parts], rest[n_parts:]
-    d_normed = own_grad_ref[0]
-    for part in parts:
-        d_normed = d_normed + part[0].astype(F32)
-    hat, inverse = norm_parts(fold(own_ref).astype(F32))
-    grad = state_grad_ref[0] + norm_back(d_normed, hat, inverse, mod_ref[1:2, :])
-    out_ref[...] = grad.astype(BF).reshape(out_ref.shape)
-    mods_ref[0] = jnp.concatenate(
-        [row_sums(d_normed), row_sums(d_normed * hat), jnp.zeros((6, hat.shape[1]), F32)], axis=0
-    )
+
+    def hook(number):
+        for f in range(frames):
+            places = frames * 3 - 1
+            due = [k for k in range(reducer.phases) if 1 + k * places // reducer.phases == f * 3 + number]
+            if f == 0 and number == 0:
+                due = [-1]
+            if due:
+
+                @pl.when(step == f)
+                def _():
+                    for k in due:
+                        reducer.phase(k) if k >= 0 else reducer.prepare()
+
+    def exponent_copy(head, f):
+        return pltpu.make_async_copy(exponent_ref.at[f, head], exponent_buf.at[head], exponent_sem.at[head])
+
+    def fellow_copy(turn, f):
+        return (
+            other_buf.at[f % 2, turn - 1], fellow_buf.at[f, turn - 1], fellow_send.at[turn - 1, f],
+            fellow_recv.at[turn - 1, f], lay.fellow(me, -turn),
+        )
+
+    def out_copy(t):
+        part, j = me["ta"] % lay.halves, lay.clip(me) % lay.clips_dev
+        return (
+            out_t_ref.at[pl.ds(t * frames, frames)], output_ref.at[j, :, part], out_send.at[t],
+            out_recv.at[j, part], lay.owner(me, t, me["ta"] // lay.halves),
+        )
+
+    def grad_copy(slot, f):
+        j = lay.clip(me) % lay.clips_dev
+        return (
+            done_buf.at[f, slot], lat_grad_ref.at[j, f], grad_send.at[slot, f], grad_recv.at[j, f],
+            lay.owner(me, me["ta"], slot),
+        )
+
+    @pl.when(step == 0)
+    def _():
+        for head in range(HEADS):
+            exponent_copy(head, 0).start()
+        fellows = [lay.fellow(me, turn) for turn in range(1, lay.group)]
+        senders = [lay.space_target(me, j) for j in range(lay.clips_dev)]
+        senders += [lay.time_target(me, j, s) for j in range(lay.clips_dev) for s in range(lay.halves)]
+        for place in fellows + senders:
+            greet(me, place)
+        takers = [lay.owner(me, me["ta"], slot) for slot in range(lay.near)]
+        takers += [lay.owner(me, t, me["ta"] // lay.halves) for t in range(lay.n_ta)]
+        await_greetings(me, fellows + takers, reducer.greet())
+        for t in range(lay.n_ta):
+            start_push(me, *out_copy(t))
+
+    mods_ref[0] = jnp.zeros(mods_ref.shape[1:], F32)
+
+    @pl.when(step < frames)
+    def _():
+        hook(0)
+        keep = (counts_ref[2] + step < counts_ref[0]).astype(F32)
+        grad = grad_ref[0].astype(F32)
+        kept = keep * grad
+        d_gate5 = row_sums(kept * branch5_ref[0].astype(F32))
+        d_branch = (kept * mod[5:6]).astype(BF)
+        kept3_ref[0] = d_branch
+        d_act = dot_nt(d_branch, down_ref[...])
+        d_lifted = (d_act * slope_ref[0].astype(F32)).astype(BF)
+        d_lifted_ref[0] = d_lifted
+        d_normed = dot_nt(d_lifted, up_ref[...])
+        hat, inverse = norm_parts(middle_ref[0])
+        grad = grad + norm_back(d_normed, hat, inverse, mod[4:5])
+        d_shift, d_scale = row_sums(d_normed), row_sums(d_normed * hat)
+        kept = (keep * grad).astype(BF)
+        kept2_ref[0] = kept
+        d_att_t = dot_nt(cross_ref[1], kept)
+        job = (
+            lambda head, at: cross_exponent_ref[0, head, at, :],
+            lambda pair: cross_query_ref[0, :, pair * LANES : (pair + 1) * LANES],
+            lambda head, at: text_keys_t_ref[head * HDIM : (head + 1) * HDIM, at],
+            lambda pair, at: text_values_ref[at, pair * LANES : (pair + 1) * LANES],
+            d_att_t,
+            cross_att_t_ref[0].astype(F32),
+            lambda head: cross_inverse_ref[0, head : head + 1, :],
+            text_values_ref.shape[0],
+            None,
+        )
+        ((d_query_t, d_keys, d_values),) = attend_back([job], CROSS_AHEAD, KEY_CHUNK)
+        d_text_keys_ref[0] = d_keys
+        d_text_values_ref[0] = d_values
+        d_query = (d_query_t.T * scale_by).astype(BF)
+        d_cross_query_ref[0] = d_query
+        grad = grad + dot_nt(d_query, cross_ref[0])
+        state_buf[step % 2] = grad
+        kept = keep * grad
+        d_gate2 = row_sums(kept * branch2_ref[0].astype(F32))
+        mods_ref[0, 2:6, :] = jnp.concatenate([d_gate2, d_shift, d_scale, d_gate5], axis=0)
+        d_branch = (kept * mod[2:3]).astype(BF)
+        kept1_ref[0] = d_branch
+        hook(1)
+        d_att_t = dot_nt(attn_ref[3], kept1_ref[0])
+        later = jnp.minimum(step + 1, frames - 1)
+
+        def exponent_of(head, at):
+            if at.start == 0:
+                exponent_copy(head, step).wait()
+            return exponent_buf[head, at, :]
+
+        job = (
+            exponent_of,
+            lambda pair: query_ref[0, :, pair * LANES : (pair + 1) * LANES],
+            lambda head, at: keys_t_ref[0, head * HDIM : (head + 1) * HDIM, at],
+            lambda pair, at: value_ref[0, at, pair * LANES : (pair + 1) * LANES],
+            d_att_t,
+            att_t_ref[0].astype(F32),
+            lambda head: inverse_ref[0, head : head + 1, :],
+            value_ref.shape[1],
+            lambda head: exponent_copy(head, later).start(),
+        )
+        ((d_query_t, d_keys, d_values),) = attend_back([job], BACK_STAGE, KEY_CHUNK)
+        d_query = (d_query_t.T * scale_by).astype(BF)
+        d_keys, d_values = d_keys.astype(BF), d_values.astype(BF)
+        d_query_ref[0] = d_query
+        d_key_ref[0] = d_keys
+        d_value_ref[0] = d_values
+        d_normed = dot_nt(d_keys, attn_ref[1]) + dot_nt(d_values, attn_ref[2])
+        own_buf[step % 2] = d_normed[:rows] + dot_nt(d_query, attn_ref[0])
+
+        @pl.when(step > 1)
+        def _():
+            for turn in range(1, lay.group):
+                push(*fellow_copy(turn, step - 2)).wait_send()
+
+        for turn in range(1, lay.group):
+            other_buf[step % 2, turn - 1] = d_normed[turn * rows : (turn + 1) * rows].astype(BF)
+            push(*fellow_copy(turn, step)).start()
+        hook(2)
+
+    @pl.when(step > 0)
+    def _():
+        f = step - 1
+        d_normed = own_buf[f % 2]
+        for turn in range(1, lay.group):
+            arrived(fellow_buf.at[f, turn - 1], fellow_recv.at[turn - 1, f])
+            d_normed = d_normed + fellow_buf[f, turn - 1].astype(F32)
+        hat, inverse = norm_parts(own_ref[0].astype(F32))
+        grad = state_buf[f % 2] + norm_back(d_normed, hat, inverse, mod[1:2])
+        done_buf[f] = grad.astype(BF).reshape(done_buf.shape[1:])
+        mods_ref[0, 0:2, :] = jnp.concatenate([row_sums(d_normed), row_sums(d_normed * hat)], axis=0)
+        for slot in range(lay.near):
+            start_push(me, *grad_copy(slot, f))
+
+    @pl.when(step == frames)
+    def _():
+        for head in range(HEADS):
+            exponent_copy(head, frames - 1).wait()
+        for turn in range(1, lay.group):
+            for f in range(max(frames - 2, 0), frames):
+                push(*fellow_copy(turn, f)).wait_send()
+        for t in range(lay.n_ta):
+            end_push(me, *out_copy(t))
+        for f in range(frames):
+            for slot in range(lay.near):
+                end_push(me, *grad_copy(slot, f))
+        for j in range(lay.clips_dev):
+            for s in range(lay.halves):
+                arrived(output_ref.at[j, :, s], out_recv.at[j, s])
+            for f in range(frames):
+                arrived(lat_grad_ref.at[j, f], grad_recv.at[j, f])
 
 
 def interleave(streams, lag):
@@ -646,6 +726,7 @@
 
 
 def time_kernel(
+    lay,
     counts_ref,
     state_ref,
     cot_ref,
@@ -655,8 +736,21 @@
     proj_ref,
     up_ref,
     down_ref,
-    out_ref,
-    grad_ref,
+    grad_s_ref,
+    early_ref,
+    late_ref,
+    d_qkv_sum_ref,
+    d_proj_sum_ref,
+    d_up_sum_ref,
+    d_down_sum_ref,
+    mods_ref,
+    exponent_ref,
+    sent_buf,
+    out_buf,
+    d_qkv_sum,
+    d_proj_sum,
+    d_up_sum,
+    d_down_sum,
     normed_ref,
     d_qkv_ref,
     att_ref,
@@ -665,11 +759,52 @@
     act_ref,
     d_lifted_ref,
     branch5_ref,
-    mods_ref,
-    exponent_ref,
+    grad_send,
+    grad_recv,
+    out_send,
+    out_recv,
 ):
+    frames, block, width = state_ref.shape
+    me = lay.here()
+    step = pl.program_id(0)
+    last = pl.num_programs(0) - 1
+
+    def grad_copy(turn, i):
+        place = lay.across(me, turn)
+        row = pl.multiple_of(me["ta"] * lay.time_patches + i * block, TILE)
+        return (
+            sent_buf.at[i, pl.ds(place["ta"] * lay.frames, lay.frames)], grad_s_ref.at[:, pl.ds(row, block)],
+            grad_send.at[turn, i], grad_recv.at[turn, i], place,
+        )
+
+    def out_copy(t, i):
+        part, j = me["ta"] % lay.halves, lay.clip(me) % lay.clips_dev
+        return (
+            out_buf.at[i, pl.ds(t * lay.frames, lay.frames)], early_ref.at[j, :, part, pl.ds(i * block, block)],
+            out_send.at[t, i], out_recv.at[j, part, i], lay.owner(me, t, me["ta"] // lay.halves),
+        )
+
+    early = lay.time_patches // block - 1
+
+    @pl.when(step == 0)
+    def _():
+        friends = [lay.across(me, turn) for turn in range(1, lay.n_ta)]
+        senders, takers = [], []
+        if early:
+            senders = [lay.time_target(me, j, s) for j in range(lay.clips_dev) for s in range(lay.halves)]
+            takers = [lay.owner(me, t, me["ta"] // lay.halves) for t in range(lay.n_ta)]
+        for place in friends + senders:
+            greet(me, place)
+        await_greetings(me, friends + takers)
+        for total in (d_qkv_sum, d_proj_sum, d_up_sum, d_down_sum):
+            total[...] = jnp.zeros_like(total)
+
+    @pl.when(step > 0)
+    def _():
+        for t in range(lay.n_ta):
+            start_push(me, *out_copy(t, step - 1))
+
     scale_by = HDIM ** (-0.5)
-    frames, block, width = state_ref.shape
     run_rows = frames * SUB
     runs = min(STREAM_RUNS, block // SUB)
     mod = mod_ref[...]
@@ -684,9 +819,9 @@
             parts = [cube[:, r * SUB : (r + 1) * SUB].reshape(run_rows, width) for r in range(runs)]
             return jnp.concatenate(parts, axis=0)
 
-        def store(ref, value):
+        def stored(value):
             parts = [value[r * run_rows : (r + 1) * run_rows].reshape(frames, SUB, width) for r in range(runs)]
-            ref[:, patches, :] = jnp.concatenate(parts, axis=1).astype(ref.dtype)
+            return jnp.concatenate(parts, axis=1).astype(BF)
 
         def run_of(value, r):
             return value[r * run_rows : (r + 1) * run_rows]
@@ -696,7 +831,7 @@
         keep = (frame < counts_ref[0]).astype(F32)
         hat1, inverse1 = norm_parts(state)
         normed = (hat1 * (1.0 + mod[1:2]) + mod[0:1]).astype(BF)
-        normed_ref[0, mine] = normed
+        normed_ref[mine] = normed
         yield
         qkv = dot(normed, qkv_ref[...])
         queries = (qkv[:, :width].astype(BF) * scale_by).astype(BF)
@@ -714,31 +849,33 @@
         att_t_runs, inverse_runs = attend(jobs, TIME_STAGE, keep_exponent)
         yield
         att = jnp.concatenate([att_t.T.astype(BF) for att_t in att_t_runs], axis=0)
-        att_ref[0, mine] = att
+        att_ref[mine] = att
         branch2 = dot(att, proj_ref[...])
         yield
         state = state + (keep * mod[2:3]) * branch2
         hat2, inverse2 = norm_parts(state)
         normed2 = (hat2 * (1.0 + mod[4:5]) + mod[3:4]).astype(BF)
-        normed2_ref[0, mine] = normed2
+        normed2_ref[mine] = normed2
         yield
         lifted = dot(normed2, up_ref[...])
         yield
         act, slope = gelu_parts(lifted)
         act = act.astype(BF)
-        act_ref[0, mine] = act
+        act_ref[mine] = act
         grad = load(cot_ref)
         kept = keep * grad
         d_branch = (kept * mod[5:6]).astype(BF)
-        branch5_ref[0, mine] = d_branch
+        branch5_ref[mine] = d_branch
         yield
         d_act = dot_nt(d_branch, down_ref[...])
         yield
         d_lifted = (d_act * slope).astype(BF)
-        d_lifted_ref[0, mine] = d_lifted
+        d_lifted_ref[mine] = d_lifted
         branch5 = dot(act, down_ref[...])
         yield
-        store(out_ref, state + (keep * mod[5:6]) * branch5)
+        final = stored(state + (keep * mod[5:6]) * branch5)
+        out_buf[step, :, patches, :] = final
+        late_ref[:, patches, :] = final
         d_gate5 = row_sums(kept * branch5)
         d_normed2 = dot_nt(d_lifted, up_ref[...])
         yield
@@ -746,7 +883,7 @@
         kept = keep * grad
         d_gate2 = row_sums(kept * branch2)
         d_branch = (kept * mod[2:3]).astype(BF)
-        branch4_ref[0, mine] = d_branch
+        branch4_ref[mine] = d_branch
         yield
         d_att_t_runs = [dot_nt(proj_ref[...], run_of(d_branch, r)) for r in range(runs)]
         yield
@@ -762,6 +899,7 @@
                 att_t_runs[r],
                 lambda head: inverse_runs[r][head],
                 run_rows,
+                None,
             )
 
         backs = attend_back([job(r) for r in range(runs)], TIME_STAGE, run_rows)
@@ -774,11 +912,11 @@
             ],
             axis=1,
         )
-        d_qkv_ref[0, mine] = d_qkv
+        d_qkv_ref[mine] = d_qkv
         d_normed1 = dot_nt(d_qkv, qkv_ref[...])
         yield
         grad = grad + norm_back(d_normed1, hat1, inverse1, mod[1:2])
-        store(grad_ref, grad)
+        sent_buf[step, :, patches, :] = stored(grad)
         totals.append(
             jnp.concatenate(
                 [
@@ -796,10 +934,38 @@
 
     interleave([stream(first) for first in range(0, block // SUB, runs)], TIME_LAG)
     mods_ref[0] = sum(totals[1:], totals[0])
+    src, dst, _, sem, _ = grad_copy(0, step)
+    pltpu.make_async_copy(src, dst, sem).start()
+    for turn in range(1, lay.n_ta):
+        push(*grad_copy(turn, step)).start()
+
+    d_qkv_sum[...] += dot_tn(normed_ref[...], d_qkv_ref[...])
+    d_proj_sum[...] += dot_tn(att_ref[...], branch4_ref[...])
+    d_up_sum[...] += dot_tn(normed2_ref[...], d_lifted_ref[...])
+    d_down_sum[...] += dot_tn(branch5_ref[...], act_ref[...])
+
+    @pl.when(step == last)
+    def _():
+        d_qkv_sum_ref[...] = d_qkv_sum[...].astype(BF)
+        d_proj_sum_ref[...] = d_proj_sum[...].astype(BF)
+        d_up_sum_ref[...] = d_up_sum[...].astype(BF)
+        d_down_sum_ref[...] = d_down_sum[...].astype(BF)
+        for i in range(early):
+            for t in range(lay.n_ta):
+                end_push(me, *out_copy(t, i))
+            for j in range(lay.clips_dev):
+                for s in range(lay.halves):
+                    arrived(early_ref.at[j, :, s, i * block : (i + 1) * block], out_recv.at[j, s, i])
+        for i in range(lay.time_patches // block):
+            for turn in range(lay.n_ta):
+                src, dst, _, sem, place = grad_copy(turn, i)
+                if turn:
+                    push(*grad_copy(turn, i)).wait_send()
+                arrived(dst, sem)
 
 
 class Reducer:
-    def __init__(self, shapes, small_rows, sizes):
+    def __init__(self, shapes, small_rows, sizes, parts):
         self.width = width = shapes[0][1]
         self.shapes = shapes
         bits = {name: [(name, 1 << i) for i in range(sizes[name].bit_length() - 1)] for name in ("ta", "pa")}
@@ -811,7 +977,8 @@
                 self.loads.append((i, row, column * width, shape[0]))
                 row += shape[0]
         self.total = row
-        self.parts = next(n for n in PARTS if row % (2 * n * TILE) == 0)
+        cut = TILE << sum(len(ways) for ways in bits.values())
+        self.parts = next((n for n in parts if row % (2 * n * cut) == 0), 1)
         self.part_rows = row // 2 // self.parts
         self.half_rows = row // 2
         self.orders = [[("dev", 1)] + kinds[PATTERN[p % len(PATTERN)]] for p in range(self.parts)]
@@ -990,7 +1157,7 @@
 
 
 def reduce_all(arrays, small, sizes):
-    reducer = Reducer([a.shape for a in arrays], small.shape[0], sizes)
+    reducer = Reducer([a.shape for a in arrays], small.shape[0], sizes, PARTS)
     n = len(arrays)
 
     def kernel(*refs):
@@ -1210,85 +1377,6 @@
             collective_id=1,
         )
 
-        def space_backward(frame_ids, grad, saved):
-            count = len(frame_ids)
-
-            def out(*shape, dtype=BF):
-                return shape_of((count,) + shape, dtype)
-
-            (_, _, query, keys_t, value, exponent, att_t, _, inverse, _, cross_query, cross_exponent, cross_att_t, _,
-             cross_inverse, middle, _, _, slope, branch2, branch5) = saved
-            start = frame_ids[0]
-
-            def framed_from(array):
-                tail = (0,) * (array.ndim - 1)
-                return pl.BlockSpec((1,) + tuple(array.shape[1:]), lambda frame: (frame + start,) + tail)
-
-            inputs = (
-                counts, grad, space_mod, patch_attn, cross_ends, text_keys.T, text_values, patch_up, patch_down,
-                query, keys_t, value, exponent, att_t, inverse, cross_query, cross_exponent, cross_att_t,
-                cross_inverse, middle, slope, branch2, branch5,
-            )
-            hidden = patch_up.shape[1]
-            outputs = (
-                out(space_rows, width, dtype=F32),
-                out(space_rows, width, dtype=F32),
-                out(other_rows, width),
-                out(space_rows, width),
-                out(space_rows, hidden),
-                out(space_rows, width),
-                out(space_rows, width),
-                out(space_rows, width),
-                out(space_rows, width),
-                out(key_rows, width),
-                out(key_rows, width),
-                out(text_rows, width, dtype=F32),
-                out(text_rows, width, dtype=F32),
-                out(8, width, dtype=F32),
-            )
-            grad_spec = pl.BlockSpec((n_ta, 1, time_patches, width), lambda frame: (0, frame, 0, 0))
-            dense = 2 * count * space_rows * width * (6 * width + 2 * hidden) + 8 * count * key_rows * width * width
-            return call(
-                lambda *refs: space_backward_kernel(frame_ids[0], *refs),
-                (count,),
-                inputs,
-                [SCALARS, grad_spec] + [whole(a) for a in inputs[2:9]] + [framed_from(a) for a in inputs[9:]],
-                outputs,
-                [framed(a) for a in outputs],
-                dense + 32 * count * space_rows * key_rows * width,
-            )
-
-        def space_finish(own, state_grad, own_grad, parts):
-            count = own.shape[0]
-            inputs = (own, state_grad, own_grad, *parts, space_mod)
-            outputs = (
-                shape_of((count, near, patches, width), BF),
-                shape_of((count, 8, width), F32),
-            )
-            return call(
-                lambda *refs: space_finish_kernel(len(parts), *refs),
-                (count,),
-                inputs,
-                [framed(a) for a in inputs[:-1]] + [whole(space_mod)],
-                outputs,
-                [framed(a) for a in outputs],
-                count * space_rows * width * 30,
-            )
-
-        frame_groups = [ids for ids in (tuple(range(min(2, frames))), tuple(range(min(2, frames), frames))) if ids]
-        slot = ta % halves
-        n_steps = halves * clips_dev
-
-        def exchange(pieces):
-            got = [lax.dynamic_index_in_dim(pieces, ta, 0, keepdims=False)]
-            for step in range(1, n_ta):
-                sent = lax.dynamic_index_in_dim(pieces, ta ^ step, 0, keepdims=False)
-                got.append(lax.ppermute(sent, "ta", ta_pairs(step)))
-            stacked = jnp.stack(got)
-            return jnp.stack(
-                [lax.dynamic_index_in_dim(stacked, ta ^ t, 0, keepdims=False) for t in range(n_ta)]
-            )
-
         block_rows = all_frames * BLOCK
         run_rows = all_frames * SUB
         ids = jnp.arange(run_rows, dtype=jnp.int32)
@@ -1297,139 +1385,157 @@
         hidden = frame_up.shape[1]
         n_blocks = time_patches // BLOCK
 
-        def tokens(features):
-            return shape_of((n_blocks, block_rows, features), BF)
-
+        early = max(n_blocks - 1, 1) * BLOCK
         frame_wide = frame_attn[:3].swapaxes(0, 1).reshape(width, 3 * width)
         time_inputs = (counts, state, cot, frame_mod, bias, frame_wide, frame_attn[3], frame_up, frame_down)
         time_outputs = (
-            shape_of((all_frames, time_patches, width), BF),
-            shape_of((all_frames, time_patches, width), BF),
-            tokens(width),
-            tokens(3 * width),
-            tokens(width),
-            tokens(width),
-            tokens(width),
-            tokens(hidden),
-            tokens(hidden),
-            tokens(width),
+            out(space_rows, width),
+            shape_of((clips_dev, frames, halves, early, width), BF),
+            shape_of((all_frames, BLOCK, width), BF),
+            shape_of((width, 3 * width), BF),
+            shape_of((width, width), BF),
+            shape_of((width, hidden), BF),
+            shape_of((width, hidden), BF),
             shape_of((n_blocks, 8, width), F32),
         )
 
         def blocked(array):
             return pl.BlockSpec((all_frames, BLOCK, array.shape[2]), lambda at: (0, at, 0))
 
-        (out_t, grad_t, normed_t, d_qkv_t, att_tt, branch4, normed4, act4, d_lifted4, branch5, frame_six) = call(
-            time_kernel,
+        def vmem(*shape, dtype=BF):
+            return pltpu.VMEM(shape, dtype)
+
+        (grad_s, early_out, late_out, d_frame_qkv, d_frame_proj, d_frame_up, d_frame_down, frame_six) = call(
+            lambda *refs: time_kernel(lay, *refs),
             (n_blocks,),
             time_inputs,
             [SCALARS, blocked(state), blocked(cot)] + [whole(a) for a in time_inputs[3:]],
             time_outputs,
-            [blocked(a) for a in time_outputs[:2]] + [framed(a) for a in time_outputs[2:]],
-            all_frames * time_patches * width * (24 * width + 12 * hidden),
-            [pltpu.VMEM((BLOCK // SUB, HEADS, run_rows, run_rows), BF)],
-        )
-
-        grad_s = exchange(grad_t.reshape(n_ta, frames, time_patches, width))
-
-        out_t, grad_s = lax.optimization_barrier((out_t, grad_s))
-        out_pieces = out_t.reshape(n_ta, frames, time_patches, width)
-        out_parts = []
-        for step in range(n_steps):
-            u, w = step % halves, step // halves
-            source = (slot - u) % halves + halves * ((clip % clips_dev - w) % clips_dev)
-            sent = lax.dynamic_index_in_dim(out_pieces, source, 0, keepdims=False)
-            out_parts.append(lax.ppermute(sent, whole_axes, back(time_pairs(step))))
-        out_stack = jnp.stack(out_parts)
-        rows = []
-        for j in range(clips_dev):
-            runs = []
-            for s in range(halves):
-                step = ((j - ta // halves) % clips_dev) * halves + (s - ta % halves) % halves
-                runs.append(lax.dynamic_index_in_dim(out_stack, step, 0, keepdims=False))
-            rows.append(jnp.concatenate(runs, axis=1))
-        output = jnp.stack(rows)
+            [HBM, HBM] + [whole(a) for a in time_outputs[2:-1]] + [framed(time_outputs[-1])],
+            all_frames * time_patches * width * (32 * width + 20 * hidden),
+            [
+                vmem(BLOCK // SUB, HEADS, run_rows, run_rows),
+                vmem(n_blocks, all_frames, BLOCK, width),
+                vmem(n_blocks, all_frames, BLOCK, width),
+                vmem(width, 3 * width, dtype=F32),
+                vmem(width, width, dtype=F32),
+                vmem(width, hidden, dtype=F32),
+                vmem(width, hidden, dtype=F32),
+                vmem(block_rows, width),
+                vmem(block_rows, 3 * width),
+                vmem(block_rows, width),
+                vmem(block_rows, width),
+                vmem(block_rows, width),
+                vmem(block_rows, hidden),
+                vmem(block_rows, hidden),
+                vmem(block_rows, width),
+                dma((n_ta, n_blocks)),
+                dma((n_ta, n_blocks)),
+                dma((n_ta, n_blocks)),
+                dma((clips_dev, halves, n_blocks)),
+            ],
+            collective_id=2,
+        )
 
         def weight_grad(left, right):
             left, right = left.reshape(-1, left.shape[-1]), right.reshape(-1, right.shape[-1])
             return lax.dot_general(left, right, (((0,), (0,)), ((), ())), preferred_element_type=F32).astype(BF)
 
-        d_frame_qkv = weight_grad(normed_t, d_qkv_t)
-        d_frame_proj = weight_grad(att_tt, branch4)
-        d_frame_up = weight_grad(normed4, d_lifted4)
-        d_frame_down = weight_grad(act4, branch5)
-
-        pieces, backs, finish_six = [], [], []
-        for i, frame_ids in enumerate(frame_groups):
-            own = saved[0][frame_ids[0] : frame_ids[-1] + 1]
-            grad = grad_s[:, frame_ids[0] : frame_ids[-1] + 1]
-            if i == 1:
-                grad, output = lax.optimization_barrier((grad, output))
-            backed = space_backward(frame_ids, grad, saved)
-            backs.append(backed)
-            other_grad = backed[2]
-            parts = []
-            for step in range(1, group):
-                sent = other_grad[:, (step - 1) * space_rows : step * space_rows]
-                parts.append(lax.ppermute(sent, pair_axes, back(group_pairs(step))))
-            done, mods = space_finish(own, backed[0], backed[1], parts)
-            finish_six.append(mods)
-            got = []
-            for step in range(clips_dev):
-                b = (clip - step) % clips_dev
-                sent = lax.dynamic_index_in_dim(done, b, 1, keepdims=False)
-                got.append(lax.ppermute(sent, pair_axes, back(space_pairs(step))))
-            stacked = jnp.stack(got)
-            pieces.append(
-                jnp.stack(
-                    [
-                        lax.dynamic_index_in_dim(stacked, (j - pa) % clips_dev, 0, keepdims=False)
-                        for j in range(clips_dev)
-                    ]
-                )
-            )
-        latents_grad = jnp.concatenate(pieces, axis=1).astype(F32)
-
-        def over_frames(lists, index):
-            picked = [entry[index] for entry in lists]
-            return picked[0] if len(picked) == 1 else jnp.concatenate(picked)
-
-        def grad_over(lists, index, others, other_index):
-            total = None
-            for ids, two in zip(frame_groups, others):
-                left, right = lists[index][ids[0] : ids[-1] + 1], two[other_index]
-                left, right = left.reshape(-1, left.shape[-1]), right.reshape(-1, right.shape[-1])
-                part = lax.dot_general(left, right, (((0,), (0,)), ((), ())), preferred_element_type=F32)
-                total = part if total is None else total + part
-            return total.astype(BF)
-
-        d_patch_up = grad_over(saved, 16, backs, 4)
-        d_patch_down = grad_over(saved, 17, backs, 3)
-        d_cross_proj = grad_over(saved, 13, backs, 5)
-        d_cross_q = grad_over(saved, 9, backs, 6)
+        (own, _, query, keys_t, value, exponent, att_t, _, inverse, _, cross_query, cross_exponent, cross_att_t, _,
+         cross_inverse, middle, _, _, slope, branch2, branch5) = saved
+        frame_grads = [d_frame_proj, d_frame_qkv, d_frame_up, d_frame_down]
+        reducer = Reducer([a.shape for a in frame_grads], 0, sizes, HIDDEN_PARTS)
+        fixed = (space_mod, patch_attn, cross_ends, text_keys.T, text_values, patch_up, patch_down)
+        by_frame = (
+            query, keys_t, value, att_t, inverse, cross_query, cross_exponent, cross_att_t, cross_inverse, middle,
+            slope, branch2, branch5,
+        )
+        back_outputs = (
+            shape_of((clips_dev, frames, halves, BLOCK, width), BF),
+            shape_of(latents.shape, BF),
+            shape_of((reducer.total, width), BF),
+            out(space_rows, width),
+            out(space_rows, hidden),
+            out(space_rows, width),
+            out(space_rows, width),
+            out(space_rows, width),
+            out(space_rows, width),
+            out(key_rows, width),
+            out(key_rows, width),
+            out(text_rows, width, dtype=F32),
+            out(text_rows, width, dtype=F32),
+            shape_of((frames + 1, 8, width), F32),
+        )
+
+        def now(array):
+            tail = (0,) * (array.ndim - 1)
+            return pl.BlockSpec((1,) + tuple(array.shape[1:]), lambda at: (jnp.minimum(at, frames - 1),) + tail)
+
+        def before(array):
+            tail = (0,) * (array.ndim - 1)
+            return pl.BlockSpec((1,) + tuple(array.shape[1:]), lambda at: (jnp.maximum(at, 1) - 1,) + tail)
+
+        dense = 2 * frames * space_rows * width * (6 * width + 2 * hidden) + 8 * frames * key_rows * width * width
+        output, lat_grad, frame_sums, *backs = call(
+            lambda *refs: space_backward_kernel(lay, reducer, *refs),
+            (frames + 1,),
+            (counts, grad_s, late_out, exponent, *frame_grads, *fixed, own, *by_frame),
+            [SCALARS, now(grad_s), HBM, HBM] + [HBM] * len(frame_grads) + [whole(a) for a in fixed] + [before(own)]
+            + [now(a) for a in by_frame],
+            back_outputs,
+            [HBM, HBM, HBM] + [now(a) for a in back_outputs[3:-1]] + [framed(back_outputs[-1])],
+            dense + 32 * frames * space_rows * key_rows * width,
+            [
+                pltpu.VMEM((HEADS, key_rows, space_rows), BF),
+                pltpu.VMEM((2, group - 1, space_rows, width), BF),
+                pltpu.VMEM((frames, group - 1, space_rows, width), BF),
+                pltpu.VMEM((2, space_rows, width), F32),
+                pltpu.VMEM((2, space_rows, width), F32),
+                pltpu.VMEM((frames, near, patches, width), BF),
+                dma((HEADS,)),
+                dma((group - 1, frames)),
+                dma((group - 1, frames)),
+                dma((n_ta,)),
+                dma((clips_dev, halves)),
+                dma((near, frames)),
+                dma((clips_dev, frames)),
+                *reducer.scratch(),
+            ],
+            collective_id=3,
+        )
+        latents_grad = lat_grad.astype(F32)
+        if n_blocks > 1:
+            output = jnp.concatenate([early_out, output], axis=3)
+        output = output.reshape(latents.shape)
+
+        kept3, d_lifted2, kept2, d_cross_query, kept1, d_query, d_key, d_value, d_tk, d_tv, space_six = backs
+        d_patch_up = weight_grad(saved[16], d_lifted2)
+        d_patch_down = weight_grad(saved[17], kept3)
+        d_cross_proj = weight_grad(saved[13], kept2)
+        d_cross_q = weight_grad(saved[9], d_cross_query)
         text_t = text.astype(F32).T
-        d_tk, d_tv = (over_frames(backs, i) for i in (11, 12))
         d_cross_k = jnp.dot(text_t, jnp.sum(d_tk, axis=0)[:text_count], precision=HIGHEST).astype(BF)
         d_cross_v = jnp.dot(text_t, jnp.sum(d_tv, axis=0)[:text_count], precision=HIGHEST).astype(BF)
-        d_patch_proj = grad_over(saved, 7, backs, 7)
-        d_patch_q = grad_over([saved[1][:, :space_rows]], 0, backs, 8)
-        d_patch_k = grad_over(saved, 1, backs, 9)
-        d_patch_v = grad_over(saved, 1, backs, 10)
-        six = jnp.sum(over_frames(backs, 13), axis=0) + jnp.sum(jnp.concatenate(finish_six), axis=0)
+        d_patch_proj = weight_grad(saved[7], kept1)
+        d_patch_q = weight_grad(saved[1][:, :space_rows], d_query)
+        d_patch_k = weight_grad(saved[1], d_key)
+        d_patch_v = weight_grad(saved[1], d_value)
+        six = jnp.sum(space_six, axis=0)
         mine = jnp.stack([six, jnp.sum(frame_six, axis=0)])
         spread = jnp.where(jnp.arange(clips)[:, None, None, None] == clip, mine[None], 0.0)
         arrays = [
             d_patch_q, d_patch_k, d_patch_v, d_patch_proj, d_cross_q, d_cross_k, d_cross_v, d_cross_proj,
-            d_patch_up, d_patch_down, d_frame_qkv, d_frame_proj, d_frame_up, d_frame_down,
+            d_patch_up, d_patch_down,
         ]
         results, by_clip = reduce_all(arrays, spread.reshape(-1, width), sizes)
         by_clip = by_clip.reshape(clips, 2, 8, width)[:, :, :6]
         d_patch_attn = jnp.stack(results[0:4])
         d_cross = jnp.stack(results[4:8])
         d_patch_up, d_patch_down = results[8:10]
-        d_frame_qkv = results[10].reshape(width, 3, width).swapaxes(0, 1)
-        d_frame_attn = jnp.concatenate([d_frame_qkv, results[11][None]])
-        d_frame_up, d_frame_down = results[12:14]
+        d_frame_proj, d_frame_qkv, d_frame_up, d_frame_down = reducer.unpack(frame_sums)
+        d_frame_qkv = d_frame_qkv.reshape(width, 3, width).swapaxes(0, 1)
+        d_frame_attn = jnp.concatenate([d_frame_qkv, d_frame_proj[None]])
+        d_frame_down = d_frame_down.T
         d_table = jnp.sum(by_clip, axis=0)
         d_step = lax.dot_general(
             embeddings,

time: 553 us -> 485 us (0.88)
  Pallas kernels: 345 us -> 393 us
  starting transfers between devices: 41.2 us -> 0 us
  matrix products: 66.5 us -> 41.2 us
  waiting for transfers between devices: 20.3 us -> 0 us
  other arithmetic: 38.7 us -> 24 us
  local copies, waits for them, and re-layouts: 31.2 us -> 18 us
    pallas_call x6 -> x3, Pallas kernels: 239 us -> 320 us  [call(): pl.pallas_call(kernel, grid=grid, in_specs=in_specs, out_specs=out_specs,...]
    ppermute x13 -> x0, starting transfers between devices: 41.2 us -> none  [the longest x4 23.8 us: per_device(): out_parts.append(lax.ppermute(sent, whole_axes, back(time_pairs(step))))]
    dot_general x16 -> x0, matrix products: 36.8 us -> none  [grad_over(): lax.dot_general(left, right, (((0,), (0,)), ((), ())), preferred_element_...]
    pallas_call x1, Pallas kernels: 107 us -> 73.5 us  [reduce_all(): pl.pallas_call(kernel, in_specs=[any_spec] * n + [vmem_spec], out_specs=[...]
    ppermute x13 -> x0, waiting for transfers between devices: 20.3 us -> none  [the longest x4 20.3 us: per_device(): got.append(lax.ppermute(sent, pair_axes, back(space_pairs(step))))]
    dot_general x4 -> x8, matrix products: 20.3 us -> 31.9 us  [weight_grad(): lax.dot_general(left, right, (((0,), (0,)), ((), ())), preferred_element_...]
    another operation x8 -> x0, other arithmetic: 8.51 us -> none  [the longest x2 1.93 us: per_device(): stacked = jnp.stack(got)]
    slice x4 -> x0, local copies, waits for them, and re-layouts: 6.76 us -> none  [the longest x2 4.62 us: per_device(): own = saved[0][frame_ids[0]:frame_ids[-1] + 1]]
  transfers between devices with their start and end apart: 13 -> 0, of which waited for: 3 -> 0; matrix products, arithmetic and copies ran while one was open for 18% -> 0% of each run, Pallas kernels for 15% -> 0%
where the time goes in v5:
time: 485 us; the launch traced here: 482 us
  Pallas kernels  393 us (81%)
  matrix products  41.2 us (8%)
  other arithmetic  24 us (5%)
  local copies, waits for them, and re-layouts  18 us (4%)
    pallas_call x3, Pallas kernels, call(): pl.pallas_call(kernel, grid=grid, in_specs=in_specs, out_specs=out_specs,...  320 us
    pallas_call x1, Pallas kernels, reduce_all(): pl.pallas_call(kernel, in_specs=[any_spec] * n + [vmem_spec], out_specs=[...  73.5 us
    dot_general x8, matrix products, weight_grad(): lax.dot_general(left, right, (((0,), (0,)), ((), ())), preferred_element_...  31.9 us

profile of v5, /device:TPU:1, one launch (start us, length us, event | category | flops | bytes accessed | tf_op | source)
XLA Modules:
  0.0 481.7 jit_solution(10326614691589571962)
XLA Ops:
  0.9 0.7 pad_add_fusion
  1.6 1.8 all-gather
  4.1 1.9 pad_add_fusion.1.refs_0_
  6.1 0.7 fusion.26
  6.9 0.7 copy_convert_fusion
  7.6 0.8 and_select_fusion.refs_4_
  8.4 1.8 slice_bitcast_fusion.12.refs_6_
  10.1 2.3 all_gather.7
  12.4 1.2 convolution_convert_fusion.2.refs_12_
  13.6 1.3 convolution_convert_fusion.3
  14.9 0.8 copy.65.refs_7_
  15.7 0.8 copy.66.refs_8_
  16.4 1.1 copy.89
  17.5 1.2 fusion.38
  18.7 0.9 pad_maximum_fusion.1.refs_6_.refs_10_
  19.6 2.3 copy.90
  21.9 1.5 copy.68.refs_5_
  23.4 0.6 copy.61
  24.1 1.0 fusion.28
  25.1 0.6 concatenate.39.refs_3_
  26.3 99.1 %shard_map.230 = (bf16[20,128,384]{2,1,0:T(8,128)(2,1)}, bf16[20,128,384]{2,1,0:T(8,128)(2,1)}, bf16[5,512,384]{2,1,0:T(8,128)(2,1)}, bf16[5,1024,384]{2,1,0:T(8...) custom-call(s32[4]{0:T(128)} %pad_add_fusion.1.refs_0_, ...), custom_call_target="tpu_custom_call" | custom-call | flops 32715571200 | bytes 101429264 | tf_op jit(solution)/shard_map/pallas_call | solution.py:1205
  125.5 86.2 %shard_map.231 = (bf16[5,512,384]{2,1,0:T(8,128)(2,1)}, bf16[2,5,2,96,384]{4,3,2,1,0:T(8,128)(2,1)}, bf16[20,32,384]{2,1,0:T(8,128)(2,1)}, bf16[384,1152]{1,0:T(...) custom-call(s32[4]{0:T(128)} %pad_add_fusion.1.refs_0_, ...), custom_call_target="tpu_custom_call" | custom-call | flops 42278584320 | bytes 15106064 | tf_op jit(solution)/shard_map/pallas_call | solution.py:1205
  211.7 134.1 %shard_map.232 = (bf16[2,5,2,32,384]{4,3,2,1,0:T(8,128)(2,1)}, bf16[2,5,256,384]{3,2,1,0:T(8,128)(2,1)}, bf16[4608,384]{1,0:T(8,128)(2,1)}, bf16[5,512,384]{2,1,...) custom-call(s32[4]{0:T(128)} %pad_add_fusion.1.refs_0_, ...), custom_call_target="tpu_custom_call" | custom-call | flops 48821698560 | bytes 112906256 | tf_op jit(solution)/shard_map/pallas_call | solution.py:1205
  345.9 9.2 %fusion.1.refs_9_ = bf16[1536,384]{1,0:T(8,128)(2,1)} fusion(bf16[5,512,1536]{2,1,0:T(8,128)(2,1)} %get-tuple-element.98, bf16[5,512,384]{2,1,0:T(8,128)(2,1)} %get-tuple-element.99), kind=kOutput, calls=%fused_computation.3 | convolution fusion | flops 3020488704 | bytes 11010048 | tf_op jit(solution)/shard_map/dot_general | solution.py:1442
  355.2 4.3 fusion.refs_8_
  359.5 1.9 fusion.9.refs_7_
  361.6 1.9 fusion.8.refs_4_
  363.7 1.9 fusion.7.refs_3_
  365.7 1.6 pad_maximum_fusion
  367.3 0.7 bitcast_select_fusion.refs_10_
  368.2 1.2 convolution_convert_fusion.refs_6_
  369.3 1.2 convolution_convert_fusion.1.refs_5_
  370.5 4.2 fusion.10.refs_0_
  374.7 5.2 %fusion.13.refs_1_ = bf16[384,384]{1,0:T(8,128)(2,1)} fusion(bf16[5,1024,384]{2,1,0:T(8,128)(2,1)S(1)} %copy-done, bf16[5,1024,384]{2,1,0:T(8,128)(2,1)} %get-tuple-element.86), kind=kOutput, calls=%fused_computation.20 | convolution fusion | flops 1510096896 | bytes 8159232 | tf_op jit(solution)/shard_map/dot_general | solution.py:1442
  379.9 3.2 fusion.14.refs_2_
  383.1 73.5 %shard_map.233 = (bf16[6144,384]{1,0:T(8,128)(2,1)}, f32[64,384]{1,0:T(8,128)}) custom-call(bf16[384,384]{1,0:T(8,128)(2,1)} %fusion.10.refs_0_, bf16[384,384]{1,0:T(8,128)(2,1)} %fusion.13.refs_1_, bf16[384,384]{1,0:T(8,128)(2,1)} %fusion.14.refs_2_, bf16[384,384]{1,0:T(8,128)(2,1)} %fusion.7.refs_3_, bf16[384,384]{1,0:T(8,128)(2,1)} %fusion.8.refs_4_, ...), custom_call_target="tpu_custom_call" | custom-call | flops 18874368 | bytes 9437184 | tf_op jit(solution)/shard_map/pallas_call | solution.py:1171
  456.6 0.9 slice_reduce_fusion
  457.5 0.6 copy.77
  458.2 3.5 fusion.25
  461.6 2.8 slice_convert_fusion
  464.5 1.3 fusion.36
  465.8 1.7 maximum_convert_fusion.2
  467.5 1.2 copy-done.3
  469.2 1.6 maximum_convert_fusion.3
  470.7 2.0 convert_bitcast_fusion
  472.8 1.9 copy.78
  474.7 3.9 convert_element_type.81
  478.6 2.6 maximum_convert_fusion
  (82 shorter events, 2.9 us)
Async XLA Ops:
  6.8 17.2 %copy-start.17 = (f32[4,128]{1,0:T(4,128)}, f32[4,128]{1,0:T(4,128)S(1)}, u32[]{:S(2)}) copy-start(f32[4,128]{1,0:T(4,128)S(1)} %get-tuple-element.168) | copy-start | bytes 6148
  6.9 17.2 %copy-start.19 = (f32[4,128]{1,0:T(4,128)}, f32[4,128]{1,0:T(4,128)S(1)}, u32[]{:S(2)}) copy-start(f32[4,128]{1,0:T(4,128)S(1)} %get-tuple-element.169) | copy-start | bytes 6148
  8.3 8.1 %slice-start.1 = ((bf16[4,384,384]{2,1,0:T(8,128)(2,1)}), bf16[2,384,384]{2,1,0:T(8,128)(2,1)S(1)}, s32[]{:S(2)}) async-start(bf16[4,384,384]{2,1,0:T(8,128)(2,1)} %refs_9_.3), calls=%async_computation.1 | async-start | bytes 1179648 | tf_op jit(solution)/shard_map/slice | solution.py:1316
  13.6 5.1 %copy-start.13 = (bf16[128,384]{1,0:T(8,128)(2,1)}, bf16[128,384]{1,0:T(8,128)(2,1)S(1)}, u32[]{:S(2)}) copy-start(bf16[128,384]{1,0:T(8,128)(2,1)S(1)} %convolution_convert_fusion.2.refs_12_) | copy-start | bytes 294916
  14.9 3.8 copy-start.14
  17.5 2.1 slice-start
  21.9 1.5 copy-start.9
  345.9 9.3 %copy-start.21 = (bf16[5,512,1536]{2,1,0:T(8,128)(2,1)S(1)}, bf16[5,512,1536]{2,1,0:T(8,128)(2,1)}, u32[]{:S(2)}) copy-start(bf16[5,512,1536]{2,1,0:T(8,128)(2,1)} %get-tuple-element.97) | copy-start | bytes 23592964
  345.9 9.2 %copy-start.22 = (bf16[5,512,384]{2,1,0:T(8,128)(2,1)S(1)}, bf16[5,512,384]{2,1,0:T(8,128)(2,1)}, u32[]{:S(2)}) copy-start(bf16[5,512,384]{2,1,0:T(8,128)(2,1)} %get-tuple-element.96) | copy-start | bytes 5898244
  355.1 4.3 copy-start.25
  355.2 4.3 copy-start.28
  359.4 1.9 copy-start.24
  359.5 2.1 copy-start.27
  361.6 1.9 copy-start.23
  361.6 2.1 copy-start.26
  363.7 1.9 copy-start.4
  363.7 1.9 copy-start.12
  365.6 1.6 copy-start.15
  365.7 1.6 copy-start.16
  365.7 2.4 copy-start.11
  365.7 2.4 copy-start.10
  370.5 4.2 copy-start
  374.7 5.2 %copy-start.1 = (bf16[5,1024,384]{2,1,0:T(8,128)(2,1)S(1)}, bf16[5,1024,384]{2,1,0:T(8,128)(2,1)}, u32[]{:S(2)}) copy-start(bf16[5,1024,384]{2,1,0:T(8,128)(2,1)} %get-tuple-element.87) | copy-start | bytes 11796484
  383.1 75.0 %copy-start.18 = (f32[4,128]{1,0:T(4,128)S(1)}, f32[4,128]{1,0:T(4,128)}, u32[]{:S(2)}) copy-start(f32[4,128]{1,0:T(4,128)} %copy-done.17) | copy-start | bytes 6148
  383.1 75.0 %copy-start.20 = (f32[4,128]{1,0:T(4,128)S(1)}, f32[4,128]{1,0:T(4,128)}, u32[]{:S(2)}) copy-start(f32[4,128]{1,0:T(4,128)} %copy-done.19) | copy-start | bytes 6148
  458.2 6.3 %copy-start.2 = (bf16[6144,384]{1,0:T(8,128)(2,1)S(1)}, bf16[6144,384]{1,0:T(8,128)(2,1)}, u32[]{:S(2)}) copy-start(bf16[6144,384]{1,0:T(8,128)(2,1)} %get-tuple-element.103) | copy-start | bytes 14155780
  465.8 2.9 copy-start.3
  474.7 3.9 copy-start.5
  474.7 3.9 copy-start.6
  474.7 3.9 copy-start.7
  474.7 3.9 copy-start.8
